TPU v7x, 32 devices: a whole 2x2x4 slice. The times are simulated.
32 devices in a mesh: seq: 8 (over z, core), blk: 4 (over y, x).
Axes of the slice: x: 2, y: 2, z: 4, core: 2. Of those that a mesh axis runs over, the one named last changes fastest.
Arguments:
- queries: float32 [4096, 3072], P(('seq', 'blk')), may hold values from -8 to 8
- key_matrix: float32 [4096, 3072], P(('seq', 'blk')), may hold values from -8 to 8
- value_matrix: float32 [4096, 3072], P(('seq', 'blk')), may hold values from -6 to 6
- gate_logits: float32 [4096, 24], P(('seq', 'blk')), may hold values from -6 to 6
- output_grad: float32 [4096, 3072], P(('seq', 'blk')), may hold values from -6 to 6
- cycle_offsets: int32 [32, 4], P(('seq', 'blk')), may hold values from -2 to 2, as said below
- block_count: int32 [32], P(('seq', 'blk')), may hold values from 1 to 4
- feature_seed: int32 [128, 256], replicated, may hold values from -3 to 3
Outputs:
- attended: float32 [4096, 3072], P(('seq', 'blk'))
- query_grad: float32 [4096, 3072], P(('seq', 'blk'))
- key_grad: float32 [4096, 3072], P(('seq', 'blk'))
- value_grad: float32 [4096, 3072], P(('seq', 'blk'))
- gate_grad: float32 [4096, 24], P(('seq', 'blk'))
Inputs may be any that keep to these rules, and one draw needn't show every extreme that they name: `cycle_offsets`: each row holds -2, -1, 1 and 2 once each.
All inputs are finite; a program needn't handle non-finite values.
Results may differ from a plain program's by a relative error of at most 0.0003.
Values sent between devices are 32-bit elements; how exact they have to be, the bound alone decides.
No kernel may reach another device: no remote copies, remote signals or barrier semaphores. Data moves between devices by JAX's collectives and lax.ppermute only.
A program may use at most 192 MiB of HBM per device.

v0:
```python
import math

import jax
import jax.numpy as jnp
from jax import lax
from jax.sharding import PartitionSpec as P

HEAD_DIM = 128


HIGH = lax.Precision.HIGHEST
CANDIDATES = (1, -1, 2, -2)
NEG_FILL = -1e30


def extended(cells, sides, width):
    for axis, dim in sides:
        count = lax.axis_size(axis)
        ends = count - 1
        head = lax.slice_in_dim(cells, 0, width, axis=dim)
        tail = lax.slice_in_dim(cells, cells.shape[dim] - width, cells.shape[dim], axis=dim)
        cells = jnp.concatenate(
            [
                lax.ppermute(tail, axis, [(i, (i + 1) % count) for i in range(ends)]),
                cells,
                lax.ppermute(head, axis, [((i + 1) % count, i) for i in range(ends)]),
            ],
            axis=dim,
        )
    return cells


def shifted(block, axis, distance):
    devices = range(lax.axis_size(axis))
    route = [((i - distance) % len(devices), i) for i in devices]
    return lax.ppermute(block, axis, route)


def feature_map(heads_in, projection):
    normed = heads_in * lax.rsqrt(jnp.mean(heads_in * heads_in, axis=-1, keepdims=True) + 1e-06)
    return jnp.exp(jnp.einsum("nhd,df->nhf", normed, projection, precision=HIGH))


def used_flags(offsets, used_count, cycle_size):
    active = jnp.arange(offsets.shape[0], dtype=jnp.int32) < used_count
    residues = jnp.mod(offsets, cycle_size)
    flag_list = []
    for position, candidate in enumerate(CANDIDATES):
        residue = candidate % cycle_size
        earlier = any((previous % cycle_size == residue for previous in CANDIDATES[:position]))
        chosen = jnp.any(active & (residues == residue))
        flag_list.append(jnp.logical_and(chosen, not earlier))
    return flag_list


def sparse_block(query_rows, key_rows, value_rows, allowed):
    heads_num = query_rows.shape[1] // HEAD_DIM
    query_heads = query_rows.reshape(query_rows.shape[0], heads_num, HEAD_DIM)
    key_heads = key_rows.reshape(key_rows.shape[0], heads_num, HEAD_DIM)
    value_heads = value_rows.reshape(value_rows.shape[0], heads_num, HEAD_DIM)
    scores = jnp.einsum("ihd,jhd->hij", query_heads, key_heads, precision=HIGH) / math.sqrt(
        HEAD_DIM
    )
    scores = jnp.where(allowed[None] > 0.0, scores, NEG_FILL)
    highest = lax.stop_gradient(jnp.max(scores, axis=-1, keepdims=True))
    weights = jnp.exp(scores - highest) * allowed[None]
    totals = jnp.sum(weights, axis=-1)
    mixed = jnp.einsum("hij,jhd->ihd", weights, value_heads, precision=HIGH)
    return (mixed / jnp.transpose(totals)[:, :, None]).reshape(query_rows.shape[0], -1)


def shards(
    queries,
    key_matrix,
    value_matrix,
    gate_logits,
    output_grad,
    cycle_offsets,
    block_count,
    feature_seed,
):
    tok_rows = queries.shape[0]
    reach = tok_rows // 2
    width_all = queries.shape[1]
    heads_num = gate_logits.shape[1]
    cycle_size = lax.axis_size("blk")
    member = lax.axis_index("blk")
    device = lax.axis_index("seq") * cycle_size + member
    total_tokens = tok_rows * cycle_size * lax.axis_size("seq")
    projection = feature_seed.astype(jnp.float32) / 13.0
    paired = jnp.concatenate([key_matrix, value_matrix], axis=1)
    padded = extended(paired, ((("seq", "blk"), 0),), reach)
    tile_rows = [shifted(paired, "blk", -candidate) for candidate in CANDIDATES]
    query_pos = device * tok_rows + jnp.arange(tok_rows, dtype=jnp.int32)
    near_pos = device * tok_rows - reach + jnp.arange(tok_rows + 2 * reach, dtype=jnp.int32)
    near_gap = jnp.abs(near_pos[None, :] - query_pos[:, None])
    allowed_list = [
        (near_gap <= reach) & (near_pos >= 0)[None, :] & (near_pos < total_tokens)[None, :]
    ]
    flag_list = used_flags(cycle_offsets[0], block_count[0], cycle_size)
    for candidate, tile_flag in zip(CANDIDATES, flag_list):
        source = device - member + jnp.mod(member + candidate, cycle_size)
        tile_pos = source * tok_rows + jnp.arange(tok_rows, dtype=jnp.int32)
        allowed_list.append(tile_flag & (jnp.abs(tile_pos[None, :] - query_pos[:, None]) > reach))
    allowed = jnp.concatenate(allowed_list, axis=1).astype(jnp.float32)
    all_paired = jnp.concatenate([padded] + tile_rows, axis=0)

    def sparse_part(query_rows, paired_rows):
        return sparse_block(
            query_rows, paired_rows[:, :width_all], paired_rows[:, width_all:], allowed
        )

    sparse_flat, sparse_pull = jax.vjp(sparse_part, queries, all_paired)

    def key_side(key_rows, value_rows):
        key_feats = feature_map(key_rows.reshape(tok_rows, heads_num, HEAD_DIM), projection)
        value_heads = value_rows.reshape(tok_rows, heads_num, HEAD_DIM)
        return (
            jnp.einsum("nhf,nhd->hfd", key_feats, value_heads, precision=HIGH),
            jnp.sum(key_feats, axis=0),
        )

    partial_sums, key_pull = jax.vjp(key_side, key_matrix, value_matrix)
    kv_sums, key_totals = lax.psum((partial_sums[0], partial_sums[1]), ("seq", "blk"))

    def query_side(query_rows, sums_in, totals_in):
        query_feats = feature_map(query_rows.reshape(tok_rows, heads_num, HEAD_DIM), projection)
        numerator = jnp.einsum("nhf,hfd->nhd", query_feats, sums_in, precision=HIGH)
        denominator = jnp.einsum("nhf,hf->nh", query_feats, totals_in, precision=HIGH)
        return numerator / denominator[:, :, None]

    low_rank, query_pull = jax.vjp(query_side, queries, kv_sums, key_totals)
    gate = jax.nn.sigmoid(gate_logits)[:, :, None]
    sparse_heads = sparse_flat.reshape(tok_rows, heads_num, HEAD_DIM)
    attended = (gate * sparse_heads + (1.0 - gate) * low_rank).reshape(tok_rows, width_all)
    grad_heads = output_grad.reshape(tok_rows, heads_num, HEAD_DIM)
    gate_grad = (
        jnp.sum(grad_heads * (sparse_heads - low_rank), axis=-1)
        * gate[:, :, 0]
        * (1.0 - gate[:, :, 0])
    )
    query_low, sums_part, totals_part = query_pull((1.0 - gate) * grad_heads)
    sums_grad, totals_grad = lax.psum((sums_part, totals_part), ("seq", "blk"))
    key_low, value_low = key_pull((sums_grad, totals_grad))
    query_sparse, paired_grad = sparse_pull((gate * grad_heads).reshape(tok_rows, width_all))
    span = tok_rows + 2 * reach
    edges = jnp.concatenate([paired_grad[:reach], paired_grad[reach + tok_rows : span]], axis=0)
    returned = extended(edges, ((("seq", "blk"), 0),), reach)
    own_grad = paired_grad[reach : reach + tok_rows] + jnp.concatenate(
        [returned[:reach], returned[3 * reach :]], axis=0
    )
    tile_grads = [
        paired_grad[span + position * tok_rows : span + (position + 1) * tok_rows]
        for position in range(len(CANDIDATES))
    ]
    back_terms = [
        shifted(tile_grad, "blk", candidate) for candidate, tile_grad in zip(CANDIDATES, tile_grads)
    ]
    back_sum = back_terms[0] + back_terms[1] + back_terms[2] + back_terms[3]
    paired_back = own_grad + back_sum
    key_grad = paired_back[:, :width_all] + key_low
    value_grad = paired_back[:, width_all:] + value_low
    query_grad = query_sparse + query_low
    return (attended, query_grad, key_grad, value_grad, gate_grad)


def solution(mesh):
    return jax.shard_map(
        shards,
        mesh=mesh,
        in_specs=(
            P(("seq", "blk"), None),
            P(("seq", "blk"), None),
            P(("seq", "blk"), None),
            P(("seq", "blk"), None),
            P(("seq", "blk"), None),
            P(("seq", "blk"), None),
            P(("seq", "blk")),
            P(),
        ),
        out_specs=(
            P(("seq", "blk"), None),
            P(("seq", "blk"), None),
            P(("seq", "blk"), None),
            P(("seq", "blk"), None),
            P(("seq", "blk"), None),
        ),
        check_vma=False,
    )
```

profile of v0, /device:TPU:1, one launch (start us, length us, event | category | flops | bytes accessed | tf_op | source)
XLA Modules:
  0.0 881.3 jit_solution(16111005048220668444)
XLA Ops:
  7.2 3.1 copy.82
  10.8 2.5 copy.72
  15.1 4.2 fusion.50
  19.3 4.5 exponential_reduce_fusion
  23.8 41.0 %psum.29 = f32[24,256]{1,0:T(8,128)S(1)} all-reduce(f32[24,256]{1,0:T(8,128)S(1)} %get-tuple-element.49), channel_id=1, replica_groups=mesh['seq'=8,'blk'=4] {'seq','blk'}, use_global_device_ids=true, to_apply=%region_9.10 | all-reduce | flops 6144 | bytes 49152 | tf_op jit(solution)/shard_map/psum | solution.py:124
  65.4 2.6 fusion.30
  68.0 8.2 fusion.23
  76.2 7.2 fusion.25
  83.4 3.0 copy.67
  86.5 3.9 pad_maximum_fusion
  93.1 3.7 fusion.8
  96.8 3.3 copy.68
  100.1 4.1 collective-permute-start
  104.2 3.3 copy.69
  107.5 4.9 collective-permute-start.1
  117.6 174.8 %collective-permute-done = f32[64,6144]{1,0:T(8,128)} collective-permute-done((f32[64,6144]{1,0:T(8,128)}, f32[64,6144]{1,0:T(8,128)}, u32[]{:S(2)}, u32[]{:S(2)}) %collective-permute-start) | collective-permute-done | bytes 1572896 | tf_op jit(solution)/shard_map/ppermute | solution.py:24
  292.4 3.3 copy.70
  295.8 16.7 %collective-permute-done.1 = f32[64,6144]{1,0:T(8,128)} collective-permute-done((f32[64,6144]{1,0:T(8,128)}, f32[64,6144]{1,0:T(8,128)}, u32[]{:S(2)}, u32[]{:S(2)}) %collective-permute-start.1) | collective-permute-done | bytes 1572896 | tf_op jit(solution)/shard_map/ppermute | solution.py:26
  312.5 3.4 copy.71
  315.8 65.1 %all-reduce.5.cloned.1.call-done = (f32[24,256,128]{2,1,0:T(8,128)}, f32[24,256,128]{2,1,0:T(8,128)}) async-done(((f32[24,256,128]{2,1,0:T(8,128)}, f32[24,256,128]{2,1,0:T(8,128)}), (f32[24,256,128]{2,1,0:T(8,128)}, f32[24,256,128]{2,1,0:T(8,128)})) %all-reduce.5.cloned.1.call-update) | async-done | bytes 6291472 | tf_op jit(solution)/shard_map/psum | solution.py:124
  381.0 8.4 fusion.32
  389.4 4.6 fusion.41
  394.0 21.7 %concatenate.20 = f32[768,6144]{0,1:T(8,128)} concatenate(f32[64,6144]{0,1:T(8,128)} %copy.70, f32[128,6144]{0,1:T(8,128)} %pad_maximum_fusion, f32[64,6144]{0,1:T(8,128)} %copy.71, f32[128,6144]{0,1:T(8,128)} %collective-permute-done.2, f32[128,6144]{0,1:T(8,128)} %collective-permute-done.3, f32[128,6144]{0,1:T(8,128)} %collective-permute-done.4, f32[128,6144]{0,1:T(8,128)} %collective-permute-done.4), dimensions={0} | concatenate | bytes 37748736 | tf_op jit(solution)/shard_map/concatenate | solution.py:106
  415.7 11.1 %fusion.89 = (f32[768,3072]{0,1:T(8,128)}, f32[768,3072]{0,1:T(8,128)S(1)}) fusion(f32[768,6144]{0,1:T(8,128)} %concatenate.20), kind=kLoop, calls=%fused_computation.158 | loop fusion | bytes 37748736 | tf_op jit(solution)/shard_map/jvp()/slice | solution.py:110
  426.8 18.4 %fusion.1 = (f32[24,128]{1,0:T(8,128)S(1)}, f32[24,768,128]{2,1,0:T(8,128)}) fusion(pred[128,768]{0,1:T(8,128)(4,1)S(1)} %copy-done.21, f32[768,24,128]{0,2,1:T(8,128)S(1)} %bitcast.133, f32[128,24,128]{0,2,1:T(8,128)S(1)} %bitcast.143), kind=kOutput, calls=%fused_computation.16 | convolution fusion | flops 3630953472 | bytes 20557824 | tf_op jit(solution)/shard_map/jvp(ihd,jhd->hij)/dot_general | solution.py:61
  445.2 6.1 fusion.4
  451.6 12.6 %fusion.2 = f32[24,128,768]{2,1,0:T(8,128)} fusion(f32[24,768,128]{2,1,0:T(8,128)S(1)} %copy-done.2, f32[128,768]{0,1:T(8,128)S(1)} %get-tuple-element.42, f32[24,128]{1,0:T(8,128)S(1)} %get-tuple-element.47, pred[128,768]{0,1:T(8,128)(4,1)S(1)} %copy-done.21, f32[128,24,128]{0,2,1:T(8,128)S(1)} %bitcast.149, f32[128,24]{0,1:T(8,128)S(1)} %bitcast.163, ...), kind=kOutput, calls=%fused_computation.22 | convolution fusion | flops 3634102272 | bytes 20975616 | tf_op jit(solution)/shard_map/transpose(jvp(hij,jhd->ihd))/dot_general | solution.py:68
  464.2 15.9 %multiply_reduce_fusion = (f32[128,24]{0,1:T(8,128)}, f32[128,24]{0,1:T(8,128)S(1)}, f32[128,24]{0,1:T(8,128)}, f32[128,24,128]{0,2,1:T(8,128)}) fusion(f32[128,24,128]{0,2,1:T(8,128)S(1)} %bitcast.150, f32[128,24]{0,1:T(8,128)S(1)} %bitcast.164, f32[128,24]{0,1:T(8,128)S(1)} %bitcast.162, f32[24,128,128]{2,1,0:T(8,128)S(1)} %copy-done.23, ...), kind=kOutput, calls=%fused_computation.77 | convolution fusion | flops 3639598080 | bytes 24207360 | tf_op jit(solution)/shard_map/jvp(hij,jhd->ihd)/dot_general | solution.py:68
  480.1 21.3 %select_multiply_fusion = f32[24,128,768]{1,2,0:T(8,128)} fusion(f32[24,768,128]{2,1,0:T(8,128)S(1)} %copy-done.2, f32[24,128]{1,0:T(8,128)S(1)} %negate_bitcast_fusion, f32[128,768]{0,1:T(8,128)S(1)} %get-tuple-element.42, f32[24,128]{1,0:T(8,128)S(1)} %get-tuple-element.47, pred[128,768]{0,1:T(8,128)(4,1)S(1)} %copy-done.21, ...), kind=kOutput, calls=%fused_computation.13 | convolution fusion | flops 3643539456 | bytes 30425088 | tf_op jit(solution)/shard_map/transpose(jvp(hij,jhd->ihd))/dot_general | solution.py:68
  501.4 9.7 %copy.89 = f32[768,3072]{1,0:T(8,128)} copy(f32[768,3072]{0,1:T(8,128)} %bitcast.146) | data formatting | bytes 18874368 | tf_op jit(solution)/shard_map/transpose(jvp())/reshape | solution.py:60
  511.0 13.0 %fusion.91 = f32[24,768,128]{1,2,0:T(8,128)} fusion(f32[24,128,768]{1,2,0:T(8,128)} %select_multiply_fusion, f32[128,24,128]{0,2,1:T(8,128)} %bitcast.141), kind=kOutput, calls=%fused_computation.160 | convolution fusion | flops 3623878656 | bytes 20447232 | tf_op jit(solution)/shard_map/transpose(jvp(ihd,jhd->hij))/dot_general | solution.py:61
  524.0 9.6 %copy.91 = f32[768,3072]{1,0:T(8,128)} copy(f32[768,3072]{0,1:T(8,128)} %bitcast.145) | data formatting | bytes 18874368 | tf_op jit(solution)/shard_map/transpose(jvp())/reshape | solution.py:59
  533.6 4.0 fusion.35
  539.4 6.9 fusion.14
  546.3 3.1 copy.98
  549.4 6.4 multiply_reduce_fusion.2
  555.9 5.0 collective-permute-start.6
  562.4 2.4 collective-permute-start.8
  564.8 15.1 %fusion.34 = f32[128,24,128]{0,2,1:T(8,128)} fusion(f32[128,24,128]{0,2,1:T(8,128)S(1)} %bitcast.144, f32[128,24,128]{0,2,1:T(8,128)S(1)} %get-tuple-element.52, f32[24,128,768]{1,2,0:T(8,128)} %select_multiply_fusion, f32[768,24,128]{0,2,1:T(8,128)} %bitcast.134, f32[128,24]{0,1:T(8,128)S(1)} %multiply_multiply_fusion.2, f32[128,24]{0,1:T(8,128)S(1)} %copy-done.36), kind=kOutput, calls=%fused_computation.58 | convolution fusion | flops 3625844736 | bytes 23617536 | tf_op jit(solution)/shard_map/transpose(jvp(ihd,jhd->hij))/dot_general | solution.py:61
  579.9 3.0 copy.99
  582.9 9.2 %fusion.20 = f32[24,128,128]{2,1,0:T(8,128)} fusion(f32[24,256,128]{2,1,0:T(8,128)} %get-tuple-element.27, f32[128,24,256]{2,0,1:T(8,128)} %get-tuple-element.50), kind=kOutput, calls=%fused_computation.41 | convolution fusion | flops 1207959552 | bytes 7864320 | tf_op jit(solution)/shard_map/transpose(jvp(nhf,nhd->hfd))/dot_general | solution.py:119
  592.1 3.0 copy.97
  596.9 233.2 %psum.30 = f32[24,256]{1,0:T(8,128)S(1)} all-reduce(f32[24,256]{1,0:T(8,128)S(1)} %bitcast.166), channel_id=1, replica_groups=mesh['seq'=8,'blk'=4] {'seq','blk'}, use_global_device_ids=true, to_apply=%region_13.14 | all-reduce | flops 6144 | bytes 49152 | tf_op jit(solution)/shard_map/psum | solution.py:143
  830.1 2.9 collective-permute-start.5
  833.0 5.5 fusion.37
  838.5 3.8 multiply_reduce_fusion.1
  845.0 18.9 %collective-permute-done.5 = f32[64,6144]{1,0:T(8,128)} collective-permute-done((f32[64,6144]{1,0:T(8,128)}, f32[64,6144]{1,0:T(8,128)}, u32[]{:S(2)}, u32[]{:S(2)}) %collective-permute-start.5) | collective-permute-done | bytes 1572896 | tf_op jit(solution)/shard_map/ppermute | solution.py:24
  863.9 8.1 fusion.12
  (134 shorter events, 20.3 us)
Async XLA Ops:
  7.2 3.2 copy-start.22
  7.2 373.8 %all-reduce.5.cloned.1.call-start = ((), (), s32[]{:S(2)}) async-start(), calls=%async_computation | async-start | bytes 12582912 | tf_op jit(solution)/shard_map/psum | solution.py:124
  10.8 3.5 copy-start.3
  10.8 4.2 copy-start.19
  14.2 5.1 copy-start.35
  15.1 8.7 copy-start.33
  15.1 4.2 copy-start.4
  19.3 45.4 %copy-start.38 = (f32[128,24]{0,1:T(8,128)S(1)}, f32[128,24]{0,1:T(8,128)}, u32[]{:S(2)}) copy-start(f32[128,24]{0,1:T(8,128)} %param.11) | copy-start | bytes 36868
  64.8 11.5 %copy-start.24 = (f32[24,256]{1,0:T(8,128)}, f32[24,256]{1,0:T(8,128)S(1)}, u32[]{:S(2)}) copy-start(f32[24,256]{1,0:T(8,128)S(1)} %psum.29) | copy-start | bytes 73732
  64.8 3.3 copy-start.10
  65.4 10.8 %copy-start.26 = (f32[128,24]{0,1:T(8,128)}, f32[128,24]{0,1:T(8,128)S(1)}, u32[]{:S(2)}) copy-start(f32[128,24]{0,1:T(8,128)S(1)} %get-tuple-element.46) | copy-start | bytes 36868
  68.0 8.2 copy-start.12
  86.5 6.7 copy-start.5
  86.5 6.7 copy-start.15
  90.4 303.5 %collective-permute-start.2 = (f32[128,6144]{0,1:T(8,128)}, f32[128,6144]{0,1:T(8,128)}, u32[]{:S(2)}, u32[]{:S(2)}) collective-permute-start(f32[128,6144]{0,1:T(8,128)} %pad_maximum_fusion), channel_id=1, source_target_pairs={{1,0},{2,1},{3,2},{0,3},{5,4},{6,5},{7,6},{4,7},{9,8},{10,9},{11,1... | collective-permute-start | bytes 9437192 | tf_op jit(solution)/shard_map/ppermute | solution.py:36
  92.4 301.6 %collective-permute-start.3 = (f32[128,6144]{0,1:T(8,128)}, f32[128,6144]{0,1:T(8,128)}, u32[]{:S(2)}, u32[]{:S(2)}) collective-permute-start(f32[128,6144]{0,1:T(8,128)} %pad_maximum_fusion), channel_id=1, source_target_pairs={{3,0},{0,1},{1,2},{2,3},{7,4},{4,5},{5,6},{6,7},{11,8},{8,9},{9,10... | collective-permute-start | bytes 9437192 | tf_op jit(solution)/shard_map/ppermute | solution.py:36
  92.6 301.4 %collective-permute-start.4 = (f32[128,6144]{0,1:T(8,128)}, f32[128,6144]{0,1:T(8,128)}, u32[]{:S(2)}, u32[]{:S(2)}) collective-permute-start(f32[128,6144]{0,1:T(8,128)} %pad_maximum_fusion), channel_id=1, source_target_pairs={{2,0},{3,1},{0,2},{1,3},{6,4},{7,5},{4,6},{5,7},{10,8},{11,9},{8,1... | collective-permute-start | bytes 9437192 | tf_op jit(solution)/shard_map/ppermute | solution.py:36
  100.1 13.1 %copy-start.43 = (s32[1,4]{1,0:T(1,128)S(1)}, s32[1,4]{1,0:T(1,128)}, u32[]{:S(2)}) copy-start(s32[1,4]{1,0:T(1,128)} %param.13) | copy-start | bytes 52
  100.1 192.3 %collective-permute-start = (f32[64,6144]{1,0:T(8,128)}, f32[64,6144]{1,0:T(8,128)}, u32[]{:S(2)}, u32[]{:S(2)}) collective-permute-start(f32[64,6144]{1,0:T(8,128)} %copy.68), channel_id=1, source_target_pairs={{0,1},{1,2},{2,3},{3,4},{4,5},{5,6},{6,7},{7,8},{8,9},{9,10},{10,1... | collective-permute-start | bytes 4718600 | tf_op jit(solution)/shard_map/ppermute | solution.py:24
  107.5 204.9 %collective-permute-start.1 = (f32[64,6144]{1,0:T(8,128)}, f32[64,6144]{1,0:T(8,128)}, u32[]{:S(2)}, u32[]{:S(2)}) collective-permute-start(f32[64,6144]{1,0:T(8,128)} %copy.69), channel_id=1, source_target_pairs={{1,0},{2,1},{3,2},{4,3},{5,4},{6,5},{7,6},{8,7},{9,8},{10,9},{11,1... | collective-permute-start | bytes 4718600 | tf_op jit(solution)/shard_map/ppermute | solution.py:26
  381.0 8.4 copy-start.13
  381.0 8.4 copy-start.16
  381.0 8.4 copy-start.27
  415.7 11.1 %copy-start.8 = (f32[128,3072]{0,1:T(8,128)S(1)}, f32[128,3072]{0,1:T(8,128)}, u32[]{:S(2)}) copy-start(f32[128,3072]{0,1:T(8,128)} %copy-done.7) | copy-start | bytes 4718596
  415.7 11.1 %copy-start.21 = (pred[128,768]{0,1:T(8,128)(4,1)S(1)}, pred[128,768]{0,1:T(8,128)(4,1)}, u32[]{:S(2)}) copy-start(pred[128,768]{0,1:T(8,128)(4,1)} %get-tuple-element.41) | copy-start | bytes 294916
  426.8 18.4 %copy-start.1 = (f32[768,3072]{0,1:T(8,128)}, f32[768,3072]{0,1:T(8,128)S(1)}, u32[]{:S(2)}) copy-start(f32[768,3072]{0,1:T(8,128)S(1)} %get-tuple-element.35) | copy-start | bytes 28311556
  426.8 24.5 %copy-start.14 = (f32[128,3072]{0,1:T(8,128)S(1)}, f32[128,3072]{0,1:T(8,128)}, u32[]{:S(2)}) copy-start(f32[128,3072]{0,1:T(8,128)} %copy.82) | copy-start | bytes 4718596
  445.2 6.4 copy-start.2
  445.2 6.4 copy-start.37
  451.6 12.6 %copy-start.23 = (f32[24,128,128]{2,1,0:T(8,128)S(1)}, f32[24,128,128]{2,1,0:T(8,128)}, u32[]{:S(2)}) copy-start(f32[24,128,128]{2,1,0:T(8,128)} %fusion.32) | copy-start | bytes 4718596
  451.6 12.6 %copy-start.28 = (f32[128,24]{0,1:T(8,128)S(1)}, f32[128,24]{0,1:T(8,128)}, u32[]{:S(2)}) copy-start(f32[128,24]{0,1:T(8,128)} %copy-done.26) | copy-start | bytes 36868
  451.6 12.6 %copy-start.40 = (f32[128,24]{0,1:T(8,128)S(1)}, f32[128,24]{0,1:T(8,128)}, u32[]{:S(2)}) copy-start(f32[128,24]{0,1:T(8,128)} %multiply_divide_fusion.6) | copy-start | bytes 36868
  533.6 5.8 copy-start
  549.4 6.4 copy-start.32
  549.4 15.4 %copy-start.9 = (f32[128,3072]{0,1:T(8,128)S(1)}, f32[128,3072]{0,1:T(8,128)}, u32[]{:S(2)}) copy-start(f32[128,3072]{0,1:T(8,128)} %copy-done.7) | copy-start | bytes 4718596
  549.4 15.4 %copy-start.36 = (f32[128,24]{0,1:T(8,128)S(1)}, f32[128,24]{0,1:T(8,128)}, u32[]{:S(2)}) copy-start(f32[128,24]{0,1:T(8,128)} %copy-done.35) | copy-start | bytes 36868
  555.9 274.2 %collective-permute-start.6 = (f32[64,6144]{1,0:T(8,128)}, f32[64,6144]{1,0:T(8,128)}, u32[]{:S(2)}, u32[]{:S(2)}) collective-permute-start(f32[64,6144]{1,0:T(8,128)} %get-tuple-element.33), channel_id=1, source_target_pairs={{1,0},{2,1},{3,2},{4,3},{5,4},{6,5},{7,6},{8,7},{9,8},{10,9},{11,1... | collective-permute-start | bytes 4718600 | tf_op jit(solution)/shard_map/ppermute | solution.py:26
  560.9 303.0 %collective-permute-start.10 = (f32[128,6144]{1,0:T(8,128)}, f32[128,6144]{1,0:T(8,128)}, u32[]{:S(2)}, u32[]{:S(2)}) collective-permute-start(f32[128,6144]{1,0:T(8,128)} %get-tuple-element.30), channel_id=1, source_target_pairs={{2,0},{3,1},{0,2},{1,3},{6,4},{7,5},{4,6},{5,7},{10,8},{11,9},{8,1... | collective-permute-start | bytes 9437192 | tf_op jit(solution)/shard_map/ppermute | solution.py:36
  561.0 302.9 %collective-permute-start.9 = (f32[128,6144]{1,0:T(8,128)}, f32[128,6144]{1,0:T(8,128)}, u32[]{:S(2)}, u32[]{:S(2)}) collective-permute-start(f32[128,6144]{1,0:T(8,128)} %get-tuple-element.31), channel_id=1, source_target_pairs={{2,0},{3,1},{0,2},{1,3},{6,4},{7,5},{4,6},{5,7},{10,8},{11,9},{8,1... | collective-permute-start | bytes 9437192 | tf_op jit(solution)/shard_map/ppermute | solution.py:36
  562.4 301.5 %collective-permute-start.7 = (f32[128,6144]{1,0:T(8,128)}, f32[128,6144]{1,0:T(8,128)}, u32[]{:S(2)}, u32[]{:S(2)}) collective-permute-start(f32[128,6144]{1,0:T(8,128)} %get-tuple-element.29), channel_id=1, source_target_pairs={{3,0},{0,1},{1,2},{2,3},{7,4},{4,5},{5,6},{6,7},{11,8},{8,9},{9,10... | collective-permute-start | bytes 9437192 | tf_op jit(solution)/shard_map/ppermute | solution.py:36
  562.4 301.5 %collective-permute-start.8 = (f32[128,6144]{1,0:T(8,128)}, f32[128,6144]{1,0:T(8,128)}, u32[]{:S(2)}, u32[]{:S(2)}) collective-permute-start(f32[128,6144]{1,0:T(8,128)} %get-tuple-element.28), channel_id=1, source_target_pairs={{1,0},{2,1},{3,2},{0,3},{5,4},{6,5},{7,6},{4,7},{9,8},{10,9},{11,1... | collective-permute-start | bytes 9437192 | tf_op jit(solution)/shard_map/ppermute | solution.py:36
  830.1 8.4 copy-start.6
  830.1 8.4 copy-start.11
  830.1 33.8 %collective-permute-start.5 = (f32[64,6144]{1,0:T(8,128)}, f32[64,6144]{1,0:T(8,128)}, u32[]{:S(2)}, u32[]{:S(2)}) collective-permute-start(f32[64,6144]{1,0:T(8,128)} %get-tuple-element.32), channel_id=1, source_target_pairs={{0,1},{1,2},{2,3},{3,4},{4,5},{5,6},{6,7},{7,8},{8,9},{9,10},{10,1... | collective-permute-start | bytes 4718600 | tf_op jit(solution)/shard_map/ppermute | solution.py:24
  838.5 3.8 copy-start.30
  838.5 3.9 copy-start.34
  845.0 27.0 %copy-start.17 = (f32[128,3072]{1,0:T(8,128)S(1)}, f32[128,3072]{1,0:T(8,128)}, u32[]{:S(2)}) copy-start(f32[128,3072]{1,0:T(8,128)} %copy.97) | copy-start | bytes 4718596
  845.0 27.1 %copy-start.18 = (f32[128,3072]{1,0:T(8,128)S(1)}, f32[128,3072]{1,0:T(8,128)}, u32[]{:S(2)}) copy-start(f32[128,3072]{1,0:T(8,128)} %copy.95) | copy-start | bytes 4718596
  (8 other events, 15.8 us)
Sparse Core Ops, SparseCore 0:
  83.6 297.3 all-reduce.4
where the time goes:
time: 893 us; the launch traced here: 881 us
  waiting for transfers between devices  276 us (31%)
  blocking collectives  274 us (31%)
  matrix products  162 us (18%)
  local copies, waits for them, and re-layouts  88.9 us (10%)
  other arithmetic  41.1 us (5%)
  starting transfers between devices  23.5 us (3%)
  between operations  15.6 us (2%)
    psum x1, blocking collectives, shards(): sums_grad, totals_grad = lax.psum((sums_part, totals_part), ('seq', 'blk'))  233 us
    ppermute x2, waiting for transfers between devices, extended(): lax.ppermute(tail, axis, [(i, (i + 1) % count) for i in range(ends)])  194 us
    psum x1, waiting for transfers between devices, shards(): lax.psum((partial_sums[0], partial_sums[1]), ('seq', 'blk'))  65.1 us
    dot_general x3, matrix products, sparse_block(): mixed = jnp.einsum('hij,jhd->ihd', weights, value_heads, precision=HIGH)  49.7 us
    dot_general x3, matrix products, sparse_block(): jnp.einsum('ihd,jhd->hij', query_heads, key_heads, precision=HIGH)  46.5 us
    psum x1, blocking collectives, shards(): lax.psum((partial_sums[0], partial_sums[1]), ('seq', 'blk'))  41 us
    dot_general x3, matrix products, key_side(): jnp.einsum('nhf,nhd->hfd', key_feats, value_heads, precision=HIGH)  22.8 us
    concatenate x1, local copies, waits for them, and re-layouts, shards(): all_paired = jnp.concatenate([padded] + tile_rows, axis=0)  21.7 us
  transfers between devices with their start and end apart: 12, of which 4 were waited for; matrix products, arithmetic and copies ran while one was open for 10% of the time, Pallas kernels for 0%

commit v1 on v0

v1 whole, which is shorter than its diff:
```python
import functools
import math

import jax
import jax.numpy as jnp
from jax import lax
from jax.experimental import pallas as pl
from jax.experimental.pallas import tpu as pltpu
from jax.sharding import PartitionSpec as P

HEAD_DIM = 128
EXT = 8
NEG_FILL = -1e30
SEED_DIV = 13.0
EPS = 1e-06
F32 = jnp.float32
BF16 = jnp.bfloat16


def split2(x):
    high = x.astype(BF16)
    return high, (x - high.astype(F32)).astype(BF16)


def mm(a, b):
    return lax.dot_general(a, b, (((1,), (0,)), ((), ())), preferred_element_type=F32)


def mm3(a, b):
    return mm(a[0], b[0]) + (mm(a[0], b[1]) + mm(a[1], b[0]))


def mm2(exact, b):
    return mm(exact, b[0]) + mm(exact, b[1])


def normed_t(x_t):
    scale = lax.rsqrt(jnp.mean(x_t * x_t, axis=0, keepdims=True) + EPS)
    return x_t * scale, scale


def features_t(seed_t, normed):
    return jnp.exp(mm2(seed_t, split2(normed)) * (1.0 / SEED_DIV))


def normed_grad_t(seed, feats_t, dfeats_t, normed, scale):
    grad = mm2(seed, split2(dfeats_t * feats_t)) * (1.0 / SEED_DIV)
    return scale * (grad - normed * jnp.mean(grad * normed, axis=0, keepdims=True))


def column_to_rows(column):
    wide = jnp.transpose(jnp.broadcast_to(column, (column.shape[0], 128)))
    row = lax.broadcasted_iota(jnp.int32, (EXT, 128), 0)
    return jnp.where(row == 0, wide[:EXT, :128], wide[:EXT, 128:])


def rows_to_column(block):
    row = jnp.concatenate([block[0:1], block[1:2]], axis=1)
    return jnp.transpose(jnp.broadcast_to(row, (128, row.shape[1])))[:, :1]


def assemble(scratch, refs, member, rows):
    for distance, ref in enumerate(refs):
        place = pl.multiple_of(jnp.bitwise_xor(member, distance) * rows, rows)
        scratch[pl.ds(place, rows), :] = ref[...]


def gate_row(ext, head, members):
    logits = jnp.concatenate([ext[pl.ds(m * EXT + head, 1), :] for m in range(members)], axis=1)
    return 1.0 / (1.0 + jnp.exp(-logits))


def copy_kernel(moves_of, n_in, *refs):
    index, ins, outs, sems = refs[0], refs[1 : 1 + n_in], refs[1 + n_in : -1], refs[-1]
    copies = [
        pltpu.make_async_copy(source, target, sems.at[position])
        for position, (source, target) in enumerate(moves_of(index, ins, outs))
    ]
    for copy in copies:
        copy.start()
    for copy in copies:
        copy.wait()


def local_copies(moves_of, n_moves, index, ins, out_shapes, name):
    size = sum(math.prod(s.shape) * 4 for s in out_shapes)
    return pl.pallas_call(
        functools.partial(copy_kernel, moves_of, len(ins)),
        grid_spec=pltpu.PrefetchScalarGridSpec(
            num_scalar_prefetch=1,
            grid=(1,),
            in_specs=[pl.BlockSpec(memory_space=pl.ANY)] * len(ins),
            out_specs=[pl.BlockSpec(s.shape, lambda i, ref: (0, 0)) for s in out_shapes],
            scratch_shapes=[pltpu.SemaphoreType.DMA((n_moves,))],
        ),
        out_shape=out_shapes,
        compiler_params=pltpu.CompilerParams(vmem_limit_bytes=32 * 1024 * 1024),
        cost_estimate=pl.CostEstimate(flops=0, bytes_accessed=2 * size, transcendentals=0),
        name=name,
    )(index, *ins)


def sums_kernel(members, rows, heads, index, *refs):
    key_refs, value_refs = refs[:members], refs[members : 2 * members]
    seed_t_ref = refs[2 * members]
    keys_out, values_out, sums_out, low_edge, high_edge = refs[2 * members + 1 :]
    head = pl.program_id(0)
    member = index[0]
    tokens = members * rows
    reach = rows // 2

    @pl.when(head == 0)
    def _():
        sums_out[pl.ds(heads * 256, sums_out.shape[0] - heads * 256), :] = jnp.zeros(
            (sums_out.shape[0] - heads * 256, 128), F32
        )

    assemble(keys_out, key_refs, member, rows)
    assemble(values_out, value_refs, member, rows)
    keys, values = keys_out[...], values_out[...]
    low_edge[:reach] = keys[:reach]
    low_edge[reach:] = values[:reach]
    high_edge[:reach] = keys[tokens - reach :]
    high_edge[reach:] = values[tokens - reach :]
    normed, _ = normed_t(jnp.transpose(keys))
    feats = features_t(seed_t_ref[...], normed)
    sums_out[pl.ds(pl.multiple_of(head * 256, 256), 256), :] = mm3(split2(feats), split2(values))
    sums_out[pl.ds(pl.multiple_of(heads * 256 + head * EXT, EXT), EXT), :] = column_to_rows(
        jnp.sum(feats, axis=1, keepdims=True)
    )


def query_kernel(members, rows, heads, index, *refs):
    query_refs, grad_refs = refs[:members], refs[members : 2 * members]
    ext_refs = refs[2 * members : 3 * members]
    sums_ref, seed_ref, seed_t_ref = refs[3 * members : 3 * members + 3]
    low_out, query_out, sums_out, queries, grads, ext = refs[3 * members + 3 :]
    head = pl.program_id(0)
    member = index[0]

    @pl.when(head == 0)
    def _():
        assemble(ext, ext_refs, member, EXT)
        sums_out[pl.ds(heads * 256, sums_out.shape[0] - heads * 256), :] = jnp.zeros(
            (sums_out.shape[0] - heads * 256, 128), F32
        )

    assemble(queries, query_refs, member, rows)
    assemble(grads, grad_refs, member, rows)
    gate = gate_row(ext, head, members)
    sums = sums_ref[pl.ds(pl.multiple_of(head * 256, 256), 256), :]
    totals = rows_to_column(sums_ref[pl.ds(pl.multiple_of(heads * 256 + head * EXT, EXT), EXT), :])
    normed, scale = normed_t(jnp.transpose(queries[...]))
    feats = features_t(seed_t_ref[...], normed)
    feats_parts = split2(feats)
    inverse = 1.0 / jnp.sum(feats * totals, axis=0, keepdims=True)
    low = mm3(split2(jnp.transpose(sums)), feats_parts) * inverse
    dnum = jnp.transpose(grads[...]) * ((1.0 - gate) * inverse)
    dden = -jnp.sum(dnum * low, axis=0, keepdims=True)
    dfeats = mm3(split2(sums), split2(dnum)) + totals * dden
    low_out[...] = low
    query_out[...] = normed_grad_t(seed_ref[...], feats, dfeats, normed, scale)
    sums_out[pl.ds(pl.multiple_of(head * 256, 256), 256), :] = mm3(
        feats_parts, split2(jnp.transpose(dnum))
    )
    sums_out[pl.ds(pl.multiple_of(heads * 256 + head * EXT, EXT), EXT), :] = column_to_rows(
        jnp.sum(feats * dden, axis=1, keepdims=True)
    )


def fill_bias(bias, ext, members, rows, first, last):
    reach = rows // 2
    key_at = lax.broadcasted_iota(jnp.int32, (rows, rows), 0)
    query_at = lax.broadcasted_iota(jnp.int32, (rows, rows), 1)
    for block in range(members):
        for other in range(members):
            gap = (other - block) * rows + key_at - query_at
            allowed = jnp.abs(gap) <= reach
            if other != block:
                flag = ext[block * EXT + EXT - 1 : block * EXT + EXT, other : other + 1]
                allowed = jnp.logical_or(allowed, jnp.broadcast_to(flag, (rows, rows)) > 0.5)
            bias[other * rows : (other + 1) * rows, block * rows : (block + 1) * rows] = jnp.where(
                allowed, 0.0, NEG_FILL
            )
        allowed = jnp.zeros((rows, rows), jnp.bool_)
        if block == 0:
            allowed = (key_at < reach) & (query_at <= key_at) & (first == 0)
        if block == members - 1:
            right = (key_at >= reach) & (query_at >= key_at) & (last == 0)
            allowed = jnp.logical_or(allowed, right)
        bias[members * rows :, block * rows : (block + 1) * rows] = jnp.where(
            allowed, 0.0, NEG_FILL
        )


def sparse_kernel(members, rows, heads, index, *refs):
    query_refs, grad_refs = refs[:members], refs[members : 2 * members]
    ext_refs = refs[2 * members : 3 * members]
    keys_ref, values_ref, left_ref, right_ref, low_ref, query_low_ref = refs[
        3 * members : 3 * members + 6
    ]
    outs = refs[3 * members + 6 :]
    messages = outs[:members]
    keys_out, values_out, left_out, right_out = outs[members : members + 4]
    queries, grads, ext, bias, keys_all, values_all = outs[members + 4 :]
    head = pl.program_id(0)
    member = index[0]
    tokens = members * rows
    reach = rows // 2

    @pl.when(head == 0)
    def _():
        assemble(ext, ext_refs, member, EXT)
        fill_bias(bias, ext, members, rows, index[1], index[2])
        for message in messages:
            message[pl.ds(2 * heads * rows, EXT), :] = jnp.zeros((EXT, 128), F32)

    assemble(queries, query_refs, member, rows)
    assemble(grads, grad_refs, member, rows)
    keys_all[:tokens] = keys_ref[...]
    keys_all[tokens : tokens + reach] = left_ref[:reach]
    keys_all[tokens + reach :] = right_ref[:reach]
    values_all[:tokens] = values_ref[...]
    values_all[tokens : tokens + reach] = left_ref[reach:]
    values_all[tokens + reach :] = right_ref[reach:]

    gate = gate_row(ext, head, members)
    root = 1.0 / math.sqrt(HEAD_DIM)
    keys = split2(keys_all[...])
    values = split2(values_all[...])
    keys_t = split2(jnp.transpose(keys_all[...]))
    values_t = split2(jnp.transpose(values_all[...]))
    scaled = queries[...] * root
    scores = mm3(keys, split2(jnp.transpose(scaled))) + bias[...]
    weights = jnp.exp(scores - jnp.max(scores, axis=0, keepdims=True))
    inverse = 1.0 / jnp.sum(weights, axis=0, keepdims=True)
    weight_parts = split2(weights)
    mixed = mm3(values_t, weight_parts) * inverse
    low = low_ref[...]
    grad_t = jnp.transpose(grads[...])
    gate_grad = jnp.sum(grad_t * (mixed - low), axis=0, keepdims=True) * gate * (1.0 - gate)
    sparse_grad = grad_t * (gate * inverse)
    delta = jnp.sum(sparse_grad * mixed, axis=0, keepdims=True)
    score_grad = weights * (mm3(values, split2(sparse_grad)) - delta)
    score_parts = split2(score_grad)
    query_grad = mm3(keys_t, score_parts) * root + query_low_ref[...]
    keys_grad = mm3(score_parts, split2(scaled))
    values_grad = mm3(weight_parts, split2(jnp.transpose(sparse_grad)))
    keys_out[...] = keys_grad[:tokens]
    values_out[...] = values_grad[:tokens]
    left_out[:reach] = keys_grad[tokens : tokens + reach]
    left_out[reach:] = values_grad[tokens : tokens + reach]
    right_out[:reach] = keys_grad[tokens + reach :]
    right_out[reach:] = values_grad[tokens + reach :]
    queries[...] = jnp.transpose(gate * mixed + (1.0 - gate) * low)
    grads[...] = jnp.transpose(query_grad)
    for m in range(members):
        ext[pl.ds(m * EXT + head, 1), :] = gate_grad[:, m * rows : (m + 1) * rows]
    for distance, message in enumerate(messages):
        other = jnp.bitwise_xor(member, distance)
        place = pl.ds(pl.multiple_of(other * rows, rows), rows)
        start = pl.multiple_of(head * 2 * rows, rows)
        message[pl.ds(start, rows), :] = queries[place, :]
        message[pl.ds(start + rows, rows), :] = grads[place, :]

    @pl.when(head == heads - 1)
    def _():
        for distance, message in enumerate(messages):
            other = jnp.bitwise_xor(member, distance)
            message[pl.ds(2 * heads * rows, EXT), :] = ext[
                pl.ds(pl.multiple_of(other * EXT, EXT), EXT), :
            ]


def keys_kernel(members, rows, heads, index, *refs):
    (keys_ref, values_ref, sums_ref, keys_grad, values_grad, left_ref, right_ref, seed_ref, seed_t_ref) = refs[:9]
    messages = refs[9 : 9 + members]
    dkeys, dvalues = refs[9 + members :]
    head = pl.program_id(0)
    member = index[0]
    tokens = members * rows
    reach = rows // 2
    sums = sums_ref[pl.ds(pl.multiple_of(head * 256, 256), 256), :]
    totals = rows_to_column(sums_ref[pl.ds(pl.multiple_of(heads * 256 + head * EXT, EXT), EXT), :])
    normed, scale = normed_t(jnp.transpose(keys_ref[...]))
    feats = features_t(seed_t_ref[...], normed)
    dfeats = mm3(split2(sums), split2(jnp.transpose(values_ref[...]))) + totals
    key_low = normed_grad_t(seed_ref[...], feats, dfeats, normed, scale)
    value_low = mm3(split2(jnp.transpose(sums)), split2(feats))
    dkeys[...] = keys_grad[...] + jnp.transpose(key_low)
    dvalues[...] = values_grad[...] + jnp.transpose(value_low)
    dkeys[:reach] += left_ref[:reach]
    dvalues[:reach] += left_ref[reach:]
    dkeys[tokens - reach :] += right_ref[:reach]
    dvalues[tokens - reach :] += right_ref[reach:]
    for distance, message in enumerate(messages):
        other = jnp.bitwise_xor(member, distance)
        place = pl.ds(pl.multiple_of(other * rows, rows), rows)
        message[:rows] = dkeys[place, :]
        message[rows:] = dvalues[place, :]


def per_head_call(kernel, members, rows, heads, index, ins, outs, scratch, flops, exps, name):
    in_specs = [spec for _, spec in ins]
    size = sum(math.prod(x.shape) * 4 for x, _ in ins[-4:]) + sum(math.prod(s.shape) * 4 for s, _ in outs)
    return pl.pallas_call(
        functools.partial(kernel, members, rows, heads),
        grid_spec=pltpu.PrefetchScalarGridSpec(
            num_scalar_prefetch=1,
            grid=(heads,),
            in_specs=in_specs,
            out_specs=[spec for _, spec in outs],
            scratch_shapes=scratch,
        ),
        out_shape=[shape for shape, _ in outs],
        compiler_params=pltpu.CompilerParams(
            vmem_limit_bytes=56 * 1024 * 1024, dimension_semantics=("arbitrary",)
        ),
        cost_estimate=pl.CostEstimate(flops=flops, bytes_accessed=size, transcendentals=exps),
        name=name,
    )(index, *[x for x, _ in ins])


def swap(block, axis, distance):
    return lax.ppermute(block, axis, [(i, i ^ distance) for i in range(lax.axis_size(axis))])


def sum_over_seq(cells):
    count = lax.axis_size("seq")
    place = lax.axis_index("seq")
    core, chip = place & 1, place >> 1
    chips = count // 2
    half = cells.shape[0] // 2
    part = half // chips

    def cut(x, at, size):
        return lax.dynamic_slice_in_dim(x, at * size, size, 0)

    summed = cut(cells, core, half) + swap(cut(cells, 1 - core, half), "seq", 1)
    own = cut(summed, chip, part)
    for d in range(1, chips):
        own = own + swap(cut(summed, chip ^ d, part), "seq", 2 * d)
    gathered = jnp.zeros((half, cells.shape[1]), F32)
    gathered = lax.dynamic_update_slice_in_dim(gathered, own, chip * part, 0)
    for d in range(1, chips):
        gathered = lax.dynamic_update_slice_in_dim(
            gathered, swap(own, "seq", 2 * d), (chip ^ d) * part, 0
        )
    other = swap(gathered, "seq", 1)
    first = jnp.where(core == 0, gathered, other)
    second = jnp.where(core == 0, other, gathered)
    return jnp.concatenate([first, second], axis=0)


def to_next(block):
    count = lax.axis_size("seq")
    return lax.ppermute(block, "seq", [(i, i + 1) for i in range(count - 1)])


def to_previous(block):
    count = lax.axis_size("seq")
    return lax.ppermute(block, "seq", [(i + 1, i) for i in range(count - 1)])


def shards(
    queries,
    key_matrix,
    value_matrix,
    gate_logits,
    output_grad,
    cycle_offsets,
    block_count,
    feature_seed,
):
    rows, width = queries.shape
    members = lax.axis_size("blk")
    member = lax.axis_index("blk")
    groups = lax.axis_size("seq")
    group = lax.axis_index("seq")
    heads = gate_logits.shape[1] // members
    tokens = members * rows
    others = range(1, members)
    index = jnp.stack(
        [member, (group == 0).astype(jnp.int32), (group == groups - 1).astype(jnp.int32)]
    ).astype(jnp.int32)
    sum_rows = -(-(heads * (256 + EXT)) // (EXT * groups)) * EXT * groups

    def shape(*dims):
        return jax.ShapeDtypeStruct(dims, F32)

    def block_of(message_rows, at):
        return pl.BlockSpec((message_rows, 128), lambda h, ref: (at(h, ref), 0))

    own_spec = pl.BlockSpec((rows, 128), lambda h, ref: (0, ref[0] * heads + h))
    head_spec = pl.BlockSpec((tokens, 128), lambda h, ref: (h, 0))
    edge_spec = pl.BlockSpec((rows, 128), lambda h, ref: (h, 0))
    wide_spec = pl.BlockSpec((128, tokens), lambda h, ref: (h, 0))

    def whole(x):
        return pl.BlockSpec(x.shape, lambda h, ref: (0,) * len(x.shape))

    def packing(index, ins, outs, extra):
        moves = []
        for d, out in zip(others, outs):
            other = jnp.bitwise_xor(index[0], d)
            for a in range(2):
                for h in range(heads):
                    column = pl.multiple_of((other * heads + h) * 128, 128)
                    moves.append(
                        (ins[a].at[:, pl.ds(column, 128)], out.at[pl.ds((a * heads + h) * rows, rows), :])
                    )
            if extra:
                start = pl.multiple_of(other * EXT, EXT)
                moves.append(
                    (ins[2].at[pl.ds(start, EXT), :], out.at[pl.ds(2 * heads * rows, EXT), :])
                )
        return moves

    def unpacking(index, ins, outs):
        moves = []
        for d, message in enumerate(ins):
            other = jnp.bitwise_xor(index[0], d)
            for a in range(2):
                for h in range(heads):
                    column = pl.multiple_of((other * heads + h) * 128, 128)
                    moves.append(
                        (message.at[pl.ds((2 * h + a) * rows, rows), :], outs[a].at[:, pl.ds(column, 128)])
                    )
        return moves

    kv_sent = local_copies(
        functools.partial(packing, extra=False),
        2 * heads * (members - 1),
        index,
        [key_matrix, value_matrix],
        [shape(2 * heads * rows, 128)] * (members - 1),
        "pack_kv",
    )
    kv = [swap(block, "blk", d) for d, block in zip(others, kv_sent)]

    active = jnp.arange(cycle_offsets.shape[1], dtype=jnp.int32) < block_count[0]
    named = jnp.mod(cycle_offsets[0] + member, members)
    lanes = jnp.arange(128, dtype=jnp.int32)
    flags = jnp.any(active[:, None] & (named[:, None] == lanes[None, :]), axis=0).astype(F32)
    logits = jnp.transpose(gate_logits).reshape(members, heads, rows)
    ext = jnp.concatenate(
        [
            logits,
            jnp.zeros((members, EXT - 1 - heads, rows), F32),
            jnp.broadcast_to(flags[None, None, :], (members, 1, 128)),
        ],
        axis=1,
    ).reshape(members * EXT, 128)
    qd_sent = local_copies(
        functools.partial(packing, extra=True),
        (2 * heads + 1) * (members - 1),
        index,
        [queries, output_grad, ext],
        [shape(2 * heads * rows + EXT, 128)] * (members - 1),
        "pack_qd",
    )
    kv, qd_sent = lax.optimization_barrier((kv, qd_sent))
    qd = [swap(block, "blk", d) for d, block in zip(others, qd_sent)]

    seed = feature_seed.astype(BF16)
    seed_t = jnp.transpose(feature_seed).astype(BF16)
    unit = 2 * tokens * 128 * 256
    first_block = block_of(rows, lambda h, ref: h)
    second_block = block_of(rows, lambda h, ref: heads + h)
    keys_full, values_full, sums, low_edge, high_edge = per_head_call(
        sums_kernel,
        members,
        rows,
        heads,
        index,
        [(key_matrix, own_spec)]
        + [(x, first_block) for x in kv]
        + [(value_matrix, own_spec)]
        + [(x, second_block) for x in kv]
        + [(seed_t, whole(seed_t))],
        [
            (shape(heads * tokens, 128), head_spec),
            (shape(heads * tokens, 128), head_spec),
            (shape(sum_rows, 128), whole(shape(sum_rows, 128))),
            (shape(heads * rows, 128), edge_spec),
            (shape(heads * rows, 128), edge_spec),
        ],
        [],
        5 * unit * heads,
        heads * tokens * 256,
        "key_sums",
    )
    right_halo = to_previous(low_edge)
    left_halo = to_next(high_edge)
    sums = sum_over_seq(sums)

    ext_block = block_of(EXT, lambda h, ref: 2 * heads * rows // EXT)
    query_side = (
        [(queries, own_spec)]
        + [(x, first_block) for x in qd]
        + [(output_grad, own_spec)]
        + [(x, second_block) for x in qd]
        + [(ext, block_of(EXT, lambda h, ref: ref[0]))]
        + [(x, ext_block) for x in qd]
    )
    row_scratch = [
        pltpu.VMEM((tokens, 128), F32),
        pltpu.VMEM((tokens, 128), F32),
        pltpu.VMEM((members * EXT, 128), F32),
    ]
    low, query_low, sums_grad = per_head_call(
        query_kernel,
        members,
        rows,
        heads,
        index,
        query_side + [(sums, whole(sums)), (seed, whole(seed)), (seed_t, whole(seed_t))],
        [
            (shape(heads * 128, tokens), wide_spec),
            (shape(heads * 128, tokens), wide_spec),
            (shape(sum_rows, 128), whole(shape(sum_rows, 128))),
        ],
        row_scratch,
        13 * unit * heads,
        heads * tokens * 256,
        "query_low_rank",
    )
    sums_grad = sum_over_seq(sums_grad)

    message = shape(2 * heads * rows + EXT, 128)
    sparse_outs = per_head_call(
        sparse_kernel,
        members,
        rows,
        heads,
        index,
        query_side
        + [
            (keys_full, head_spec),
            (values_full, head_spec),
            (left_halo, edge_spec),
            (right_halo, edge_spec),
            (low, wide_spec),
            (query_low, wide_spec),
        ],
        [(message, whole(message))] * members
        + [
            (shape(heads * tokens, 128), head_spec),
            (shape(heads * tokens, 128), head_spec),
            (shape(heads * rows, 128), edge_spec),
            (shape(heads * rows, 128), edge_spec),
        ],
        row_scratch
        + [
            pltpu.VMEM((tokens + rows, tokens), F32),
            pltpu.VMEM((tokens + rows, 128), F32),
            pltpu.VMEM((tokens + rows, 128), F32),
        ],
        36 * tokens * (tokens + rows) * 128 * heads,
        heads * tokens * (tokens + rows),
        "sparse",
    )
    od_sent = sparse_outs[:members]
    keys_sparse, values_sparse, left_grad, right_grad = sparse_outs[members:]
    od = [od_sent[0]] + [swap(block, "blk", d) for d, block in zip(others, od_sent[1:])]
    back_right = to_previous(left_grad)
    back_left = to_next(right_grad)

    dkv_sent = per_head_call(
        keys_kernel,
        members,
        rows,
        heads,
        index,
        [
            (keys_full, head_spec),
            (values_full, head_spec),
            (sums_grad, whole(sums_grad)),
            (keys_sparse, head_spec),
            (values_sparse, head_spec),
            (back_left, edge_spec),
            (back_right, edge_spec),
            (seed, whole(seed)),
            (seed_t, whole(seed_t)),
        ],
        [(shape(2 * heads * rows, 128), pl.BlockSpec((2 * rows, 128), lambda h, ref: (h, 0)))]
        * members,
        [pltpu.VMEM((tokens, 128), F32), pltpu.VMEM((tokens, 128), F32)],
        10 * unit * heads,
        heads * tokens * 256,
        "key_low_rank",
    )
    dkv = [dkv_sent[0]] + [swap(block, "blk", d) for d, block in zip(others, dkv_sent[1:])]

    attended, query_grad = local_copies(
        unpacking, 2 * heads * members, index, od, [shape(rows, width)] * 2, "unpack_od"
    )
    ext_back = jnp.zeros((members, EXT, 128), F32)
    for d, block in enumerate(od):
        ext_back = lax.dynamic_update_slice_in_dim(
            ext_back, block[None, 2 * heads * rows :, :], member ^ d, 0
        )
    gate_grad = jnp.transpose(ext_back[:, :heads, :].reshape(members * heads, rows))
    key_grad, value_grad = local_copies(
        unpacking, 2 * heads * members, index, dkv, [shape(rows, width)] * 2, "unpack_kv"
    )
    return (attended, query_grad, key_grad, value_grad, gate_grad)


def solution(mesh):
    row_spec = P(("seq", "blk"), None)
    return jax.shard_map(
        shards,
        mesh=mesh,
        in_specs=(row_spec,) * 6 + (P(("seq", "blk")), P()),
        out_specs=(row_spec,) * 5,
        check_vma=False,
    )
```

time: 893 us -> 278 us (0.31); the launches traced: 881 us -> 277 us
  blocking collectives: 274 us -> 0 us
  matrix products: 162 us -> 0 us
  waiting for transfers between devices: 276 us -> 128 us
  local copies, waits for them, and re-layouts: 88.9 us -> 15.2 us
  Pallas kernels: 0 us -> 68.6 us
  other arithmetic: 41.1 us -> 8.69 us
  starting transfers between devices: 23.5 us -> 54.9 us
  between operations: 15.6 us -> 1.74 us
    psum x2 -> x0, blocking collectives: 274 us -> none  [the longest x1 233 us: shards(): sums_grad, totals_grad = lax.psum((sums_part, totals_part), ('seq', 'blk'))]
    dot_general x18 -> x0, matrix products: 162 us -> none  [the longest x3 49.7 us: sparse_block(): mixed = jnp.einsum('hij,jhd->ihd', weights, value_heads, precision=HIGH)]
    ppermute x11 -> x32, waiting for transfers between devices: 210 us -> 128 us  [the longest x28 122 us: swap(): lax.ppermute(block, axis, [(i, i ^ distance) for i in range(lax.axis_size...]
    pallas_call x0 -> x8, Pallas kernels: none -> 68.6 us  [the longest x4 57.1 us: per_head_call(): pl.pallas_call(functools.partial(kernel, members, rows, heads), grid_spec...]
    psum x1 -> x0, waiting for transfers between devices: 65.1 us -> none  [shards(): lax.psum((partial_sums[0], partial_sums[1]), ('seq', 'blk'))]
    ppermute x11 -> x32, starting transfers between devices: 23.5 us -> 54.9 us  [the longest x28 44.2 us: swap(): lax.ppermute(block, axis, [(i, i ^ distance) for i in range(lax.axis_size...]
    reshape x4 -> x2, local copies, waits for them, and re-layouts: 23.9 us -> 0.61 us  [the longest x1 0.6 us: shards(): ext_back[:, :heads, :].reshape(members * heads, rows)]
    concatenate x2 -> x1, local copies, waits for them, and re-layouts: 21.7 us -> 0.07 us  [shards(): jnp.concatenate([logits, jnp.zeros((members, EXT - 1 - heads, rows), F32)...]
  transfers between devices with their start and end apart: 12 -> 32, of which waited for: 4 -> 21; matrix products, arithmetic and copies ran while one was open for 10% -> 3% of each run, Pallas kernels for 0% -> 15%
where the time goes in v1:
time: 278 us; the launch traced here: 277 us
  waiting for transfers between devices  128 us (46%)
  Pallas kernels  68.6 us (25%)
  starting transfers between devices  54.9 us (20%)
  local copies, waits for them, and re-layouts  15.2 us (5%)
  other arithmetic  8.69 us (3%)
    ppermute x28, waiting for transfers between devices, swap(): lax.ppermute(block, axis, [(i, i ^ distance) for i in range(lax.axis_size...  122 us
    pallas_call x4, Pallas kernels, per_head_call(): pl.pallas_call(functools.partial(kernel, members, rows, heads), grid_spec...  57.1 us
    ppermute x28, starting transfers between devices, swap(): lax.ppermute(block, axis, [(i, i ^ distance) for i in range(lax.axis_size...  44.2 us
    pallas_call x4, Pallas kernels, local_copies(): pl.pallas_call(functools.partial(copy_kernel, moves_of, len(ins)), grid_s...  11.5 us
    unnamed x47, local copies, waits for them, and re-layouts  8.18 us
    ppermute x2, starting transfers between devices, to_next(): return lax.ppermute(block, 'seq', [(i, i + 1) for i in range(count - 1)])  6.66 us
  transfers between devices with their start and end apart: 32, of which 21 were waited for; matrix products, arithmetic and copies ran while one was open for 3% of the time, Pallas kernels for 15%

profile of v1, /device:TPU:1, one launch (start us, length us, event | category | flops | bytes accessed | tf_op | source)
XLA Modules:
  0.0 276.9 jit_solution(7657398722721600893)
XLA Ops:
  0.7 1.4 copy-done
  2.1 1.4 copy-done.1
  3.5 2.7 pack_kv.1
  6.3 2.1 collective-permute-start
  8.4 1.2 collective-permute-start.1
  12.3 1.4 pack_qd.1
  17.0 9.0 %collective-permute-done.refs_1_.refs_5_ = f32[1536,128]{1,0:T(8,128)} collective-permute-done((f32[1536,128]{1,0:T(8,128)}, f32[1536,128]{1,0:T(8,128)}, u32[]{:S(2)}, u32[]{:S(2)}) %collective-permute-start) | collective-permute-done | bytes 786464 | tf_op jit(solution)/shard_map/ppermute | solution.py:325
  26.8 17.0 %collective-permute-done.2.refs_3_.refs_7_ = f32[1536,128]{1,0:T(8,128)} collective-permute-done((f32[1536,128]{1,0:T(8,128)}, f32[1536,128]{1,0:T(8,128)}, u32[]{:S(2)}, u32[]{:S(2)}) %collective-permute-start.2) | collective-permute-done | bytes 786464 | tf_op jit(solution)/shard_map/ppermute | solution.py:325
  43.7 8.1 %key_sums.1 = (f32[3072,128]{1,0:T(8,128)}, f32[3072,128]{1,0:T(8,128)}, f32[1600,128]{1,0:T(8,128)}, f32[768,128]{1,0:T(8,128)}, f32[768,128]{1,0:T(8,128)}) custom-call(s32[3]{0:T(128)} %copy-done.7, f32[128,3072]{1,0:T(8,128)} %refs_0_.3, f32[1536,128]{1,0:T(8,128)} %collective-permute-done.refs_1_.refs_5_, ...), custom_call_target="tpu_custom_call" | custom-call | flops 1006632960 | bytes 7241728 | tf_op jit(solution)/shard_map/key_sums/pallas_call | solution.py:306
  52.9 1.8 collective-permute-start.8
  54.7 1.5 collective-permute-done.8
  56.2 1.2 dynamic-slice_add_fusion.1
  58.1 2.3 collective-permute-start.10
  61.7 5.5 %collective-permute-done.10 = f32[200,128]{1,0:T(8,128)S(1)} collective-permute-done((f32[200,128]{1,0:T(8,128)}, f32[200,128]{1,0:T(8,128)S(1)}, u32[]{:S(2)}, u32[]{:S(2)}) %collective-permute-start.10) | collective-permute-done | bytes 102432 | tf_op jit(solution)/shard_map/ppermute | solution.py:325
  68.7 3.8 %collective-permute-start.12 = (f32[200,128]{1,0:T(8,128)S(1)}, f32[200,128]{1,0:T(8,128)S(1)}, u32[]{:S(2)}, u32[]{:S(2)}) collective-permute-start(f32[200,128]{1,0:T(8,128)S(1)} %get-tuple-element.80), channel_id=1, source_target_pairs={{0,8},{4,12},{8,0},{12,4},{16,24},{20,28},{24,16},{28,20},{1,9},{5... | collective-permute-start | bytes 307208 | tf_op jit(solution)/shard_map/ppermute | solution.py:325
  72.5 1.9 collective-permute-start.13
  74.4 1.2 collective-permute-start.14
  77.5 5.0 %collective-permute-done.14 = f32[200,128]{1,0:T(8,128)S(1)} collective-permute-done((f32[200,128]{1,0:T(8,128)S(1)}, f32[200,128]{1,0:T(8,128)S(1)}, u32[]{:S(2)}, u32[]{:S(2)}) %collective-permute-start.14) | collective-permute-done | bytes 102432 | tf_op jit(solution)/shard_map/ppermute | solution.py:325
  83.2 1.4 collective-permute-start.15
  86.0 1.2 collective-permute-start.5
  88.0 1.2 broadcast_select_fusion.3
  90.1 13.8 %collective-permute-done.3.refs_1_.refs_5_.refs_9_ = f32[1544,128]{1,0:T(8,128)S(1)} collective-permute-done((f32[1544,128]{1,0:T(8,128)S(1)}, f32[1544,128]{1,0:T(8,128)S(1)}, u32[]{:S(2)}, u32[]{:S(2)}) %collective-permute-start.3) | collective-permute-done | bytes 790560 | tf_op jit(solution)/shard_map/ppermute | solution.py:325
  104.5 17.3 %collective-permute-done.5.refs_3_.refs_7_.refs_11_ = f32[1544,128]{1,0:T(8,128)} collective-permute-done((f32[1544,128]{1,0:T(8,128)S(1)}, f32[1544,128]{1,0:T(8,128)}, u32[]{:S(2)}, u32[]{:S(2)}) %collective-permute-start.5) | collective-permute-done | bytes 790560 | tf_op jit(solution)/shard_map/ppermute | solution.py:325
  121.8 12.1 %query_low_rank.1 = (f32[768,512]{1,0:T(8,128)}, f32[768,512]{1,0:T(8,128)}, f32[1600,128]{1,0:T(8,128)}) custom-call(s32[3]{0:T(128)} %copy-done.7, f32[128,3072]{1,0:T(8,128)} %refs_0_.5, f32[1544,128]{1,0:T(8,128)} %copy-done.15, f32[1544,128]{1,0:T(8,128)} %collective-permute-done.4.refs_2_.refs_6_.refs_10_, ...), custom_call_target="tpu_custom_call" | custom-call | flops 2617245696 | bytes 5836800 | tf_op jit(solution)/shard_map/query_low_rank/pallas_call | solution.py:306
  135.9 1.4 collective-permute-done.19
  138.3 1.8 collective-permute-start.20
  140.1 1.8 collective-permute-start.21
  143.1 1.5 collective-permute-done.21
  144.6 5.5 %collective-permute-done.22 = f32[200,128]{1,0:T(8,128)S(1)} collective-permute-done((f32[200,128]{1,0:T(8,128)S(1)}, f32[200,128]{1,0:T(8,128)S(1)}, u32[]{:S(2)}, u32[]{:S(2)}) %collective-permute-start.22) | collective-permute-done | bytes 102432 | tf_op jit(solution)/shard_map/ppermute | solution.py:325
  150.1 2.4 collective-permute-start.23
  152.5 2.7 collective-permute-start.6
  155.2 1.9 collective-permute-start.7
  157.1 3.3 %collective-permute-start.24 = (f32[200,128]{1,0:T(8,128)S(1)}, f32[200,128]{1,0:T(8,128)S(1)}, u32[]{:S(2)}, u32[]{:S(2)}) collective-permute-start(f32[200,128]{1,0:T(8,128)S(1)} %get-tuple-element.78), channel_id=1, source_target_pairs={{0,16},{4,20},{8,24},{12,28},{16,0},{20,4},{24,8},{28,12},{1,17},{... | collective-permute-start | bytes 307208 | tf_op jit(solution)/shard_map/ppermute | solution.py:325
  161.1 3.4 %collective-permute-done.24 = f32[200,128]{1,0:T(8,128)S(1)} collective-permute-done((f32[200,128]{1,0:T(8,128)S(1)}, f32[200,128]{1,0:T(8,128)S(1)}, u32[]{:S(2)}, u32[]{:S(2)}) %collective-permute-start.24) | collective-permute-done | bytes 102432 | tf_op jit(solution)/shard_map/ppermute | solution.py:325
  164.5 2.4 collective-permute-done.25
  166.9 7.2 %collective-permute-start.26 = (f32[800,128]{1,0:T(8,128)S(1)}, f32[800,128]{1,0:T(8,128)}, u32[]{:S(2)}, u32[]{:S(2)}) collective-permute-start(f32[800,128]{1,0:T(8,128)S(1)} %constant_dynamic-update-slice_fusion.4), channel_id=1, source_target_pairs={{0,4},{4,0},{8,12},{12,8},{16,20},{20,16},{24,28},{28,24},{1,5},{5... | collective-permute-start | bytes 1228808 | tf_op jit(solution)/shard_map/ppermute | solution.py:325
  175.0 26.2 %sparse.1 = (f32[1544,128]{1,0:T(8,128)}, f32[1544,128]{1,0:T(8,128)}, f32[1544,128]{1,0:T(8,128)}, f32[1544,128]{1,0:T(8,128)}, f32[3072,128]{1,0:T(8,128)}, /*...) custom-call(s32[3]{0:T(128)} %copy-done.7, f32[128,3072]{1,0:T(8,128)} %refs_0_.5, ...), custom_call_target="tpu_custom_call" | custom-call | flops 9059696640 | bytes 11026432 | tf_op jit(solution)/shard_map/sparse/pallas_call | solution.py:306
  201.8 1.2 collective-permute-start.17
  204.0 4.0 %collective-permute-start.27 = (f32[768,128]{1,0:T(8,128)}, f32[768,128]{1,0:T(8,128)S(1)}, u32[]{:S(2)}, u32[]{:S(2)}) collective-permute-start(f32[768,128]{1,0:T(8,128)} %get-tuple-element.69), channel_id=1, source_target_pairs={{0,4},{4,8},{8,12},{12,16},{16,20},{20,24},{24,28},{1,5},{5,9},{9,... | collective-permute-start | bytes 1179656 | tf_op jit(solution)/shard_map/ppermute | solution.py:357
  208.0 2.1 collective-permute-start.28
  213.0 4.6 %collective-permute-done.28.refs_6_ = f32[768,128]{1,0:T(8,128)S(1)} collective-permute-done((f32[768,128]{1,0:T(8,128)}, f32[768,128]{1,0:T(8,128)S(1)}, u32[]{:S(2)}, u32[]{:S(2)}) %collective-permute-start.28) | collective-permute-done | bytes 393248 | tf_op jit(solution)/shard_map/ppermute | solution.py:362
  218.3 10.6 %key_low_rank.1 = (f32[1536,128]{1,0:T(8,128)}, f32[1536,128]{1,0:T(8,128)}, f32[1536,128]{1,0:T(8,128)}, f32[1536,128]{1,0:T(8,128)}) custom-call(s32[3]{0:T(128)} %copy-done.7, f32[3072,128]{1,0:T(8,128)} %get-tuple-element.53.refs_12_.refs_0_, f32[3072,128]{1,0:T(8,128)} %get-tuple-element.54.refs_13_.refs_1_, f32[1600,128]{1,0:T(8,128)} %pad_maximum_fusion.1.refs_2_, ...), custom_call_target="tpu_custom_call" | custom-call | flops 2013265920 | bytes 4194304 | tf_op jit(solution)/shard_map/key_low_rank/pallas_call | solution.py:306
  229.5 1.2 collective-permute-start.30
  231.7 6.3 %collective-permute-done.18.refs_4_ = f32[1544,128]{1,0:T(8,128)S(1)} collective-permute-done((f32[1544,128]{1,0:T(8,128)}, f32[1544,128]{1,0:T(8,128)S(1)}, u32[]{:S(2)}, u32[]{:S(2)}) %collective-permute-start.18) | collective-permute-done | bytes 790560 | tf_op jit(solution)/shard_map/ppermute | solution.py:325
  238.6 3.1 %unpack_od.1 = (f32[128,3072]{1,0:T(8,128)}, f32[128,3072]{1,0:T(8,128)}) custom-call(s32[3]{0:T(128)S(1)} %copy-done.8, f32[1544,128]{1,0:T(8,128)S(1)} %copy-done.4, f32[1544,128]{1,0:T(8,128)S(1)} %collective-permute-done.16.refs_2_, f32[1544,128]{1,0:T(8,128)S(1)} %collective-permute-done.17.refs_3_, f32[1544,128]{1,0:T(8,128)S(1)} %collective-permute-done.18.refs_4_), custom_call_target="tpu_custom_call" | custom-call | bytes 6291456 | tf_op jit(solution)/shard_map/unpack_od/pallas_call | solution.py:87
  241.7 13.0 %collective-permute-done.29.refs_2_ = f32[1536,128]{1,0:T(8,128)} collective-permute-done((f32[1536,128]{1,0:T(8,128)}, f32[1536,128]{1,0:T(8,128)}, u32[]{:S(2)}, u32[]{:S(2)}) %collective-permute-start.29) | collective-permute-done | bytes 786464 | tf_op jit(solution)/shard_map/ppermute | solution.py:325
  254.7 17.7 %collective-permute-done.30.refs_3_ = f32[1536,128]{1,0:T(8,128)} collective-permute-done((f32[1536,128]{1,0:T(8,128)}, f32[1536,128]{1,0:T(8,128)}, u32[]{:S(2)}, u32[]{:S(2)}) %collective-permute-start.30) | collective-permute-done | bytes 786464 | tf_op jit(solution)/shard_map/ppermute | solution.py:325
  272.4 4.4 %unpack_kv.1 = (f32[128,3072]{1,0:T(8,128)}, f32[128,3072]{1,0:T(8,128)}) custom-call(s32[3]{0:T(128)S(1)} %copy-done.8, f32[1536,128]{1,0:T(8,128)S(1)} %copy-done.5, f32[1536,128]{1,0:T(8,128)} %collective-permute-done.29.refs_2_, f32[1536,128]{1,0:T(8,128)} %collective-permute-done.30.refs_3_, f32[1536,128]{1,0:T(8,128)} %collective-permute-done.31.refs_4_), custom_call_target="tpu_custom_call" | custom-call | bytes 6291456 | tf_op jit(solution)/shard_map/unpack_kv/pallas_call | solution.py:87
  (109 shorter events, 30.2 us)
Async XLA Ops:
  0.7 1.4 copy-start
  2.1 1.4 copy-start.1
  3.5 8.7 %copy-start.7 = (s32[3]{0:T(128)}, s32[3]{0:T(128)S(1)}, u32[]{:S(2)}) copy-start(s32[3]{0:T(128)S(1)} %pad_add_fusion.refs_0_.index) | copy-start | bytes 40
  3.5 7.5 %copy-start.18 = (f32[128,24]{0,1:T(8,128)S(1)}, f32[128,24]{0,1:T(8,128)}, u32[]{:S(2)}) copy-start(f32[128,24]{0,1:T(8,128)} %param.11) | copy-start | bytes 36868
  3.5 8.7 %copy-start.2 = (f32[128,3072]{1,0:T(8,128)S(1)}, f32[128,3072]{1,0:T(8,128)}, u32[]{:S(2)}) copy-start(f32[128,3072]{1,0:T(8,128)} %refs_0_.5) | copy-start | bytes 4718596
  3.5 8.7 %copy-start.3 = (f32[128,3072]{1,0:T(8,128)S(1)}, f32[128,3072]{1,0:T(8,128)}, u32[]{:S(2)}) copy-start(f32[128,3072]{1,0:T(8,128)} %refs_4_.5) | copy-start | bytes 4718596
  6.3 19.7 %collective-permute-start = (f32[1536,128]{1,0:T(8,128)}, f32[1536,128]{1,0:T(8,128)}, u32[]{:S(2)}, u32[]{:S(2)}) collective-permute-start(f32[1536,128]{1,0:T(8,128)} %get-tuple-element.41), channel_id=1, source_target_pairs={{0,1},{1,0},{2,3},{3,2},{4,5},{5,4},{6,7},{7,6},{8,9},{9,8},{10,11... | collective-permute-start | bytes 2359304 | tf_op jit(solution)/shard_map/ppermute | solution.py:325
  8.4 18.4 %collective-permute-start.1 = (f32[1536,128]{1,0:T(8,128)}, f32[1536,128]{1,0:T(8,128)}, u32[]{:S(2)}, u32[]{:S(2)}) collective-permute-start(f32[1536,128]{1,0:T(8,128)} %get-tuple-element.42), channel_id=1, source_target_pairs={{0,2},{1,3},{2,0},{3,1},{4,6},{5,7},{6,4},{7,5},{8,10},{9,11},{10,... | collective-permute-start | bytes 2359304 | tf_op jit(solution)/shard_map/ppermute | solution.py:325
  9.6 34.1 %collective-permute-start.2 = (f32[1536,128]{1,0:T(8,128)}, f32[1536,128]{1,0:T(8,128)}, u32[]{:S(2)}, u32[]{:S(2)}) collective-permute-start(f32[1536,128]{1,0:T(8,128)} %get-tuple-element.43), channel_id=1, source_target_pairs={{0,3},{1,2},{2,1},{3,0},{4,7},{5,6},{6,5},{7,4},{8,11},{9,10},{10,... | collective-permute-start | bytes 2359304 | tf_op jit(solution)/shard_map/ppermute | solution.py:325
  52.9 3.3 %collective-permute-start.8 = (f32[800,128]{1,0:T(8,128)S(1)}, f32[800,128]{1,0:T(8,128)}, u32[]{:S(2)}, u32[]{:S(2)}) collective-permute-start(f32[800,128]{1,0:T(8,128)S(1)} %constant_dynamic-slice_fusion.7), channel_id=1, source_target_pairs={{0,4},{4,0},{8,12},{12,8},{16,20},{20,16},{24,28},{28,24},{1,5},{5... | collective-permute-start | bytes 1228808 | tf_op jit(solution)/shard_map/ppermute | solution.py:325
  54.7 29.8 %copy-start.14 = (f32[1544,128]{1,0:T(8,128)S(1)}, f32[1544,128]{1,0:T(8,128)}, u32[]{:S(2)}) copy-start(f32[1544,128]{1,0:T(8,128)} %copy-done.13) | copy-start | bytes 2371588
  54.7 30.8 %copy-start.12 = (f32[1544,128]{1,0:T(8,128)S(1)}, f32[1544,128]{1,0:T(8,128)}, u32[]{:S(2)}) copy-start(f32[1544,128]{1,0:T(8,128)} %copy-done.11) | copy-start | bytes 2371588
  54.7 31.3 %copy-start.10 = (f32[1544,128]{1,0:T(8,128)S(1)}, f32[1544,128]{1,0:T(8,128)}, u32[]{:S(2)}) copy-start(f32[1544,128]{1,0:T(8,128)} %copy-done.9) | copy-start | bytes 2371588
  58.1 9.1 %collective-permute-start.10 = (f32[200,128]{1,0:T(8,128)}, f32[200,128]{1,0:T(8,128)S(1)}, u32[]{:S(2)}, u32[]{:S(2)}) collective-permute-start(f32[200,128]{1,0:T(8,128)} %get-tuple-element.90), channel_id=1, source_target_pairs={{0,16},{4,20},{8,24},{12,28},{16,0},{20,4},{24,8},{28,12},{1,17},{... | collective-permute-start | bytes 307208 | tf_op jit(solution)/shard_map/ppermute | solution.py:325
  60.4 6.8 %collective-permute-start.11 = (f32[200,128]{1,0:T(8,128)S(1)}, f32[200,128]{1,0:T(8,128)S(1)}, u32[]{:S(2)}, u32[]{:S(2)}) collective-permute-start(f32[200,128]{1,0:T(8,128)S(1)} %get-tuple-element.89), channel_id=1, source_target_pairs={{0,24},{4,28},{8,16},{12,20},{16,8},{20,12},{24,0},{28,4},{1,25},{... | collective-permute-start | bytes 307208 | tf_op jit(solution)/shard_map/ppermute | solution.py:325
  61.4 5.8 %collective-permute-start.9 = (f32[200,128]{1,0:T(8,128)S(1)}, f32[200,128]{1,0:T(8,128)S(1)}, u32[]{:S(2)}, u32[]{:S(2)}) collective-permute-start(f32[200,128]{1,0:T(8,128)S(1)} %get-tuple-element.88), channel_id=1, source_target_pairs={{0,8},{4,12},{8,0},{12,4},{16,24},{20,28},{24,16},{28,20},{1,9},{5... | collective-permute-start | bytes 307208 | tf_op jit(solution)/shard_map/ppermute | solution.py:325
  68.7 6.9 %collective-permute-start.12 = (f32[200,128]{1,0:T(8,128)S(1)}, f32[200,128]{1,0:T(8,128)S(1)}, u32[]{:S(2)}, u32[]{:S(2)}) collective-permute-start(f32[200,128]{1,0:T(8,128)S(1)} %get-tuple-element.80), channel_id=1, source_target_pairs={{0,8},{4,12},{8,0},{12,4},{16,24},{20,28},{24,16},{28,20},{1,9},{5... | collective-permute-start | bytes 307208 | tf_op jit(solution)/shard_map/ppermute | solution.py:325
  72.5 4.4 %collective-permute-start.13 = (f32[200,128]{1,0:T(8,128)S(1)}, f32[200,128]{1,0:T(8,128)S(1)}, u32[]{:S(2)}, u32[]{:S(2)}) collective-permute-start(f32[200,128]{1,0:T(8,128)S(1)} %get-tuple-element.80), channel_id=1, source_target_pairs={{0,16},{4,20},{8,24},{12,28},{16,0},{20,4},{24,8},{28,12},{1,17},{... | collective-permute-start | bytes 307208 | tf_op jit(solution)/shard_map/ppermute | solution.py:325
  74.4 8.1 %collective-permute-start.14 = (f32[200,128]{1,0:T(8,128)S(1)}, f32[200,128]{1,0:T(8,128)S(1)}, u32[]{:S(2)}, u32[]{:S(2)}) collective-permute-start(f32[200,128]{1,0:T(8,128)S(1)} %get-tuple-element.80), channel_id=1, source_target_pairs={{0,24},{4,28},{8,16},{12,20},{16,8},{20,12},{24,0},{28,4},{1,25},{... | collective-permute-start | bytes 307208 | tf_op jit(solution)/shard_map/ppermute | solution.py:325
  83.2 4.8 %collective-permute-start.15 = (f32[800,128]{1,0:T(8,128)}, f32[800,128]{1,0:T(8,128)}, u32[]{:S(2)}, u32[]{:S(2)}) collective-permute-start(f32[800,128]{1,0:T(8,128)} %constant_dynamic-update-slice_fusion.8), channel_id=1, source_target_pairs={{0,4},{4,0},{8,12},{12,8},{16,20},{20,16},{24,28},{28,24},{1,5},{5... | collective-permute-start | bytes 1228808 | tf_op jit(solution)/shard_map/ppermute | solution.py:325
  84.5 19.4 %collective-permute-start.3 = (f32[1544,128]{1,0:T(8,128)S(1)}, f32[1544,128]{1,0:T(8,128)S(1)}, u32[]{:S(2)}, u32[]{:S(2)}) collective-permute-start(f32[1544,128]{1,0:T(8,128)S(1)} %copy-done.14), channel_id=1, source_target_pairs={{0,1},{1,0},{2,3},{3,2},{4,5},{5,4},{6,7},{7,6},{8,9},{9,8},{10,11... | collective-permute-start | bytes 2371592 | tf_op jit(solution)/shard_map/ppermute | solution.py:325
  85.5 19.0 %collective-permute-start.4 = (f32[1544,128]{1,0:T(8,128)S(1)}, f32[1544,128]{1,0:T(8,128)}, u32[]{:S(2)}, u32[]{:S(2)}) collective-permute-start(f32[1544,128]{1,0:T(8,128)S(1)} %copy-done.12), channel_id=1, source_target_pairs={{0,2},{1,3},{2,0},{3,1},{4,6},{5,7},{6,4},{7,5},{8,10},{9,11},{10,... | collective-permute-start | bytes 2371592 | tf_op jit(solution)/shard_map/ppermute | solution.py:325
  86.0 35.8 %collective-permute-start.5 = (f32[1544,128]{1,0:T(8,128)S(1)}, f32[1544,128]{1,0:T(8,128)}, u32[]{:S(2)}, u32[]{:S(2)}) collective-permute-start(f32[1544,128]{1,0:T(8,128)S(1)} %copy-done.10), channel_id=1, source_target_pairs={{0,3},{1,2},{2,1},{3,0},{4,7},{5,6},{6,5},{7,4},{8,11},{9,10},{10,... | collective-permute-start | bytes 2371592 | tf_op jit(solution)/shard_map/ppermute | solution.py:325
  103.9 17.9 %copy-start.15 = (f32[1544,128]{1,0:T(8,128)}, f32[1544,128]{1,0:T(8,128)S(1)}, u32[]{:S(2)}) copy-start(f32[1544,128]{1,0:T(8,128)S(1)} %collective-permute-done.3.refs_1_.refs_5_.refs_9_) | copy-start | bytes 2371588
  135.0 17.5 %copy-start.20 = (f32[768,128]{1,0:T(8,128)S(1)}, f32[768,128]{1,0:T(8,128)}, u32[]{:S(2)}) copy-start(f32[768,128]{1,0:T(8,128)} %get-tuple-element.55) | copy-start | bytes 1179652
  135.0 20.2 %copy-start.19 = (f32[768,128]{1,0:T(8,128)S(1)}, f32[768,128]{1,0:T(8,128)}, u32[]{:S(2)}) copy-start(f32[768,128]{1,0:T(8,128)} %get-tuple-element.56) | copy-start | bytes 1179652
  135.0 2.2 collective-permute-start.19
  138.3 4.8 %collective-permute-start.20 = (f32[200,128]{1,0:T(8,128)S(1)}, f32[200,128]{1,0:T(8,128)S(1)}, u32[]{:S(2)}, u32[]{:S(2)}) collective-permute-start(f32[200,128]{1,0:T(8,128)S(1)} %get-tuple-element.85), channel_id=1, source_target_pairs={{0,8},{4,12},{8,0},{12,4},{16,24},{20,28},{24,16},{28,20},{1,9},{5... | collective-permute-start | bytes 307208 | tf_op jit(solution)/shard_map/ppermute | solution.py:325
  140.1 4.5 %collective-permute-start.21 = (f32[200,128]{1,0:T(8,128)S(1)}, f32[200,128]{1,0:T(8,128)S(1)}, u32[]{:S(2)}, u32[]{:S(2)}) collective-permute-start(f32[200,128]{1,0:T(8,128)S(1)} %get-tuple-element.87), channel_id=1, source_target_pairs={{0,16},{4,20},{8,24},{12,28},{16,0},{20,4},{24,8},{28,12},{1,17},{... | collective-permute-start | bytes 307208 | tf_op jit(solution)/shard_map/ppermute | solution.py:325
  141.9 8.2 %collective-permute-start.22 = (f32[200,128]{1,0:T(8,128)S(1)}, f32[200,128]{1,0:T(8,128)S(1)}, u32[]{:S(2)}, u32[]{:S(2)}) collective-permute-start(f32[200,128]{1,0:T(8,128)S(1)} %get-tuple-element.86), channel_id=1, source_target_pairs={{0,24},{4,28},{8,16},{12,20},{16,8},{20,12},{24,0},{28,4},{1,25},{... | collective-permute-start | bytes 307208 | tf_op jit(solution)/shard_map/ppermute | solution.py:325
  150.1 11.0 %collective-permute-start.23 = (f32[200,128]{1,0:T(8,128)S(1)}, f32[200,128]{1,0:T(8,128)S(1)}, u32[]{:S(2)}, u32[]{:S(2)}) collective-permute-start(f32[200,128]{1,0:T(8,128)S(1)} %get-tuple-element.78), channel_id=1, source_target_pairs={{0,8},{4,12},{8,0},{12,4},{16,24},{20,28},{24,16},{28,20},{1,9},{5... | collective-permute-start | bytes 307208 | tf_op jit(solution)/shard_map/ppermute | solution.py:325
  152.5 21.6 %collective-permute-start.6 = (f32[768,128]{1,0:T(8,128)S(1)}, f32[768,128]{1,0:T(8,128)S(1)}, u32[]{:S(2)}, u32[]{:S(2)}) collective-permute-start(f32[768,128]{1,0:T(8,128)S(1)} %copy-done.20), channel_id=1, source_target_pairs={{0,4},{4,8},{8,12},{12,16},{16,20},{20,24},{24,28},{1,5},{5,9},{9,... | collective-permute-start | bytes 1179656 | tf_op jit(solution)/shard_map/ppermute | solution.py:357
  155.2 18.9 %collective-permute-start.7 = (f32[768,128]{1,0:T(8,128)S(1)}, f32[768,128]{1,0:T(8,128)S(1)}, u32[]{:S(2)}, u32[]{:S(2)}) collective-permute-start(f32[768,128]{1,0:T(8,128)S(1)} %copy-done.19), channel_id=1, source_target_pairs={{4,0},{8,4},{12,8},{16,12},{20,16},{24,20},{28,24},{5,1},{9,5},{13... | collective-permute-start | bytes 1179656 | tf_op jit(solution)/shard_map/ppermute | solution.py:362
  157.1 7.3 %collective-permute-start.24 = (f32[200,128]{1,0:T(8,128)S(1)}, f32[200,128]{1,0:T(8,128)S(1)}, u32[]{:S(2)}, u32[]{:S(2)}) collective-permute-start(f32[200,128]{1,0:T(8,128)S(1)} %get-tuple-element.78), channel_id=1, source_target_pairs={{0,16},{4,20},{8,24},{12,28},{16,0},{20,4},{24,8},{28,12},{1,17},{... | collective-permute-start | bytes 307208 | tf_op jit(solution)/shard_map/ppermute | solution.py:325
  160.4 6.5 %collective-permute-start.25 = (f32[200,128]{1,0:T(8,128)S(1)}, f32[200,128]{1,0:T(8,128)S(1)}, u32[]{:S(2)}, u32[]{:S(2)}) collective-permute-start(f32[200,128]{1,0:T(8,128)S(1)} %get-tuple-element.78), channel_id=1, source_target_pairs={{0,24},{4,28},{8,16},{12,20},{16,8},{20,12},{24,0},{28,4},{1,25},{... | collective-permute-start | bytes 307208 | tf_op jit(solution)/shard_map/ppermute | solution.py:325
  166.9 41.0 %collective-permute-start.26 = (f32[800,128]{1,0:T(8,128)S(1)}, f32[800,128]{1,0:T(8,128)}, u32[]{:S(2)}, u32[]{:S(2)}) collective-permute-start(f32[800,128]{1,0:T(8,128)S(1)} %constant_dynamic-update-slice_fusion.4), channel_id=1, source_target_pairs={{0,4},{4,0},{8,12},{12,8},{16,20},{20,16},{24,28},{28,24},{1,5},{5... | collective-permute-start | bytes 1228808 | tf_op jit(solution)/shard_map/ppermute | solution.py:325
  201.2 29.5 %collective-permute-start.16 = (f32[1544,128]{1,0:T(8,128)}, f32[1544,128]{1,0:T(8,128)S(1)}, u32[]{:S(2)}, u32[]{:S(2)}) collective-permute-start(f32[1544,128]{1,0:T(8,128)} %get-tuple-element.61), channel_id=1, source_target_pairs={{0,1},{1,0},{2,3},{3,2},{4,5},{5,4},{6,7},{7,6},{8,9},{9,8},{10,11... | collective-permute-start | bytes 2371592 | tf_op jit(solution)/shard_map/ppermute | solution.py:325
  201.8 29.9 %collective-permute-start.17 = (f32[1544,128]{1,0:T(8,128)}, f32[1544,128]{1,0:T(8,128)S(1)}, u32[]{:S(2)}, u32[]{:S(2)}) collective-permute-start(f32[1544,128]{1,0:T(8,128)} %get-tuple-element.62), channel_id=1, source_target_pairs={{0,2},{1,3},{2,0},{3,1},{4,6},{5,7},{6,4},{7,5},{8,10},{9,11},{10,... | collective-permute-start | bytes 2371592 | tf_op jit(solution)/shard_map/ppermute | solution.py:325
  203.1 35.0 %collective-permute-start.18 = (f32[1544,128]{1,0:T(8,128)}, f32[1544,128]{1,0:T(8,128)S(1)}, u32[]{:S(2)}, u32[]{:S(2)}) collective-permute-start(f32[1544,128]{1,0:T(8,128)} %get-tuple-element.63), channel_id=1, source_target_pairs={{0,3},{1,2},{2,1},{3,0},{4,7},{5,6},{6,5},{7,4},{8,11},{9,10},{10,... | collective-permute-start | bytes 2371592 | tf_op jit(solution)/shard_map/ppermute | solution.py:325
  204.0 9.0 %collective-permute-start.27 = (f32[768,128]{1,0:T(8,128)}, f32[768,128]{1,0:T(8,128)S(1)}, u32[]{:S(2)}, u32[]{:S(2)}) collective-permute-start(f32[768,128]{1,0:T(8,128)} %get-tuple-element.69), channel_id=1, source_target_pairs={{0,4},{4,8},{8,12},{12,16},{16,20},{20,24},{24,28},{1,5},{5,9},{9,... | collective-permute-start | bytes 1179656 | tf_op jit(solution)/shard_map/ppermute | solution.py:357
  208.0 9.6 %collective-permute-start.28 = (f32[768,128]{1,0:T(8,128)}, f32[768,128]{1,0:T(8,128)S(1)}, u32[]{:S(2)}, u32[]{:S(2)}) collective-permute-start(f32[768,128]{1,0:T(8,128)} %get-tuple-element.70), channel_id=1, source_target_pairs={{4,0},{8,4},{12,8},{16,12},{20,16},{24,20},{28,24},{5,1},{9,5},{13... | collective-permute-start | bytes 1179656 | tf_op jit(solution)/shard_map/ppermute | solution.py:362
  213.0 4.6 %copy-start.16 = (f32[768,128]{1,0:T(8,128)}, f32[768,128]{1,0:T(8,128)S(1)}, u32[]{:S(2)}) copy-start(f32[768,128]{1,0:T(8,128)S(1)} %collective-permute-done.27.refs_5_) | copy-start | bytes 1179652
  218.3 13.3 %copy-start.4 = (f32[1544,128]{1,0:T(8,128)S(1)}, f32[1544,128]{1,0:T(8,128)}, u32[]{:S(2)}) copy-start(f32[1544,128]{1,0:T(8,128)} %get-tuple-element.60.refs_1_) | copy-start | bytes 2371588
  218.3 20.3 %copy-start.8 = (s32[3]{0:T(128)S(1)}, s32[3]{0:T(128)}, u32[]{:S(2)}) copy-start(s32[3]{0:T(128)} %copy-done.7) | copy-start | bytes 40
  229.0 25.7 %collective-permute-start.29 = (f32[1536,128]{1,0:T(8,128)}, f32[1536,128]{1,0:T(8,128)}, u32[]{:S(2)}, u32[]{:S(2)}) collective-permute-start(f32[1536,128]{1,0:T(8,128)} %get-tuple-element.72), channel_id=1, source_target_pairs={{0,1},{1,0},{2,3},{3,2},{4,5},{5,4},{6,7},{7,6},{8,9},{9,8},{10,11... | collective-permute-start | bytes 2359304 | tf_op jit(solution)/shard_map/ppermute | solution.py:325
  229.5 42.8 %collective-permute-start.30 = (f32[1536,128]{1,0:T(8,128)}, f32[1536,128]{1,0:T(8,128)}, u32[]{:S(2)}, u32[]{:S(2)}) collective-permute-start(f32[1536,128]{1,0:T(8,128)} %get-tuple-element.73), channel_id=1, source_target_pairs={{0,2},{1,3},{2,0},{3,1},{4,6},{5,7},{6,4},{7,5},{8,10},{9,11},{10,... | collective-permute-start | bytes 2359304 | tf_op jit(solution)/shard_map/ppermute | solution.py:325
  230.8 41.6 %collective-permute-start.31 = (f32[1536,128]{1,0:T(8,128)}, f32[1536,128]{1,0:T(8,128)}, u32[]{:S(2)}, u32[]{:S(2)}) collective-permute-start(f32[1536,128]{1,0:T(8,128)} %get-tuple-element.74), channel_id=1, source_target_pairs={{0,3},{1,2},{2,1},{3,0},{4,7},{5,6},{6,5},{7,4},{8,11},{9,10},{10,... | collective-permute-start | bytes 2359304 | tf_op jit(solution)/shard_map/ppermute | solution.py:325
  238.6 33.7 %copy-start.5 = (f32[1536,128]{1,0:T(8,128)S(1)}, f32[1536,128]{1,0:T(8,128)}, u32[]{:S(2)}) copy-start(f32[1536,128]{1,0:T(8,128)} %get-tuple-element.71.refs_1_) | copy-start | bytes 2359300
  (7 other events, 6.5 us)

commit v2 on v1

--- a/solution.py
+++ b/solution.py
@@ -30,8 +30,24 @@
     return mm(a[0], b[0]) + (mm(a[0], b[1]) + mm(a[1], b[0]))
 
 
-def mm2(exact, b):
-    return mm(exact, b[0]) + mm(exact, b[1])
+def split3(x):
+    high = x.astype(BF16)
+    rest = x - high.astype(F32)
+    middle = rest.astype(BF16)
+    return high, middle, (rest - middle.astype(F32)).astype(BF16)
+
+
+def mm_exact(exact, b):
+    total = mm(exact, b[-1])
+    for part in b[-2::-1]:
+        total = mm(exact, part) + total
+    return total
+
+
+def mm6(a, b):
+    left = jnp.concatenate([a[0], a[1], a[2], a[0], a[1], a[0]], axis=1)
+    right = jnp.concatenate([b[0], b[0], b[0], b[1], b[1], b[2]], axis=0)
+    return mm(left, right)
 
 
 def normed_t(x_t):
@@ -40,11 +56,11 @@
 
 
 def features_t(seed_t, normed):
-    return jnp.exp(mm2(seed_t, split2(normed)) * (1.0 / SEED_DIV))
+    return jnp.exp(mm_exact(seed_t, split3(normed)) * (1.0 / SEED_DIV))
 
 
 def normed_grad_t(seed, feats_t, dfeats_t, normed, scale):
-    grad = mm2(seed, split2(dfeats_t * feats_t)) * (1.0 / SEED_DIV)
+    grad = mm_exact(seed, split2(dfeats_t * feats_t)) * (1.0 / SEED_DIV)
     return scale * (grad - normed * jnp.mean(grad * normed, axis=0, keepdims=True))
 
 
@@ -63,6 +79,32 @@
     for distance, ref in enumerate(refs):
         place = pl.multiple_of(jnp.bitwise_xor(member, distance) * rows, rows)
         scratch[pl.ds(place, rows), :] = ref[...]
+
+
+def assemble_sums(scratch, mine_ref, other_ref, index, chips):
+    half = mine_ref.shape[0]
+    part = half // chips
+    for position, ref in ((index[3], mine_ref), (1 - index[3], other_ref)):
+        for distance in range(chips):
+            place = position * half + jnp.bitwise_xor(index[4], distance) * part
+            scratch[pl.ds(pl.multiple_of(place, EXT), part), :] = ref[
+                distance * part : (distance + 1) * part
+            ]
+
+
+def split_sums(scratch, mine_out, other_out, index):
+    half = mine_out.shape[0]
+    mine_out[...] = scratch[pl.ds(pl.multiple_of(index[3] * half, EXT), half), :]
+    other_out[...] = scratch[pl.ds(pl.multiple_of((1 - index[3]) * half, EXT), half), :]
+
+
+def cut_kernel(index, mine_ref, got_ref, *refs):
+    parts, total = refs[:-1], refs[-1]
+    total[...] = mine_ref[...] + got_ref[...]
+    size = parts[0].shape[0]
+    for distance, part in enumerate(parts):
+        place = jnp.bitwise_xor(index[4], distance) * size
+        part[...] = total[pl.ds(pl.multiple_of(place, EXT), size), :]
 
 
 def gate_row(ext, head, members):
@@ -100,10 +142,13 @@
     )(index, *ins)
 
 
-def sums_kernel(members, rows, heads, index, *refs):
+def sums_kernel(dims, index, *refs):
+    members, rows, heads, _, _, _ = dims
     key_refs, value_refs = refs[:members], refs[members : 2 * members]
     seed_t_ref = refs[2 * members]
-    keys_out, values_out, sums_out, low_edge, high_edge = refs[2 * members + 1 :]
+    keys_out, values_out, mine_out, other_out, low_edge, high_edge, sums_out = refs[
+        2 * members + 1 :
+    ]
     head = pl.program_id(0)
     member = index[0]
     tokens = members * rows
@@ -129,18 +174,26 @@
         jnp.sum(feats, axis=1, keepdims=True)
     )
 
-
-def query_kernel(members, rows, heads, index, *refs):
+    @pl.when(head == heads - 1)
+    def _():
+        split_sums(sums_out, mine_out, other_out, index)
+
+
+def query_kernel(dims, index, *refs):
+    members, rows, heads, chips, _, _ = dims
     query_refs, grad_refs = refs[:members], refs[members : 2 * members]
     ext_refs = refs[2 * members : 3 * members]
-    sums_ref, seed_ref, seed_t_ref = refs[3 * members : 3 * members + 3]
-    low_out, query_out, sums_out, queries, grads, ext = refs[3 * members + 3 :]
+    mine_ref, other_ref, seed_ref, seed_t_ref = refs[3 * members : 3 * members + 4]
+    low_out, query_out, mine_out, other_out, queries, grads, ext, sums_ref, sums_out = refs[
+        3 * members + 4 :
+    ]
     head = pl.program_id(0)
     member = index[0]
 
     @pl.when(head == 0)
     def _():
         assemble(ext, ext_refs, member, EXT)
+        assemble_sums(sums_ref, mine_ref, other_ref, index, chips)
         sums_out[pl.ds(heads * 256, sums_out.shape[0] - heads * 256), :] = jnp.zeros(
             (sums_out.shape[0] - heads * 256, 128), F32
         )
@@ -166,6 +219,10 @@
     sums_out[pl.ds(pl.multiple_of(heads * 256 + head * EXT, EXT), EXT), :] = column_to_rows(
         jnp.sum(feats * dden, axis=1, keepdims=True)
     )
+
+    @pl.when(head == heads - 1)
+    def _():
+        split_sums(sums_out, mine_out, other_out, index)
 
 
 def fill_bias(bias, ext, members, rows, first, last):
@@ -193,7 +250,8 @@
         )
 
 
-def sparse_kernel(members, rows, heads, index, *refs):
+def sparse_kernel(dims, index, *refs):
+    members, rows, heads, _, start, _ = dims
     query_refs, grad_refs = refs[:members], refs[members : 2 * members]
     ext_refs = refs[2 * members : 3 * members]
     keys_ref, values_ref, left_ref, right_ref, low_ref, query_low_ref = refs[
@@ -203,12 +261,13 @@
     messages = outs[:members]
     keys_out, values_out, left_out, right_out = outs[members : members + 4]
     queries, grads, ext, bias, keys_all, values_all = outs[members + 4 :]
-    head = pl.program_id(0)
+    step = pl.program_id(0)
+    head = step + start
     member = index[0]
     tokens = members * rows
     reach = rows // 2
 
-    @pl.when(head == 0)
+    @pl.when(step == 0)
     def _():
         assemble(ext, ext_refs, member, EXT)
         fill_bias(bias, ext, members, rows, index[1], index[2])
@@ -226,12 +285,11 @@
 
     gate = gate_row(ext, head, members)
     root = 1.0 / math.sqrt(HEAD_DIM)
-    keys = split2(keys_all[...])
     values = split2(values_all[...])
     keys_t = split2(jnp.transpose(keys_all[...]))
     values_t = split2(jnp.transpose(values_all[...]))
     scaled = queries[...] * root
-    scores = mm3(keys, split2(jnp.transpose(scaled))) + bias[...]
+    scores = mm6(split3(keys_all[...]), split3(jnp.transpose(scaled))) + bias[...]
     weights = jnp.exp(scores - jnp.max(scores, axis=0, keepdims=True))
     inverse = 1.0 / jnp.sum(weights, axis=0, keepdims=True)
     weight_parts = split2(weights)
@@ -259,11 +317,11 @@
     for distance, message in enumerate(messages):
         other = jnp.bitwise_xor(member, distance)
         place = pl.ds(pl.multiple_of(other * rows, rows), rows)
-        start = pl.multiple_of(head * 2 * rows, rows)
-        message[pl.ds(start, rows), :] = queries[place, :]
-        message[pl.ds(start + rows, rows), :] = grads[place, :]
-
-    @pl.when(head == heads - 1)
+        at = pl.multiple_of(step * 2 * rows, rows)
+        message[pl.ds(at, rows), :] = queries[place, :]
+        message[pl.ds(at + rows, rows), :] = grads[place, :]
+
+    @pl.when(step == heads - 1)
     def _():
         for distance, message in enumerate(messages):
             other = jnp.bitwise_xor(member, distance)
@@ -272,14 +330,22 @@
             ]
 
 
-def keys_kernel(members, rows, heads, index, *refs):
-    (keys_ref, values_ref, sums_ref, keys_grad, values_grad, left_ref, right_ref, seed_ref, seed_t_ref) = refs[:9]
-    messages = refs[9 : 9 + members]
-    dkeys, dvalues = refs[9 + members :]
-    head = pl.program_id(0)
+def keys_kernel(dims, index, *refs):
+    members, rows, _, chips, start, heads = dims
+    keys_ref, values_ref, mine_ref, other_ref, keys_grad, values_grad = refs[:6]
+    left_ref, right_ref, seed_ref, seed_t_ref = refs[6:10]
+    messages = refs[10 : 10 + members]
+    dkeys, dvalues, sums_ref = refs[10 + members :]
+    step = pl.program_id(0)
+    head = step + start
     member = index[0]
     tokens = members * rows
     reach = rows // 2
+
+    @pl.when(step == 0)
+    def _():
+        assemble_sums(sums_ref, mine_ref, other_ref, index, chips)
+
     sums = sums_ref[pl.ds(pl.multiple_of(head * 256, 256), 256), :]
     totals = rows_to_column(sums_ref[pl.ds(pl.multiple_of(heads * 256 + head * EXT, EXT), EXT), :])
     normed, scale = normed_t(jnp.transpose(keys_ref[...]))
@@ -300,15 +366,15 @@
         message[rows:] = dvalues[place, :]
 
 
-def per_head_call(kernel, members, rows, heads, index, ins, outs, scratch, flops, exps, name):
-    in_specs = [spec for _, spec in ins]
-    size = sum(math.prod(x.shape) * 4 for x, _ in ins[-4:]) + sum(math.prod(s.shape) * 4 for s, _ in outs)
+def per_head_call(kernel, dims, index, ins, outs, scratch, flops, exps, name):
+    heads = dims[2]
+    size = sum(math.prod(s.shape) * 4 for s, _ in outs)
     return pl.pallas_call(
-        functools.partial(kernel, members, rows, heads),
+        functools.partial(kernel, dims),
         grid_spec=pltpu.PrefetchScalarGridSpec(
             num_scalar_prefetch=1,
             grid=(heads,),
-            in_specs=in_specs,
+            in_specs=[spec for _, spec in ins],
             out_specs=[spec for _, spec in outs],
             scratch_shapes=scratch,
         ),
@@ -316,7 +382,9 @@
         compiler_params=pltpu.CompilerParams(
             vmem_limit_bytes=56 * 1024 * 1024, dimension_semantics=("arbitrary",)
         ),
-        cost_estimate=pl.CostEstimate(flops=flops, bytes_accessed=size, transcendentals=exps),
+        cost_estimate=pl.CostEstimate(
+            flops=flops * heads, bytes_accessed=2 * size, transcendentals=exps * heads
+        ),
         name=name,
     )(index, *[x for x, _ in ins])
 
@@ -325,31 +393,40 @@
     return lax.ppermute(block, axis, [(i, i ^ distance) for i in range(lax.axis_size(axis))])
 
 
-def sum_over_seq(cells):
-    count = lax.axis_size("seq")
-    place = lax.axis_index("seq")
-    core, chip = place & 1, place >> 1
-    chips = count // 2
-    half = cells.shape[0] // 2
-    part = half // chips
-
-    def cut(x, at, size):
-        return lax.dynamic_slice_in_dim(x, at * size, size, 0)
-
-    summed = cut(cells, core, half) + swap(cut(cells, 1 - core, half), "seq", 1)
-    own = cut(summed, chip, part)
-    for d in range(1, chips):
-        own = own + swap(cut(summed, chip ^ d, part), "seq", 2 * d)
-    gathered = jnp.zeros((half, cells.shape[1]), F32)
-    gathered = lax.dynamic_update_slice_in_dim(gathered, own, chip * part, 0)
-    for d in range(1, chips):
-        gathered = lax.dynamic_update_slice_in_dim(
-            gathered, swap(own, "seq", 2 * d), (chip ^ d) * part, 0
-        )
-    other = swap(gathered, "seq", 1)
-    first = jnp.where(core == 0, gathered, other)
-    second = jnp.where(core == 0, other, gathered)
-    return jnp.concatenate([first, second], axis=0)
+def cut_sums(index, mine, got):
+    chips = lax.axis_size("seq") // 2
+    part = jax.ShapeDtypeStruct((mine.shape[0] // chips, 128), F32)
+    return pl.pallas_call(
+        cut_kernel,
+        grid_spec=pltpu.PrefetchScalarGridSpec(
+            num_scalar_prefetch=1,
+            grid=(1,),
+            in_specs=[pl.BlockSpec(mine.shape, lambda i, ref: (0, 0))] * 2,
+            out_specs=[pl.BlockSpec(part.shape, lambda i, ref: (0, 0))] * chips,
+            scratch_shapes=[pltpu.VMEM(mine.shape, F32)],
+        ),
+        out_shape=[part] * chips,
+        cost_estimate=pl.CostEstimate(
+            flops=mine.size, bytes_accessed=12 * mine.size, transcendentals=0
+        ),
+        name="cut_sums",
+    )(index, mine, got)
+
+
+def reduce_parts(parts):
+    own = parts[0]
+    for d, part in enumerate(parts[1:], 1):
+        own = own + swap(part, "seq", 2 * d)
+    return own
+
+
+def gather_parts(own):
+    chips = lax.axis_size("seq") // 2
+    return jnp.concatenate([own] + [swap(own, "seq", 2 * d) for d in range(1, chips)], axis=0)
+
+
+def after(value, *others):
+    return lax.optimization_barrier((value, *others))[0]
 
 
 def to_next(block):
@@ -377,24 +454,31 @@
     member = lax.axis_index("blk")
     groups = lax.axis_size("seq")
     group = lax.axis_index("seq")
+    chips = groups // 2
     heads = gate_logits.shape[1] // members
     tokens = members * rows
     others = range(1, members)
     index = jnp.stack(
-        [member, (group == 0).astype(jnp.int32), (group == groups - 1).astype(jnp.int32)]
+        [
+            member,
+            (group == 0).astype(jnp.int32),
+            (group == groups - 1).astype(jnp.int32),
+            group & 1,
+            group >> 1,
+        ]
     ).astype(jnp.int32)
     sum_rows = -(-(heads * (256 + EXT)) // (EXT * groups)) * EXT * groups
-
-    def shape(*dims):
-        return jax.ShapeDtypeStruct(dims, F32)
+    chunks = [(0, heads // 2), (heads // 2, heads - heads // 2)]
+    dims = (members, rows, heads, chips, 0, heads)
+
+    def shape(*sizes):
+        return jax.ShapeDtypeStruct(sizes, F32)
 
     def block_of(message_rows, at):
         return pl.BlockSpec((message_rows, 128), lambda h, ref: (at(h, ref), 0))
 
-    own_spec = pl.BlockSpec((rows, 128), lambda h, ref: (0, ref[0] * heads + h))
-    head_spec = pl.BlockSpec((tokens, 128), lambda h, ref: (h, 0))
-    edge_spec = pl.BlockSpec((rows, 128), lambda h, ref: (h, 0))
-    wide_spec = pl.BlockSpec((128, tokens), lambda h, ref: (h, 0))
+    def per_head(block, start=0):
+        return pl.BlockSpec(block, lambda h, ref: (h + start, 0))
 
     def whole(x):
         return pl.BlockSpec(x.shape, lambda h, ref: (0,) * len(x.shape))
@@ -407,7 +491,10 @@
                 for h in range(heads):
                     column = pl.multiple_of((other * heads + h) * 128, 128)
                     moves.append(
-                        (ins[a].at[:, pl.ds(column, 128)], out.at[pl.ds((a * heads + h) * rows, rows), :])
+                        (
+                            ins[a].at[:, pl.ds(column, 128)],
+                            out.at[pl.ds((a * heads + h) * rows, rows), :],
+                        )
                     )
             if extra:
                 start = pl.multiple_of(other * EXT, EXT)
@@ -418,14 +505,19 @@
 
     def unpacking(index, ins, outs):
         moves = []
-        for d, message in enumerate(ins):
-            other = jnp.bitwise_xor(index[0], d)
-            for a in range(2):
-                for h in range(heads):
-                    column = pl.multiple_of((other * heads + h) * 128, 128)
-                    moves.append(
-                        (message.at[pl.ds((2 * h + a) * rows, rows), :], outs[a].at[:, pl.ds(column, 128)])
-                    )
+        for chunk, (start, count) in enumerate(chunks):
+            for d in range(members):
+                other = jnp.bitwise_xor(index[0], d)
+                message = ins[chunk * members + d]
+                for a in range(2):
+                    for h in range(count):
+                        column = pl.multiple_of((other * heads + start + h) * 128, 128)
+                        moves.append(
+                            (
+                                message.at[pl.ds((2 * h + a) * rows, rows), :],
+                                outs[a].at[:, pl.ds(column, 128)],
+                            )
+                        )
         return moves
 
     kv_sent = local_copies(
@@ -465,146 +557,181 @@
     seed = feature_seed.astype(BF16)
     seed_t = jnp.transpose(feature_seed).astype(BF16)
     unit = 2 * tokens * 128 * 256
-    first_block = block_of(rows, lambda h, ref: h)
-    second_block = block_of(rows, lambda h, ref: heads + h)
-    keys_full, values_full, sums, low_edge, high_edge = per_head_call(
+    exps = tokens * 256
+    half = shape(sum_rows // 2, 128)
+    all_sums = pltpu.VMEM((sum_rows, 128), F32)
+    own_spec = pl.BlockSpec((rows, 128), lambda h, ref: (0, ref[0] * heads + h))
+    keys_full, values_full, sums, sums_other, low_edge, high_edge = per_head_call(
         sums_kernel,
-        members,
-        rows,
-        heads,
+        dims,
         index,
         [(key_matrix, own_spec)]
-        + [(x, first_block) for x in kv]
+        + [(x, per_head((rows, 128))) for x in kv]
         + [(value_matrix, own_spec)]
-        + [(x, second_block) for x in kv]
+        + [(x, per_head((rows, 128), heads)) for x in kv]
         + [(seed_t, whole(seed_t))],
         [
-            (shape(heads * tokens, 128), head_spec),
-            (shape(heads * tokens, 128), head_spec),
-            (shape(sum_rows, 128), whole(shape(sum_rows, 128))),
-            (shape(heads * rows, 128), edge_spec),
-            (shape(heads * rows, 128), edge_spec),
+            (shape(heads * tokens, 128), per_head((tokens, 128))),
+            (shape(heads * tokens, 128), per_head((tokens, 128))),
+            (half, whole(half)),
+            (half, whole(half)),
+            (shape(heads * rows, 128), per_head((rows, 128))),
+            (shape(heads * rows, 128), per_head((rows, 128))),
         ],
-        [],
-        5 * unit * heads,
-        heads * tokens * 256,
+        [all_sums],
+        6 * unit,
+        exps,
         "key_sums",
     )
     right_halo = to_previous(low_edge)
     left_halo = to_next(high_edge)
-    sums = sum_over_seq(sums)
+    sums = reduce_parts(cut_sums(index, sums, swap(sums_other, "seq", 1)))
+    sums, *qd[:2] = lax.optimization_barrier((sums, *qd[:2]))
+    sums = gather_parts(sums)
+    sums_other = swap(sums, "seq", 1)
 
     ext_block = block_of(EXT, lambda h, ref: 2 * heads * rows // EXT)
-    query_side = (
-        [(queries, own_spec)]
-        + [(x, first_block) for x in qd]
-        + [(output_grad, own_spec)]
-        + [(x, second_block) for x in qd]
-        + [(ext, block_of(EXT, lambda h, ref: ref[0]))]
-        + [(x, ext_block) for x in qd]
-    )
+
+    def query_side(start):
+        own = pl.BlockSpec((rows, 128), lambda h, ref: (0, ref[0] * heads + start + h))
+        return (
+            [(queries, own)]
+            + [(x, per_head((rows, 128), start)) for x in qd]
+            + [(output_grad, own)]
+            + [(x, per_head((rows, 128), heads + start)) for x in qd]
+            + [(ext, block_of(EXT, lambda h, ref: ref[0]))]
+            + [(x, ext_block) for x in qd]
+        )
+
     row_scratch = [
         pltpu.VMEM((tokens, 128), F32),
         pltpu.VMEM((tokens, 128), F32),
         pltpu.VMEM((members * EXT, 128), F32),
     ]
-    low, query_low, sums_grad = per_head_call(
+    low, query_low, sums_grad, grad_other = per_head_call(
         query_kernel,
-        members,
-        rows,
-        heads,
+        dims,
         index,
-        query_side + [(sums, whole(sums)), (seed, whole(seed)), (seed_t, whole(seed_t))],
-        [
-            (shape(heads * 128, tokens), wide_spec),
-            (shape(heads * 128, tokens), wide_spec),
-            (shape(sum_rows, 128), whole(shape(sum_rows, 128))),
-        ],
-        row_scratch,
-        13 * unit * heads,
-        heads * tokens * 256,
-        "query_low_rank",
-    )
-    sums_grad = sum_over_seq(sums_grad)
-
-    message = shape(2 * heads * rows + EXT, 128)
-    sparse_outs = per_head_call(
-        sparse_kernel,
-        members,
-        rows,
-        heads,
-        index,
-        query_side
+        query_side(0)
         + [
-            (keys_full, head_spec),
-            (values_full, head_spec),
-            (left_halo, edge_spec),
-            (right_halo, edge_spec),
-            (low, wide_spec),
-            (query_low, wide_spec),
-        ],
-        [(message, whole(message))] * members
-        + [
-            (shape(heads * tokens, 128), head_spec),
-            (shape(heads * tokens, 128), head_spec),
-            (shape(heads * rows, 128), edge_spec),
-            (shape(heads * rows, 128), edge_spec),
-        ],
-        row_scratch
-        + [
-            pltpu.VMEM((tokens + rows, tokens), F32),
-            pltpu.VMEM((tokens + rows, 128), F32),
-            pltpu.VMEM((tokens + rows, 128), F32),
-        ],
-        36 * tokens * (tokens + rows) * 128 * heads,
-        heads * tokens * (tokens + rows),
-        "sparse",
-    )
-    od_sent = sparse_outs[:members]
-    keys_sparse, values_sparse, left_grad, right_grad = sparse_outs[members:]
-    od = [od_sent[0]] + [swap(block, "blk", d) for d, block in zip(others, od_sent[1:])]
-    back_right = to_previous(left_grad)
-    back_left = to_next(right_grad)
-
-    dkv_sent = per_head_call(
-        keys_kernel,
-        members,
-        rows,
-        heads,
-        index,
-        [
-            (keys_full, head_spec),
-            (values_full, head_spec),
-            (sums_grad, whole(sums_grad)),
-            (keys_sparse, head_spec),
-            (values_sparse, head_spec),
-            (back_left, edge_spec),
-            (back_right, edge_spec),
+            (sums, whole(sums)),
+            (sums_other, whole(sums_other)),
             (seed, whole(seed)),
             (seed_t, whole(seed_t)),
         ],
-        [(shape(2 * heads * rows, 128), pl.BlockSpec((2 * rows, 128), lambda h, ref: (h, 0)))]
-        * members,
-        [pltpu.VMEM((tokens, 128), F32), pltpu.VMEM((tokens, 128), F32)],
-        10 * unit * heads,
-        heads * tokens * 256,
-        "key_low_rank",
-    )
-    dkv = [dkv_sent[0]] + [swap(block, "blk", d) for d, block in zip(others, dkv_sent[1:])]
-
+        [
+            (shape(heads * 128, tokens), per_head((128, tokens))),
+            (shape(heads * 128, tokens), per_head((128, tokens))),
+            (half, whole(half)),
+            (half, whole(half)),
+        ],
+        row_scratch + [all_sums, all_sums],
+        14 * unit,
+        exps,
+        "query_low_rank",
+    )
+
+    def sparse(chunk, low, query_low):
+        start, count = chunks[chunk]
+        message = shape(2 * count * rows + EXT, 128)
+        outs = per_head_call(
+            sparse_kernel,
+            (members, rows, count, chips, start, heads),
+            index,
+            query_side(start)
+            + [
+                (keys_full, per_head((tokens, 128), start)),
+                (values_full, per_head((tokens, 128), start)),
+                (left_halo, per_head((rows, 128), start)),
+                (right_halo, per_head((rows, 128), start)),
+                (low, per_head((128, tokens), start)),
+                (query_low, per_head((128, tokens), start)),
+            ],
+            [(message, whole(message))] * members
+            + [(shape(count * tokens, 128), per_head((tokens, 128)))] * 2
+            + [(shape(count * rows, 128), per_head((rows, 128)))] * 2,
+            row_scratch
+            + [
+                pltpu.VMEM((tokens + rows, tokens), F32),
+                pltpu.VMEM((tokens + rows, 128), F32),
+                pltpu.VMEM((tokens + rows, 128), F32),
+            ],
+            42 * tokens * (tokens + rows) * 128,
+            tokens * (tokens + rows),
+            "sparse",
+        )
+        return outs[:members], outs[members:]
+
+    def key_side(chunk, parts, sums, sums_other):
+        start, count = chunks[chunk]
+        keys_sparse, values_sparse, left_grad, right_grad = parts
+        back_right = to_previous(left_grad)
+        back_left = to_next(right_grad)
+        message = shape(2 * count * rows, 128)
+        return per_head_call(
+            keys_kernel,
+            (members, rows, count, chips, start, heads),
+            index,
+            [
+                (keys_full, per_head((tokens, 128), start)),
+                (values_full, per_head((tokens, 128), start)),
+                (sums, whole(sums)),
+                (sums_other, whole(sums_other)),
+                (keys_sparse, per_head((tokens, 128))),
+                (values_sparse, per_head((tokens, 128))),
+                (back_left, per_head((rows, 128))),
+                (back_right, per_head((rows, 128))),
+                (seed, whole(seed)),
+                (seed_t, whole(seed_t)),
+            ],
+            [(message, per_head((2 * rows, 128)))] * members,
+            [pltpu.VMEM((tokens, 128), F32), pltpu.VMEM((tokens, 128), F32), all_sums],
+            13 * unit,
+            exps,
+            "key_low_rank",
+        )
+
+    def back(messages):
+        return [messages[0]] + [swap(block, "blk", d) for d, block in zip(others, messages[1:])]
+
+    parts = cut_sums(index, sums_grad, swap(grad_other, "seq", 1))
+    low, query_low, *parts = lax.optimization_barrier((low, query_low, *parts))
+    od_first, keys_first = sparse(0, low, query_low)
+    own = reduce_parts(parts)
+    low, query_low, own, *od_first = lax.optimization_barrier((low, query_low, own, *od_first))
+    od_first = back(od_first)
+    od_second, keys_second = sparse(1, low, query_low)
+    sums = gather_parts(own)
+    sums, *od_second = lax.optimization_barrier((sums, *od_second))
+    sums_other = swap(sums, "seq", 1)
+    od_second = back(od_second)
+    dkv_first = back(key_side(0, keys_first, sums, sums_other))
+    dkv_second = back(key_side(1, keys_second, sums, sums_other))
+
+    od = od_first + od_second
+    n_moves = 2 * heads * members
     attended, query_grad = local_copies(
-        unpacking, 2 * heads * members, index, od, [shape(rows, width)] * 2, "unpack_od"
-    )
-    ext_back = jnp.zeros((members, EXT, 128), F32)
-    for d, block in enumerate(od):
-        ext_back = lax.dynamic_update_slice_in_dim(
-            ext_back, block[None, 2 * heads * rows :, :], member ^ d, 0
-        )
-    gate_grad = jnp.transpose(ext_back[:, :heads, :].reshape(members * heads, rows))
+        unpacking, n_moves, index, od, [shape(rows, width)] * 2, "unpack_od"
+    )
+    gate_parts = []
+    for chunk, (start, count) in enumerate(chunks):
+        rows_back = jnp.zeros((members, EXT, 128), F32)
+        for d in range(members):
+            block = od[chunk * members + d]
+            rows_back = lax.dynamic_update_slice_in_dim(
+                rows_back, block[None, 2 * count * rows :, :], member ^ d, 0
+            )
+        gate_parts.append(rows_back[:, start : start + count, :])
+    gate_grad = jnp.concatenate(gate_parts, axis=1).reshape(members * heads, rows)
     key_grad, value_grad = local_copies(
-        unpacking, 2 * heads * members, index, dkv, [shape(rows, width)] * 2, "unpack_kv"
-    )
-    return (attended, query_grad, key_grad, value_grad, gate_grad)
+        unpacking,
+        n_moves,
+        index,
+        dkv_first + dkv_second,
+        [shape(rows, width)] * 2,
+        "unpack_kv",
+    )
+    return (attended, query_grad, key_grad, value_grad, jnp.transpose(gate_grad))
 
 
 def solution(mesh):

time: 278 us -> 223 us (0.80)
  waiting for transfers between devices: 128 us -> 67.6 us
  Pallas kernels: 68.6 us -> 83.5 us
  other arithmetic: 8.69 us -> 1.83 us
  local copies, waits for them, and re-layouts: 15.2 us -> 10.1 us
    ppermute x28 -> x34, waiting for transfers between devices: 122 us -> 62 us  [swap(): lax.ppermute(block, axis, [(i, i ^ distance) for i in range(lax.axis_size...]
    pallas_call x4 -> x8, Pallas kernels: 57.1 us -> 70.9 us  [the longest x6 65.7 us: per_head_call(): pl.pallas_call(functools.partial(kernel, dims), grid_spec=pltpu.PrefetchS...]
    ppermute x28 -> x34, starting transfers between devices: 44.2 us -> 39.4 us  [swap(): lax.ppermute(block, axis, [(i, i ^ distance) for i in range(lax.axis_size...]
    ppermute x2 -> x3, starting transfers between devices: 6.66 us -> 10.7 us  [to_next(): return lax.ppermute(block, 'seq', [(i, i + 1) for i in range(count - 1)])]
    dynamic_slice x4 -> x0, local copies, waits for them, and re-layouts: 2.78 us -> none  [cut(): return lax.dynamic_slice_in_dim(x, at * size, size, 0)]
    ppermute x2 -> x3, starting transfers between devices: 4.02 us -> 6.27 us  [to_previous(): return lax.ppermute(block, 'seq', [(i + 1, i) for i in range(count - 1)])]
    ppermute x2 -> x3, waiting for transfers between devices: 4.6 us -> 5.58 us  [to_previous(): return lax.ppermute(block, 'seq', [(i + 1, i) for i in range(count - 1)])]
    unnamed x47 -> x74, local copies, waits for them, and re-layouts: 8.18 us -> 7.84 us
  transfers between devices with their start and end apart: 32 -> 40, of which waited for: 21 -> 16; matrix products, arithmetic and copies ran while one was open for 3% -> 2% of each run, Pallas kernels for 15% -> 29%
where the time goes in v2:
time: 223 us; the launch traced here: 221 us
  Pallas kernels  83.5 us (37%)
  waiting for transfers between devices  67.6 us (30%)
  starting transfers between devices  56.4 us (25%)
  local copies, waits for them, and re-layouts  10.1 us (5%)
    pallas_call x6, Pallas kernels, per_head_call(): pl.pallas_call(functools.partial(kernel, dims), grid_spec=pltpu.PrefetchS...  65.7 us
    ppermute x34, waiting for transfers between devices, swap(): lax.ppermute(block, axis, [(i, i ^ distance) for i in range(lax.axis_size...  62 us
    ppermute x34, starting transfers between devices, swap(): lax.ppermute(block, axis, [(i, i ^ distance) for i in range(lax.axis_size...  39.4 us
    pallas_call x4, Pallas kernels, local_copies(): pl.pallas_call(functools.partial(copy_kernel, moves_of, len(ins)), grid_s...  12.5 us
    ppermute x3, starting transfers between devices, to_next(): return lax.ppermute(block, 'seq', [(i, i + 1) for i in range(count - 1)])  10.7 us
    unnamed x74, local copies, waits for them, and re-layouts  7.84 us
    ppermute x3, starting transfers between devices, to_previous(): return lax.ppermute(block, 'seq', [(i + 1, i) for i in range(count - 1)])  6.27 us
    ppermute x3, waiting for transfers between devices, to_previous(): return lax.ppermute(block, 'seq', [(i + 1, i) for i in range(count - 1)])  5.58 us
  transfers between devices with their start and end apart: 40, of which 16 were waited for; matrix products, arithmetic and copies ran while one was open for 2% of the time, Pallas kernels for 29%

profile of v2, /device:TPU:1, one launch (start us, length us, event | category | flops | bytes accessed | tf_op | source)
XLA Modules:
  0.0 221.4 jit_solution(6088361163390044832)
XLA Ops:
  0.7 1.4 copy-done
  2.1 1.4 copy-done.1
  3.6 2.7 %pack_kv.1 = (f32[1536,128]{1,0:T(8,128)}, f32[1536,128]{1,0:T(8,128)}, f32[1536,128]{1,0:T(8,128)}) custom-call(s32[5]{0:T(128)S(1)} %stack.31.refs_0_.index, f32[128,3072]{1,0:T(8,128)S(1)} %copy-done, f32[128,3072]{1,0:T(8,128)S(1)} %copy-done.1), custom_call_target="tpu_custom_call" | custom-call | bytes 4718592 | tf_op jit(solution)/shard_map/pack_kv/pallas_call | solution.py:129
  6.3 2.1 collective-permute-start
  8.4 1.2 collective-permute-start.1
  11.6 2.5 %pack_qd.1 = (f32[1544,128]{1,0:T(8,128)}, f32[1544,128]{1,0:T(8,128)}, f32[1544,128]{1,0:T(8,128)S(1)}) custom-call(s32[5]{0:T(128)S(1)} %stack.31.refs_0_.index, f32[128,3072]{1,0:T(8,128)S(1)} %copy-done.2, f32[128,3072]{1,0:T(8,128)S(1)} %copy-done.3, f32[32,128]{1,0:T(8,128)S(1)} %maximum_bitcast_fusion.refs_3_.refs_8_), custom_call_target="tpu_custom_call" | custom-call | bytes 4743168 | tf_op jit(solution)/shard_map/pack_qd/pallas_call | solution.py:129
  15.7 10.3 %collective-permute-done.refs_1_.refs_5_ = f32[1536,128]{1,0:T(8,128)} collective-permute-done((f32[1536,128]{1,0:T(8,128)}, f32[1536,128]{1,0:T(8,128)}, u32[]{:S(2)}, u32[]{:S(2)}) %collective-permute-start) | collective-permute-done | bytes 786464 | tf_op jit(solution)/shard_map/ppermute | solution.py:393
  26.8 17.0 %collective-permute-done.2.refs_3_.refs_7_ = f32[1536,128]{1,0:T(8,128)} collective-permute-done((f32[1536,128]{1,0:T(8,128)}, f32[1536,128]{1,0:T(8,128)}, u32[]{:S(2)}, u32[]{:S(2)}) %collective-permute-start.2) | collective-permute-done | bytes 786464 | tf_op jit(solution)/shard_map/ppermute | solution.py:393
  43.8 1.2 collective-permute-start.7
  45.2 9.1 %key_sums.1 = (f32[3072,128]{1,0:T(8,128)}, f32[3072,128]{1,0:T(8,128)}, f32[800,128]{1,0:T(8,128)}, f32[800,128]{1,0:T(8,128)}, f32[768,128]{1,0:T(8,128)}, /*index=5*/f32[768,128]{1,0:T(8,128)}) custom-call(s32[5]{0:T(128)} %copy-done.11, f32[128,3072]{1,0:T(8,128)} %refs_0_.4, f32[1536,128]{1,0:T(8,128)} %collective-permute-done.refs_1_.refs_5_, ...), custom_call_target="tpu_custom_call" | custom-call | flops 1207959552 | bytes 9502720 | tf_op jit(solution)/shard_map/key_sums/pallas_call | solution.py:372
  54.3 2.4 %collective-permute-start.3 = (f32[800,128]{1,0:T(8,128)}, f32[800,128]{1,0:T(8,128)S(1)}, u32[]{:S(2)}, u32[]{:S(2)}) collective-permute-start(f32[800,128]{1,0:T(8,128)} %get-tuple-element.94), channel_id=1, source_target_pairs={{0,4},{4,0},{8,12},{12,8},{16,20},{20,16},{24,28},{28,24},{1,5},{5... | collective-permute-start | bytes 1228808 | tf_op jit(solution)/shard_map/ppermute | solution.py:393
  56.8 1.6 collective-permute-done.3.got_ref
  59.1 2.6 %cut_sums.2 = (f32[200,128]{1,0:T(8,128)}, f32[200,128]{1,0:T(8,128)}, f32[200,128]{1,0:T(8,128)}, f32[200,128]{1,0:T(8,128)}) custom-call(s32[5]{0:T(128)} %copy-done.11, f32[800,128]{1,0:T(8,128)} %get-tuple-element.93.mine_ref, f32[800,128]{1,0:T(8,128)} %copy-done.21), custom_call_target="tpu_custom_call" | custom-call | flops 102400 | bytes 1228800 | tf_op jit(solution)/shard_map/cut_sums/pallas_call | solution.py:399
  61.7 1.3 collective-permute-start.4
  63.0 2.3 %collective-permute-start.5 = (f32[200,128]{1,0:T(8,128)}, f32[200,128]{1,0:T(8,128)S(1)}, u32[]{:S(2)}, u32[]{:S(2)}) collective-permute-start(f32[200,128]{1,0:T(8,128)} %get-tuple-element.97), channel_id=1, source_target_pairs={{0,16},{4,20},{8,24},{12,28},{16,0},{20,4},{24,8},{28,12},{1,17},{... | collective-permute-start | bytes 307208 | tf_op jit(solution)/shard_map/ppermute | solution.py:393
  66.0 1.2 collective-permute-start.9
  67.6 4.8 %collective-permute-done.6 = f32[200,128]{1,0:T(8,128)S(1)} collective-permute-done((f32[200,128]{1,0:T(8,128)}, f32[200,128]{1,0:T(8,128)S(1)}, u32[]{:S(2)}, u32[]{:S(2)}) %collective-permute-start.6) | collective-permute-done | bytes 102432 | tf_op jit(solution)/shard_map/ppermute | solution.py:393
  73.4 2.6 %collective-permute-start.10 = (f32[200,128]{1,0:T(8,128)S(1)}, f32[200,128]{1,0:T(8,128)S(1)}, u32[]{:S(2)}, u32[]{:S(2)}) collective-permute-start(f32[200,128]{1,0:T(8,128)S(1)} %add_add_fusion.1), channel_id=1, source_target_pairs={{0,8},{4,12},{8,0},{12,4},{16,24},{20,28},{24,16},{28,20},{1,9},{5... | collective-permute-start | bytes 307208 | tf_op jit(solution)/shard_map/ppermute | solution.py:393
  76.1 1.0 collective-permute-start.11
  77.1 1.2 collective-permute-start.12
  78.5 3.6 %collective-permute-done.11 = f32[200,128]{1,0:T(8,128)S(1)} collective-permute-done((f32[200,128]{1,0:T(8,128)S(1)}, f32[200,128]{1,0:T(8,128)S(1)}, u32[]{:S(2)}, u32[]{:S(2)}) %collective-permute-start.11) | collective-permute-done | bytes 102432 | tf_op jit(solution)/shard_map/ppermute | solution.py:393
  82.2 1.6 collective-permute-done.12
  83.8 4.0 %collective-permute-start.13 = (f32[800,128]{1,0:T(8,128)S(1)}, f32[800,128]{1,0:T(8,128)}, u32[]{:S(2)}, u32[]{:S(2)}) collective-permute-start(f32[800,128]{1,0:T(8,128)S(1)} %constant_dynamic-update-slice_fusion.refs_12_), channel_id=1, source_target_pairs={{0,4},{4,0},{8,12},{12,8},{16,20},{20,16},{24,28},{28,24},{1,5},{5... | collective-permute-start | bytes 1228808 | tf_op jit(solution)/shard_map/ppermute | solution.py:393
  89.4 12.9 %query_low_rank.1 = (f32[768,512]{1,0:T(8,128)}, f32[768,512]{1,0:T(8,128)}, f32[800,128]{1,0:T(8,128)}, f32[800,128]{1,0:T(8,128)}) custom-call(s32[5]{0:T(128)} %copy-done.11, f32[128,3072]{1,0:T(8,128)} %refs_0_.7, f32[1544,128]{1,0:T(8,128)} %copy-done.15, f32[1544,128]{1,0:T(8,128)} %copy-done.16, ...), custom_call_target="tpu_custom_call" | custom-call | flops 2818572288 | bytes 7929856 | tf_op jit(solution)/shard_map/query_low_rank/pallas_call | solution.py:372
  102.8 3.3 %collective-permute-start.18 = (f32[768,128]{1,0:T(8,128)}, f32[768,128]{1,0:T(8,128)S(1)}, u32[]{:S(2)}, u32[]{:S(2)}) collective-permute-start(f32[768,128]{1,0:T(8,128)} %get-tuple-element.121), channel_id=1, source_target_pairs={{0,4},{4,8},{8,12},{12,16},{16,20},{20,24},{24,28},{1,5},{5,9},{9,... | collective-permute-start | bytes 1179656 | tf_op jit(solution)/shard_map/ppermute | solution.py:434
  106.1 2.1 collective-permute-start.19
  109.0 2.6 %cut_sums.3 = (f32[200,128]{1,0:T(8,128)}, f32[200,128]{1,0:T(8,128)}, f32[200,128]{1,0:T(8,128)}, f32[200,128]{1,0:T(8,128)}) custom-call(s32[5]{0:T(128)} %copy-done.11, f32[800,128]{1,0:T(8,128)} %get-tuple-element.107.mine_ref, f32[800,128]{1,0:T(8,128)} %copy-done.20), custom_call_target="tpu_custom_call" | custom-call | flops 102400 | bytes 1228800 | tf_op jit(solution)/shard_map/cut_sums/pallas_call | solution.py:399
  111.6 1.0 collective-permute-start.15
  112.8 2.3 %collective-permute-start.17 = (f32[200,128]{1,0:T(8,128)}, f32[200,128]{1,0:T(8,128)S(1)}, u32[]{:S(2)}, u32[]{:S(2)}) collective-permute-start(f32[200,128]{1,0:T(8,128)} %get-tuple-element.118), channel_id=1, source_target_pairs={{0,24},{4,28},{8,16},{12,20},{16,8},{20,12},{24,0},{28,4},{1,25},{... | collective-permute-start | bytes 307208 | tf_op jit(solution)/shard_map/ppermute | solution.py:393
  116.9 14.9 %sparse.2 = (f32[776,128]{1,0:T(8,128)}, f32[776,128]{1,0:T(8,128)}, f32[776,128]{1,0:T(8,128)}, f32[776,128]{1,0:T(8,128)}, f32[1536,128]{1,0:T(8,128)}, /*inde...) custom-call(s32[5]{0:T(128)} %copy-done.11, f32[128,3072]{1,0:T(8,128)} %refs_0_.7, f32[1544,128]{1,0:T(8,128)} %copy-done.15, ...), custom_call_target="tpu_custom_call" | custom-call | flops 5284823040 | bytes 7110656 | tf_op jit(solution)/shard_map/sparse/pallas_call | solution.py:372
  132.3 3.1 %collective-permute-start.25 = (f32[200,128]{1,0:T(8,128)S(1)}, f32[200,128]{1,0:T(8,128)S(1)}, u32[]{:S(2)}, u32[]{:S(2)}) collective-permute-start(f32[200,128]{1,0:T(8,128)S(1)} %add_add_fusion), channel_id=1, source_target_pairs={{0,24},{4,28},{8,16},{12,20},{16,8},{20,12},{24,0},{28,4},{1,25},{... | collective-permute-start | bytes 307208 | tf_op jit(solution)/shard_map/ppermute | solution.py:393
  135.5 1.2 collective-permute-start.20
  136.9 14.7 %sparse.3 = (f32[776,128]{1,0:T(8,128)}, f32[776,128]{1,0:T(8,128)}, f32[776,128]{1,0:T(8,128)}, f32[776,128]{1,0:T(8,128)}, f32[1536,128]{1,0:T(8,128)}, /*inde...) custom-call(s32[5]{0:T(128)} %copy-done.11, f32[128,3072]{1,0:T(8,128)} %refs_0_.7, f32[1544,128]{1,0:T(8,128)} %copy-done.15, ...), custom_call_target="tpu_custom_call" | custom-call | flops 5284823040 | bytes 7110656 | tf_op jit(solution)/shard_map/sparse/pallas_call | solution.py:372
  151.7 1.3 collective-permute-start.22
  153.0 3.5 %collective-permute-start.35 = (f32[384,128]{1,0:T(8,128)}, f32[384,128]{1,0:T(8,128)S(1)}, u32[]{:S(2)}, u32[]{:S(2)}) collective-permute-start(f32[384,128]{1,0:T(8,128)} %get-tuple-element.155), channel_id=1, source_target_pairs={{0,4},{4,8},{8,12},{12,16},{16,20},{20,24},{24,28},{1,5},{5,9},{9,... | collective-permute-start | bytes 589832 | tf_op jit(solution)/shard_map/ppermute | solution.py:434
  156.5 1.9 collective-permute-start.36
  159.2 1.3 collective-permute-start.26
  160.5 3.9 %collective-permute-start.30 = (f32[384,128]{1,0:T(8,128)S(1)}, f32[384,128]{1,0:T(8,128)S(1)}, u32[]{:S(2)}, u32[]{:S(2)}) collective-permute-start(f32[384,128]{1,0:T(8,128)S(1)} %copy-done.33), channel_id=1, source_target_pairs={{0,4},{4,8},{8,12},{12,16},{16,20},{20,24},{24,28},{1,5},{5,9},{9,... | collective-permute-start | bytes 589832 | tf_op jit(solution)/shard_map/ppermute | solution.py:434
  164.9 1.4 collective-permute-start.28
  166.4 7.1 %key_low_rank.3 = (f32[768,128]{1,0:T(8,128)}, f32[768,128]{1,0:T(8,128)}, f32[768,128]{1,0:T(8,128)}, f32[768,128]{1,0:T(8,128)}) custom-call(s32[5]{0:T(128)} %copy-done.11, f32[3072,128]{1,0:T(8,128)} %get-tuple-element.119.refs_12_.refs_0_, f32[3072,128]{1,0:T(8,128)} %get-tuple-element.120.refs_13_.refs_1_, f32[800,128]{1,0:T(8,128)} %copy-done.17, ...), custom_call_target="tpu_custom_call" | custom-call | flops 1308622848 | bytes 3145728 | tf_op jit(solution)/shard_map/key_low_rank/pallas_call | solution.py:372
  174.3 2.2 %collective-permute-start.31 = (f32[384,128]{1,0:T(8,128)S(1)}, f32[384,128]{1,0:T(8,128)S(1)}, u32[]{:S(2)}, u32[]{:S(2)}) collective-permute-start(f32[384,128]{1,0:T(8,128)S(1)} %copy-done.32), channel_id=1, source_target_pairs={{4,0},{8,4},{12,8},{16,12},{20,16},{24,20},{28,24},{5,1},{9,5},{13... | collective-permute-start | bytes 589832 | tf_op jit(solution)/shard_map/ppermute | solution.py:439
  177.0 4.6 %collective-permute-done.31.refs_7_ = f32[384,128]{1,0:T(8,128)S(1)} collective-permute-done((f32[384,128]{1,0:T(8,128)S(1)}, f32[384,128]{1,0:T(8,128)S(1)}, u32[]{:S(2)}, u32[]{:S(2)}) %collective-permute-start.31) | collective-permute-done | bytes 196640 | tf_op jit(solution)/shard_map/ppermute | solution.py:439
  182.6 7.1 %key_low_rank.2 = (f32[768,128]{1,0:T(8,128)}, f32[768,128]{1,0:T(8,128)}, f32[768,128]{1,0:T(8,128)}, f32[768,128]{1,0:T(8,128)}) custom-call(s32[5]{0:T(128)} %copy-done.11, f32[3072,128]{1,0:T(8,128)} %get-tuple-element.119.refs_12_.refs_0_, f32[3072,128]{1,0:T(8,128)} %get-tuple-element.120.refs_13_.refs_1_, f32[800,128]{1,0:T(8,128)} %copy-done.17, ...), custom_call_target="tpu_custom_call" | custom-call | flops 1308622848 | bytes 3145728 | tf_op jit(solution)/shard_map/key_low_rank/pallas_call | solution.py:372
  193.8 3.1 %unpack_od.1 = (f32[128,3072]{1,0:T(8,128)}, f32[128,3072]{1,0:T(8,128)}) custom-call(s32[5]{0:T(128)S(1)} %copy-done.12, f32[776,128]{1,0:T(8,128)S(1)} %copy-done.4, f32[776,128]{1,0:T(8,128)S(1)} %collective-permute-done.20.refs_2_, f32[776,128]{1,0:T(8,128)S(1)} %collective-permute-done.21.refs_3_, f32[776,128]{1,0:T(8,128)S(1)} %collective-permute-done.22.refs_4_, ...), custom_call_target="tpu_custom_call" | custom-call | bytes 6291456 | tf_op jit(solution)/shard_map/unpack_od/pallas_call | solution.py:129
  196.9 4.5 %collective-permute-done.38.refs_7_ = f32[768,128]{1,0:T(8,128)} collective-permute-done((f32[768,128]{1,0:T(8,128)}, f32[768,128]{1,0:T(8,128)}, u32[]{:S(2)}, u32[]{:S(2)}) %collective-permute-start.38) | collective-permute-done | bytes 393248 | tf_op jit(solution)/shard_map/ppermute | solution.py:393
  201.4 3.3 %collective-permute-done.32.refs_2_ = f32[768,128]{1,0:T(8,128)} collective-permute-done((f32[768,128]{1,0:T(8,128)}, f32[768,128]{1,0:T(8,128)}, u32[]{:S(2)}, u32[]{:S(2)}) %collective-permute-start.32) | collective-permute-done | bytes 393248 | tf_op jit(solution)/shard_map/ppermute | solution.py:393
  204.8 12.2 %collective-permute-done.33.refs_3_ = f32[768,128]{1,0:T(8,128)} collective-permute-done((f32[768,128]{1,0:T(8,128)}, f32[768,128]{1,0:T(8,128)}, u32[]{:S(2)}, u32[]{:S(2)}) %collective-permute-start.33) | collective-permute-done | bytes 393248 | tf_op jit(solution)/shard_map/ppermute | solution.py:393
  217.0 4.2 %unpack_kv.1 = (f32[128,3072]{1,0:T(8,128)}, f32[128,3072]{1,0:T(8,128)}) custom-call(s32[5]{0:T(128)S(1)} %copy-done.12, f32[768,128]{1,0:T(8,128)S(1)} %copy-done.9, f32[768,128]{1,0:T(8,128)} %collective-permute-done.32.refs_2_, f32[768,128]{1,0:T(8,128)} %collective-permute-done.33.refs_3_, f32[768,128]{1,0:T(8,128)} %collective-permute-done.34.refs_4_, ...), custom_call_target="tpu_custom_call" | custom-call | bytes 6291456 | tf_op jit(solution)/shard_map/unpack_kv/pallas_call | solution.py:129
  (148 shorter events, 20.1 us)
Async XLA Ops:
  6.3 19.7 %collective-permute-start = (f32[1536,128]{1,0:T(8,128)}, f32[1536,128]{1,0:T(8,128)}, u32[]{:S(2)}, u32[]{:S(2)}) collective-permute-start(f32[1536,128]{1,0:T(8,128)} %get-tuple-element.84), channel_id=1, source_target_pairs={{0,1},{1,0},{2,3},{3,2},{4,5},{5,4},{6,7},{7,6},{8,9},{9,8},{10,11... | collective-permute-start | bytes 2359304 | tf_op jit(solution)/shard_map/ppermute | solution.py:393
  8.4 18.4 %collective-permute-start.1 = (f32[1536,128]{1,0:T(8,128)}, f32[1536,128]{1,0:T(8,128)}, u32[]{:S(2)}, u32[]{:S(2)}) collective-permute-start(f32[1536,128]{1,0:T(8,128)} %get-tuple-element.85), channel_id=1, source_target_pairs={{0,2},{1,3},{2,0},{3,1},{4,6},{5,7},{6,4},{7,5},{8,10},{9,11},{10,... | collective-permute-start | bytes 2359304 | tf_op jit(solution)/shard_map/ppermute | solution.py:393
  9.6 34.1 %collective-permute-start.2 = (f32[1536,128]{1,0:T(8,128)}, f32[1536,128]{1,0:T(8,128)}, u32[]{:S(2)}, u32[]{:S(2)}) collective-permute-start(f32[1536,128]{1,0:T(8,128)} %get-tuple-element.86), channel_id=1, source_target_pairs={{0,3},{1,2},{2,1},{3,0},{4,7},{5,6},{6,5},{7,4},{8,11},{9,10},{10,... | collective-permute-start | bytes 2359304 | tf_op jit(solution)/shard_map/ppermute | solution.py:393
  43.8 22.2 %copy-start.14 = (f32[1544,128]{1,0:T(8,128)S(1)}, f32[1544,128]{1,0:T(8,128)}, u32[]{:S(2)}) copy-start(f32[1544,128]{1,0:T(8,128)} %copy-done.13) | copy-start | bytes 2371588
  43.8 29.6 %collective-permute-start.7 = (f32[1544,128]{1,0:T(8,128)}, f32[1544,128]{1,0:T(8,128)S(1)}, u32[]{:S(2)}, u32[]{:S(2)}) collective-permute-start(f32[1544,128]{1,0:T(8,128)} %get-tuple-element.99), channel_id=1, source_target_pairs={{0,1},{1,0},{2,3},{3,2},{4,5},{5,4},{6,7},{7,6},{8,9},{9,8},{10,11... | collective-permute-start | bytes 2371592 | tf_op jit(solution)/shard_map/ppermute | solution.py:393
  44.9 28.5 %collective-permute-start.8 = (f32[1544,128]{1,0:T(8,128)}, f32[1544,128]{1,0:T(8,128)S(1)}, u32[]{:S(2)}, u32[]{:S(2)}) collective-permute-start(f32[1544,128]{1,0:T(8,128)} %get-tuple-element.100), channel_id=1, source_target_pairs={{0,2},{1,3},{2,0},{3,1},{4,6},{5,7},{6,4},{7,5},{8,10},{9,11},{10,... | collective-permute-start | bytes 2371592 | tf_op jit(solution)/shard_map/ppermute | solution.py:393
  54.3 4.0 %collective-permute-start.3 = (f32[800,128]{1,0:T(8,128)}, f32[800,128]{1,0:T(8,128)S(1)}, u32[]{:S(2)}, u32[]{:S(2)}) collective-permute-start(f32[800,128]{1,0:T(8,128)} %get-tuple-element.94), channel_id=1, source_target_pairs={{0,4},{4,0},{8,12},{12,8},{16,20},{20,16},{24,28},{28,24},{1,5},{5... | collective-permute-start | bytes 1228808 | tf_op jit(solution)/shard_map/ppermute | solution.py:393
  61.7 4.3 %collective-permute-start.4 = (f32[200,128]{1,0:T(8,128)}, f32[200,128]{1,0:T(8,128)S(1)}, u32[]{:S(2)}, u32[]{:S(2)}) collective-permute-start(f32[200,128]{1,0:T(8,128)} %get-tuple-element.96), channel_id=1, source_target_pairs={{0,8},{4,12},{8,0},{12,4},{16,24},{20,28},{24,16},{28,20},{1,9},{5... | collective-permute-start | bytes 307208 | tf_op jit(solution)/shard_map/ppermute | solution.py:393
  63.0 4.6 %collective-permute-start.5 = (f32[200,128]{1,0:T(8,128)}, f32[200,128]{1,0:T(8,128)S(1)}, u32[]{:S(2)}, u32[]{:S(2)}) collective-permute-start(f32[200,128]{1,0:T(8,128)} %get-tuple-element.97), channel_id=1, source_target_pairs={{0,16},{4,20},{8,24},{12,28},{16,0},{20,4},{24,8},{28,12},{1,17},{... | collective-permute-start | bytes 307208 | tf_op jit(solution)/shard_map/ppermute | solution.py:393
  65.3 7.2 %collective-permute-start.6 = (f32[200,128]{1,0:T(8,128)}, f32[200,128]{1,0:T(8,128)S(1)}, u32[]{:S(2)}, u32[]{:S(2)}) collective-permute-start(f32[200,128]{1,0:T(8,128)} %get-tuple-element.98), channel_id=1, source_target_pairs={{0,24},{4,28},{8,16},{12,20},{16,8},{20,12},{24,0},{28,4},{1,25},{... | collective-permute-start | bytes 307208 | tf_op jit(solution)/shard_map/ppermute | solution.py:393
  66.0 22.6 %collective-permute-start.9 = (f32[1544,128]{1,0:T(8,128)S(1)}, f32[1544,128]{1,0:T(8,128)}, u32[]{:S(2)}, u32[]{:S(2)}) collective-permute-start(f32[1544,128]{1,0:T(8,128)S(1)} %copy-done.14), channel_id=1, source_target_pairs={{0,3},{1,2},{2,1},{3,0},{4,7},{5,6},{6,5},{7,4},{8,11},{9,10},{10,... | collective-permute-start | bytes 2371592 | tf_op jit(solution)/shard_map/ppermute | solution.py:393
  73.4 5.1 %collective-permute-start.10 = (f32[200,128]{1,0:T(8,128)S(1)}, f32[200,128]{1,0:T(8,128)S(1)}, u32[]{:S(2)}, u32[]{:S(2)}) collective-permute-start(f32[200,128]{1,0:T(8,128)S(1)} %add_add_fusion.1), channel_id=1, source_target_pairs={{0,8},{4,12},{8,0},{12,4},{16,24},{20,28},{24,16},{28,20},{1,9},{5... | collective-permute-start | bytes 307208 | tf_op jit(solution)/shard_map/ppermute | solution.py:393
  76.1 6.1 %collective-permute-start.11 = (f32[200,128]{1,0:T(8,128)S(1)}, f32[200,128]{1,0:T(8,128)S(1)}, u32[]{:S(2)}, u32[]{:S(2)}) collective-permute-start(f32[200,128]{1,0:T(8,128)S(1)} %add_add_fusion.1), channel_id=1, source_target_pairs={{0,16},{4,20},{8,24},{12,28},{16,0},{20,4},{24,8},{28,12},{1,17},{... | collective-permute-start | bytes 307208 | tf_op jit(solution)/shard_map/ppermute | solution.py:393
  77.1 6.7 %collective-permute-start.12 = (f32[200,128]{1,0:T(8,128)S(1)}, f32[200,128]{1,0:T(8,128)S(1)}, u32[]{:S(2)}, u32[]{:S(2)}) collective-permute-start(f32[200,128]{1,0:T(8,128)S(1)} %add_add_fusion.1), channel_id=1, source_target_pairs={{0,24},{4,28},{8,16},{12,20},{16,8},{20,12},{24,0},{28,4},{1,25},{... | collective-permute-start | bytes 307208 | tf_op jit(solution)/shard_map/ppermute | solution.py:393
  83.8 5.6 %collective-permute-start.13 = (f32[800,128]{1,0:T(8,128)S(1)}, f32[800,128]{1,0:T(8,128)}, u32[]{:S(2)}, u32[]{:S(2)}) collective-permute-start(f32[800,128]{1,0:T(8,128)S(1)} %constant_dynamic-update-slice_fusion.refs_12_), channel_id=1, source_target_pairs={{0,4},{4,0},{8,12},{12,8},{16,20},{20,16},{24,28},{28,24},{1,5},{5... | collective-permute-start | bytes 1228808 | tf_op jit(solution)/shard_map/ppermute | solution.py:393
  88.6 17.5 %copy-start.29 = (f32[768,128]{1,0:T(8,128)S(1)}, f32[768,128]{1,0:T(8,128)}, u32[]{:S(2)}) copy-start(f32[768,128]{1,0:T(8,128)} %get-tuple-element.122) | copy-start | bytes 1179652
  102.3 5.9 %collective-permute-start.14 = (f32[800,128]{1,0:T(8,128)}, f32[800,128]{1,0:T(8,128)S(1)}, u32[]{:S(2)}, u32[]{:S(2)}) collective-permute-start(f32[800,128]{1,0:T(8,128)} %get-tuple-element.108), channel_id=1, source_target_pairs={{0,4},{4,0},{8,12},{12,8},{16,20},{20,16},{24,28},{28,24},{1,5},{5... | collective-permute-start | bytes 1228808 | tf_op jit(solution)/shard_map/ppermute | solution.py:393
  102.8 12.3 %collective-permute-start.18 = (f32[768,128]{1,0:T(8,128)}, f32[768,128]{1,0:T(8,128)S(1)}, u32[]{:S(2)}, u32[]{:S(2)}) collective-permute-start(f32[768,128]{1,0:T(8,128)} %get-tuple-element.121), channel_id=1, source_target_pairs={{0,4},{4,8},{8,12},{12,16},{16,20},{20,24},{24,28},{1,5},{5,9},{9,... | collective-permute-start | bytes 1179656 | tf_op jit(solution)/shard_map/ppermute | solution.py:434
  106.1 10.0 %collective-permute-start.19 = (f32[768,128]{1,0:T(8,128)S(1)}, f32[768,128]{1,0:T(8,128)S(1)}, u32[]{:S(2)}, u32[]{:S(2)}) collective-permute-start(f32[768,128]{1,0:T(8,128)S(1)} %copy-done.29), channel_id=1, source_target_pairs={{4,0},{8,4},{12,8},{16,12},{20,16},{24,20},{28,24},{5,1},{9,5},{13... | collective-permute-start | bytes 1179656 | tf_op jit(solution)/shard_map/ppermute | solution.py:439
  111.6 20.2 %collective-permute-start.15 = (f32[200,128]{1,0:T(8,128)}, f32[200,128]{1,0:T(8,128)S(1)}, u32[]{:S(2)}, u32[]{:S(2)}) collective-permute-start(f32[200,128]{1,0:T(8,128)} %get-tuple-element.116), channel_id=1, source_target_pairs={{0,8},{4,12},{8,0},{12,4},{16,24},{20,28},{24,16},{28,20},{1,9},{5... | collective-permute-start | bytes 307208 | tf_op jit(solution)/shard_map/ppermute | solution.py:393
  112.6 19.2 %collective-permute-start.16 = (f32[200,128]{1,0:T(8,128)}, f32[200,128]{1,0:T(8,128)S(1)}, u32[]{:S(2)}, u32[]{:S(2)}) collective-permute-start(f32[200,128]{1,0:T(8,128)} %get-tuple-element.117), channel_id=1, source_target_pairs={{0,16},{4,20},{8,24},{12,28},{16,0},{20,4},{24,8},{28,12},{1,17},{... | collective-permute-start | bytes 307208 | tf_op jit(solution)/shard_map/ppermute | solution.py:393
  112.8 18.9 %collective-permute-start.17 = (f32[200,128]{1,0:T(8,128)}, f32[200,128]{1,0:T(8,128)S(1)}, u32[]{:S(2)}, u32[]{:S(2)}) collective-permute-start(f32[200,128]{1,0:T(8,128)} %get-tuple-element.118), channel_id=1, source_target_pairs={{0,24},{4,28},{8,16},{12,20},{16,8},{20,12},{24,0},{28,4},{1,25},{... | collective-permute-start | bytes 307208 | tf_op jit(solution)/shard_map/ppermute | solution.py:393
  131.8 19.8 %copy-start.4 = (f32[776,128]{1,0:T(8,128)S(1)}, f32[776,128]{1,0:T(8,128)}, u32[]{:S(2)}) copy-start(f32[776,128]{1,0:T(8,128)} %get-tuple-element.127.refs_1_) | copy-start | bytes 1191940
  131.8 19.8 %copy-start.28 = (f32[776,128]{1,0:T(8,128)S(1)}, f32[776,128]{1,0:T(8,128)}, u32[]{:S(2)}) copy-start(f32[776,128]{1,0:T(8,128)} %get-tuple-element.130) | copy-start | bytes 1191940
  131.8 28.6 %copy-start.33 = (f32[384,128]{1,0:T(8,128)S(1)}, f32[384,128]{1,0:T(8,128)}, u32[]{:S(2)}) copy-start(f32[384,128]{1,0:T(8,128)} %get-tuple-element.147) | copy-start | bytes 589828
  131.9 19.8 %collective-permute-start.23 = (f32[200,128]{1,0:T(8,128)S(1)}, f32[200,128]{1,0:T(8,128)S(1)}, u32[]{:S(2)}, u32[]{:S(2)}) collective-permute-start(f32[200,128]{1,0:T(8,128)S(1)} %add_add_fusion), channel_id=1, source_target_pairs={{0,8},{4,12},{8,0},{12,4},{16,24},{20,28},{24,16},{28,20},{1,9},{5... | collective-permute-start | bytes 307208 | tf_op jit(solution)/shard_map/ppermute | solution.py:393
  132.0 20.9 %collective-permute-start.24 = (f32[200,128]{1,0:T(8,128)S(1)}, f32[200,128]{1,0:T(8,128)S(1)}, u32[]{:S(2)}, u32[]{:S(2)}) collective-permute-start(f32[200,128]{1,0:T(8,128)S(1)} %add_add_fusion), channel_id=1, source_target_pairs={{0,16},{4,20},{8,24},{12,28},{16,0},{20,4},{24,8},{28,12},{1,17},{... | collective-permute-start | bytes 307208 | tf_op jit(solution)/shard_map/ppermute | solution.py:393
  132.3 24.2 %collective-permute-start.25 = (f32[200,128]{1,0:T(8,128)S(1)}, f32[200,128]{1,0:T(8,128)S(1)}, u32[]{:S(2)}, u32[]{:S(2)}) collective-permute-start(f32[200,128]{1,0:T(8,128)S(1)} %add_add_fusion), channel_id=1, source_target_pairs={{0,24},{4,28},{8,16},{12,20},{16,8},{20,12},{24,0},{28,4},{1,25},{... | collective-permute-start | bytes 307208 | tf_op jit(solution)/shard_map/ppermute | solution.py:393
  135.5 23.7 %collective-permute-start.20 = (f32[776,128]{1,0:T(8,128)}, f32[776,128]{1,0:T(8,128)S(1)}, u32[]{:S(2)}, u32[]{:S(2)}) collective-permute-start(f32[776,128]{1,0:T(8,128)} %get-tuple-element.128), channel_id=1, source_target_pairs={{0,1},{1,0},{2,3},{3,2},{4,5},{5,4},{6,7},{7,6},{8,9},{9,8},{10,11... | collective-permute-start | bytes 1191944 | tf_op jit(solution)/shard_map/ppermute | solution.py:393
  136.7 22.5 %collective-permute-start.21 = (f32[776,128]{1,0:T(8,128)}, f32[776,128]{1,0:T(8,128)S(1)}, u32[]{:S(2)}, u32[]{:S(2)}) collective-permute-start(f32[776,128]{1,0:T(8,128)} %get-tuple-element.129), channel_id=1, source_target_pairs={{0,2},{1,3},{2,0},{3,1},{4,6},{5,7},{6,4},{7,5},{8,10},{9,11},{10,... | collective-permute-start | bytes 1191944 | tf_op jit(solution)/shard_map/ppermute | solution.py:393
  151.7 21.8 %collective-permute-start.22 = (f32[776,128]{1,0:T(8,128)S(1)}, f32[776,128]{1,0:T(8,128)S(1)}, u32[]{:S(2)}, u32[]{:S(2)}) collective-permute-start(f32[776,128]{1,0:T(8,128)S(1)} %copy-done.28), channel_id=1, source_target_pairs={{0,3},{1,2},{2,1},{3,0},{4,7},{5,6},{6,5},{7,4},{8,11},{9,10},{10,... | collective-permute-start | bytes 1191944 | tf_op jit(solution)/shard_map/ppermute | solution.py:393
  153.0 7.5 %collective-permute-start.35 = (f32[384,128]{1,0:T(8,128)}, f32[384,128]{1,0:T(8,128)S(1)}, u32[]{:S(2)}, u32[]{:S(2)}) collective-permute-start(f32[384,128]{1,0:T(8,128)} %get-tuple-element.155), channel_id=1, source_target_pairs={{0,4},{4,8},{8,12},{12,16},{16,20},{20,24},{24,28},{1,5},{5,9},{9,... | collective-permute-start | bytes 589832 | tf_op jit(solution)/shard_map/ppermute | solution.py:434
  156.5 7.9 %collective-permute-start.36 = (f32[384,128]{1,0:T(8,128)}, f32[384,128]{1,0:T(8,128)S(1)}, u32[]{:S(2)}, u32[]{:S(2)}) collective-permute-start(f32[384,128]{1,0:T(8,128)} %get-tuple-element.156), channel_id=1, source_target_pairs={{4,0},{8,4},{12,8},{16,12},{20,16},{24,20},{28,24},{5,1},{9,5},{13... | collective-permute-start | bytes 589832 | tf_op jit(solution)/shard_map/ppermute | solution.py:439
  159.2 5.7 %collective-permute-start.29 = (f32[800,128]{1,0:T(8,128)S(1)}, f32[800,128]{1,0:T(8,128)S(1)}, u32[]{:S(2)}, u32[]{:S(2)}) collective-permute-start(f32[800,128]{1,0:T(8,128)S(1)} %pad_maximum_fusion.refs_2_), channel_id=1, source_target_pairs={{0,4},{4,0},{8,12},{12,8},{16,20},{20,16},{24,28},{28,24},{1,5},{5... | collective-permute-start | bytes 1228808 | tf_op jit(solution)/shard_map/ppermute | solution.py:393
  159.2 15.1 %collective-permute-start.26 = (f32[776,128]{1,0:T(8,128)}, f32[776,128]{1,0:T(8,128)S(1)}, u32[]{:S(2)}, u32[]{:S(2)}) collective-permute-start(f32[776,128]{1,0:T(8,128)} %get-tuple-element.139), channel_id=1, source_target_pairs={{0,1},{1,0},{2,3},{3,2},{4,5},{5,4},{6,7},{7,6},{8,9},{9,8},{10,11... | collective-permute-start | bytes 1191944 | tf_op jit(solution)/shard_map/ppermute | solution.py:393
  160.5 16.1 %collective-permute-start.30 = (f32[384,128]{1,0:T(8,128)S(1)}, f32[384,128]{1,0:T(8,128)S(1)}, u32[]{:S(2)}, u32[]{:S(2)}) collective-permute-start(f32[384,128]{1,0:T(8,128)S(1)} %copy-done.33), channel_id=1, source_target_pairs={{0,4},{4,8},{8,12},{12,16},{16,20},{20,24},{24,28},{1,5},{5,9},{9,... | collective-permute-start | bytes 589832 | tf_op jit(solution)/shard_map/ppermute | solution.py:434
  164.4 25.2 %collective-permute-start.27 = (f32[776,128]{1,0:T(8,128)}, f32[776,128]{1,0:T(8,128)S(1)}, u32[]{:S(2)}, u32[]{:S(2)}) collective-permute-start(f32[776,128]{1,0:T(8,128)} %get-tuple-element.140), channel_id=1, source_target_pairs={{0,2},{1,3},{2,0},{3,1},{4,6},{5,7},{6,4},{7,5},{8,10},{9,11},{10,... | collective-permute-start | bytes 1191944 | tf_op jit(solution)/shard_map/ppermute | solution.py:393
  164.9 25.6 %collective-permute-start.28 = (f32[776,128]{1,0:T(8,128)}, f32[776,128]{1,0:T(8,128)S(1)}, u32[]{:S(2)}, u32[]{:S(2)}) collective-permute-start(f32[776,128]{1,0:T(8,128)} %get-tuple-element.141), channel_id=1, source_target_pairs={{0,3},{1,2},{2,1},{3,0},{4,7},{5,6},{6,5},{7,4},{8,11},{9,10},{10,... | collective-permute-start | bytes 1191944 | tf_op jit(solution)/shard_map/ppermute | solution.py:393
  173.5 18.0 %collective-permute-start.37 = (f32[768,128]{1,0:T(8,128)}, f32[768,128]{1,0:T(8,128)S(1)}, u32[]{:S(2)}, u32[]{:S(2)}) collective-permute-start(f32[768,128]{1,0:T(8,128)} %get-tuple-element.158), channel_id=1, source_target_pairs={{0,1},{1,0},{2,3},{3,2},{4,5},{5,4},{6,7},{7,6},{8,9},{9,8},{10,11... | collective-permute-start | bytes 1179656 | tf_op jit(solution)/shard_map/ppermute | solution.py:393
  174.3 7.3 %collective-permute-start.31 = (f32[384,128]{1,0:T(8,128)S(1)}, f32[384,128]{1,0:T(8,128)S(1)}, u32[]{:S(2)}, u32[]{:S(2)}) collective-permute-start(f32[384,128]{1,0:T(8,128)S(1)} %copy-done.32), channel_id=1, source_target_pairs={{4,0},{8,4},{12,8},{16,12},{20,16},{24,20},{28,24},{5,1},{9,5},{13... | collective-permute-start | bytes 589832 | tf_op jit(solution)/shard_map/ppermute | solution.py:439
  176.6 24.8 %collective-permute-start.38 = (f32[768,128]{1,0:T(8,128)}, f32[768,128]{1,0:T(8,128)}, u32[]{:S(2)}, u32[]{:S(2)}) collective-permute-start(f32[768,128]{1,0:T(8,128)} %get-tuple-element.159), channel_id=1, source_target_pairs={{0,2},{1,3},{2,0},{3,1},{4,6},{5,7},{6,4},{7,5},{8,10},{9,11},{10,... | collective-permute-start | bytes 1179656 | tf_op jit(solution)/shard_map/ppermute | solution.py:393
  181.6 19.8 %collective-permute-start.39 = (f32[768,128]{1,0:T(8,128)}, f32[768,128]{1,0:T(8,128)}, u32[]{:S(2)}, u32[]{:S(2)}) collective-permute-start(f32[768,128]{1,0:T(8,128)} %get-tuple-element.160), channel_id=1, source_target_pairs={{0,3},{1,2},{2,1},{3,0},{4,7},{5,6},{6,5},{7,4},{8,11},{9,10},{10,... | collective-permute-start | bytes 1179656 | tf_op jit(solution)/shard_map/ppermute | solution.py:393
  189.7 15.1 %collective-permute-start.32 = (f32[768,128]{1,0:T(8,128)}, f32[768,128]{1,0:T(8,128)}, u32[]{:S(2)}, u32[]{:S(2)}) collective-permute-start(f32[768,128]{1,0:T(8,128)} %get-tuple-element.150), channel_id=1, source_target_pairs={{0,1},{1,0},{2,3},{3,2},{4,5},{5,4},{6,7},{7,6},{8,9},{9,8},{10,11... | collective-permute-start | bytes 1179656 | tf_op jit(solution)/shard_map/ppermute | solution.py:393
  190.5 26.4 %collective-permute-start.33 = (f32[768,128]{1,0:T(8,128)}, f32[768,128]{1,0:T(8,128)}, u32[]{:S(2)}, u32[]{:S(2)}) collective-permute-start(f32[768,128]{1,0:T(8,128)} %get-tuple-element.151), channel_id=1, source_target_pairs={{0,2},{1,3},{2,0},{3,1},{4,6},{5,7},{6,4},{7,5},{8,10},{9,11},{10,... | collective-permute-start | bytes 1179656 | tf_op jit(solution)/shard_map/ppermute | solution.py:393
  192.2 24.7 %collective-permute-start.34 = (f32[768,128]{1,0:T(8,128)}, f32[768,128]{1,0:T(8,128)}, u32[]{:S(2)}, u32[]{:S(2)}) collective-permute-start(f32[768,128]{1,0:T(8,128)} %get-tuple-element.152), channel_id=1, source_target_pairs={{0,3},{1,2},{2,1},{3,0},{4,7},{5,6},{6,5},{7,4},{8,11},{9,10},{10,... | collective-permute-start | bytes 1179656 | tf_op jit(solution)/shard_map/ppermute | solution.py:393
  193.8 23.2 %copy-start.6 = (f32[768,128]{1,0:T(8,128)S(1)}, f32[768,128]{1,0:T(8,128)}, u32[]{:S(2)}) copy-start(f32[768,128]{1,0:T(8,128)} %get-tuple-element.157.refs_5_) | copy-start | bytes 1179652
  193.8 23.2 %copy-start.8 = (f32[768,128]{1,0:T(8,128)S(1)}, f32[768,128]{1,0:T(8,128)}, u32[]{:S(2)}) copy-start(f32[768,128]{1,0:T(8,128)} %copy-done.7) | copy-start | bytes 1179652
  193.8 23.2 %copy-start.9 = (f32[768,128]{1,0:T(8,128)S(1)}, f32[768,128]{1,0:T(8,128)}, u32[]{:S(2)}) copy-start(f32[768,128]{1,0:T(8,128)} %get-tuple-element.149.refs_1_) | copy-start | bytes 1179652
  (27 other events, 158.0 us)

commit v3 on v2

--- a/solution.py
+++ b/solution.py
@@ -26,8 +26,22 @@
     return lax.dot_general(a, b, (((1,), (0,)), ((), ())), preferred_element_type=F32)
 
 
-def mm3(a, b):
-    return mm(a[0], b[0]) + (mm(a[0], b[1]) + mm(a[1], b[0]))
+def mm3_deep(a, b):
+    return mm(
+        jnp.concatenate([a[0], a[1], a[0]], axis=1), jnp.concatenate([b[0], b[0], b[1]], axis=0)
+    )
+
+
+def mm3_tall(a, b):
+    rows = a[0].shape[0]
+    both = mm(jnp.concatenate(a, axis=0), b[0])
+    return both[:rows] + (both[rows:] + mm(a[0], b[1]))
+
+
+def mm3_wide(a, b):
+    columns = b[0].shape[1]
+    both = mm(a[0], jnp.concatenate(b, axis=1))
+    return both[:, :columns] + (both[:, columns:] + mm(a[1], b[0]))
 
 
 def split3(x):
@@ -38,10 +52,7 @@
 
 
 def mm_exact(exact, b):
-    total = mm(exact, b[-1])
-    for part in b[-2::-1]:
-        total = mm(exact, part) + total
-    return total
+    return mm(jnp.concatenate([exact] * len(b), axis=1), jnp.concatenate(b[::-1], axis=0))
 
 
 def mm6(a, b):
@@ -169,7 +180,7 @@
     high_edge[reach:] = values[tokens - reach :]
     normed, _ = normed_t(jnp.transpose(keys))
     feats = features_t(seed_t_ref[...], normed)
-    sums_out[pl.ds(pl.multiple_of(head * 256, 256), 256), :] = mm3(split2(feats), split2(values))
+    sums_out[pl.ds(pl.multiple_of(head * 256, 256), 256), :] = mm3_wide(split2(feats), split2(values))
     sums_out[pl.ds(pl.multiple_of(heads * 256 + head * EXT, EXT), EXT), :] = column_to_rows(
         jnp.sum(feats, axis=1, keepdims=True)
     )
@@ -207,13 +218,13 @@
     feats = features_t(seed_t_ref[...], normed)
     feats_parts = split2(feats)
     inverse = 1.0 / jnp.sum(feats * totals, axis=0, keepdims=True)
-    low = mm3(split2(jnp.transpose(sums)), feats_parts) * inverse
+    low = mm3_tall(split2(jnp.transpose(sums)), feats_parts) * inverse
     dnum = jnp.transpose(grads[...]) * ((1.0 - gate) * inverse)
     dden = -jnp.sum(dnum * low, axis=0, keepdims=True)
-    dfeats = mm3(split2(sums), split2(dnum)) + totals * dden
+    dfeats = mm3_deep(split2(sums), split2(dnum)) + totals * dden
     low_out[...] = low
     query_out[...] = normed_grad_t(seed_ref[...], feats, dfeats, normed, scale)
-    sums_out[pl.ds(pl.multiple_of(head * 256, 256), 256), :] = mm3(
+    sums_out[pl.ds(pl.multiple_of(head * 256, 256), 256), :] = mm3_wide(
         feats_parts, split2(jnp.transpose(dnum))
     )
     sums_out[pl.ds(pl.multiple_of(heads * 256 + head * EXT, EXT), EXT), :] = column_to_rows(
@@ -293,17 +304,17 @@
     weights = jnp.exp(scores - jnp.max(scores, axis=0, keepdims=True))
     inverse = 1.0 / jnp.sum(weights, axis=0, keepdims=True)
     weight_parts = split2(weights)
-    mixed = mm3(values_t, weight_parts) * inverse
+    mixed = mm3_tall(values_t, weight_parts) * inverse
     low = low_ref[...]
     grad_t = jnp.transpose(grads[...])
     gate_grad = jnp.sum(grad_t * (mixed - low), axis=0, keepdims=True) * gate * (1.0 - gate)
     sparse_grad = grad_t * (gate * inverse)
     delta = jnp.sum(sparse_grad * mixed, axis=0, keepdims=True)
-    score_grad = weights * (mm3(values, split2(sparse_grad)) - delta)
+    score_grad = weights * (mm3_deep(values, split2(sparse_grad)) - delta)
     score_parts = split2(score_grad)
-    query_grad = mm3(keys_t, score_parts) * root + query_low_ref[...]
-    keys_grad = mm3(score_parts, split2(scaled))
-    values_grad = mm3(weight_parts, split2(jnp.transpose(sparse_grad)))
+    query_grad = mm3_tall(keys_t, score_parts) * root + query_low_ref[...]
+    keys_grad = mm3_wide(score_parts, split2(scaled))
+    values_grad = mm3_wide(weight_parts, split2(jnp.transpose(sparse_grad)))
     keys_out[...] = keys_grad[:tokens]
     values_out[...] = values_grad[:tokens]
     left_out[:reach] = keys_grad[tokens : tokens + reach]
@@ -350,9 +361,9 @@
     totals = rows_to_column(sums_ref[pl.ds(pl.multiple_of(heads * 256 + head * EXT, EXT), EXT), :])
     normed, scale = normed_t(jnp.transpose(keys_ref[...]))
     feats = features_t(seed_t_ref[...], normed)
-    dfeats = mm3(split2(sums), split2(jnp.transpose(values_ref[...]))) + totals
+    dfeats = mm3_deep(split2(sums), split2(jnp.transpose(values_ref[...]))) + totals
     key_low = normed_grad_t(seed_ref[...], feats, dfeats, normed, scale)
-    value_low = mm3(split2(jnp.transpose(sums)), split2(feats))
+    value_low = mm3_tall(split2(jnp.transpose(sums)), split2(feats))
     dkeys[...] = keys_grad[...] + jnp.transpose(key_low)
     dvalues[...] = values_grad[...] + jnp.transpose(value_low)
     dkeys[:reach] += left_ref[:reach]

time: 223 us -> 216 us (0.969)
  Pallas kernels: 83.5 us -> 76.8 us
    pallas_call x6, Pallas kernels: 65.7 us -> 59 us  [per_head_call(): pl.pallas_call(functools.partial(kernel, dims), grid_spec=pltpu.PrefetchS...]
  transfers between devices with their start and end apart: 40 -> 40, of which waited for: 16 -> 16; matrix products, arithmetic and copies ran while one was open for 2% -> 2% of each run, Pallas kernels for 29% -> 27%
where the time goes in v3:
time: 216 us; the launch traced here: 215 us
  Pallas kernels  76.8 us (36%)
  waiting for transfers between devices  68.3 us (32%)
  starting transfers between devices  56.1 us (26%)
  local copies, waits for them, and re-layouts  10.1 us (5%)
    ppermute x34, waiting for transfers between devices, swap(): lax.ppermute(block, axis, [(i, i ^ distance) for i in range(lax.axis_size...  62.5 us
    pallas_call x6, Pallas kernels, per_head_call(): pl.pallas_call(functools.partial(kernel, dims), grid_spec=pltpu.PrefetchS...  59 us
    ppermute x34, starting transfers between devices, swap(): lax.ppermute(block, axis, [(i, i ^ distance) for i in range(lax.axis_size...  39 us
    pallas_call x4, Pallas kernels, local_copies(): pl.pallas_call(functools.partial(copy_kernel, moves_of, len(ins)), grid_s...  12.5 us
    ppermute x3, starting transfers between devices, to_next(): return lax.ppermute(block, 'seq', [(i, i + 1) for i in range(count - 1)])  10.8 us
    unnamed x74, local copies, waits for them, and re-layouts  7.84 us
    ppermute x3, starting transfers between devices, to_previous(): return lax.ppermute(block, 'seq', [(i + 1, i) for i in range(count - 1)])  6.32 us
    ppermute x3, waiting for transfers between devices, to_previous(): return lax.ppermute(block, 'seq', [(i + 1, i) for i in range(count - 1)])  5.83 us
  transfers between devices with their start and end apart: 40, of which 16 were waited for; matrix products, arithmetic and copies ran while one was open for 2% of the time, Pallas kernels for 27%

profile of v3, /device:TPU:1, one launch (start us, length us, event | category | flops | bytes accessed | tf_op | source)
XLA Modules:
  0.0 215.1 jit_solution(15523965882174949727)
XLA Ops:
  0.7 1.4 copy-done
  2.1 1.4 copy-done.1
  3.6 2.7 %pack_kv.1 = (f32[1536,128]{1,0:T(8,128)}, f32[1536,128]{1,0:T(8,128)}, f32[1536,128]{1,0:T(8,128)}) custom-call(s32[5]{0:T(128)S(1)} %stack.31.refs_0_.index, f32[128,3072]{1,0:T(8,128)S(1)} %copy-done, f32[128,3072]{1,0:T(8,128)S(1)} %copy-done.1), custom_call_target="tpu_custom_call" | custom-call | bytes 4718592 | tf_op jit(solution)/shard_map/pack_kv/pallas_call | solution.py:140
  6.3 2.1 collective-permute-start
  8.4 1.2 collective-permute-start.1
  11.6 2.5 %pack_qd.1 = (f32[1544,128]{1,0:T(8,128)}, f32[1544,128]{1,0:T(8,128)}, f32[1544,128]{1,0:T(8,128)S(1)}) custom-call(s32[5]{0:T(128)S(1)} %stack.31.refs_0_.index, f32[128,3072]{1,0:T(8,128)S(1)} %copy-done.2, f32[128,3072]{1,0:T(8,128)S(1)} %copy-done.3, f32[32,128]{1,0:T(8,128)S(1)} %maximum_bitcast_fusion.refs_3_.refs_8_), custom_call_target="tpu_custom_call" | custom-call | bytes 4743168 | tf_op jit(solution)/shard_map/pack_qd/pallas_call | solution.py:140
  15.7 10.3 %collective-permute-done.refs_1_.refs_5_ = f32[1536,128]{1,0:T(8,128)} collective-permute-done((f32[1536,128]{1,0:T(8,128)}, f32[1536,128]{1,0:T(8,128)}, u32[]{:S(2)}, u32[]{:S(2)}) %collective-permute-start) | collective-permute-done | bytes 786464 | tf_op jit(solution)/shard_map/ppermute | solution.py:404
  26.8 17.0 %collective-permute-done.2.refs_3_.refs_7_ = f32[1536,128]{1,0:T(8,128)} collective-permute-done((f32[1536,128]{1,0:T(8,128)}, f32[1536,128]{1,0:T(8,128)}, u32[]{:S(2)}, u32[]{:S(2)}) %collective-permute-start.2) | collective-permute-done | bytes 786464 | tf_op jit(solution)/shard_map/ppermute | solution.py:404
  43.8 1.2 collective-permute-start.7
  45.2 8.5 %key_sums.1 = (f32[3072,128]{1,0:T(8,128)}, f32[3072,128]{1,0:T(8,128)}, f32[800,128]{1,0:T(8,128)}, f32[800,128]{1,0:T(8,128)}, f32[768,128]{1,0:T(8,128)}, /*index=5*/f32[768,128]{1,0:T(8,128)}) custom-call(s32[5]{0:T(128)} %copy-done.11, f32[128,3072]{1,0:T(8,128)} %refs_0_.4, f32[1536,128]{1,0:T(8,128)} %collective-permute-done.refs_1_.refs_5_, ...), custom_call_target="tpu_custom_call" | custom-call | flops 1207959552 | bytes 9502720 | tf_op jit(solution)/shard_map/key_sums/pallas_call | solution.py:383
  53.7 2.4 %collective-permute-start.3 = (f32[800,128]{1,0:T(8,128)}, f32[800,128]{1,0:T(8,128)S(1)}, u32[]{:S(2)}, u32[]{:S(2)}) collective-permute-start(f32[800,128]{1,0:T(8,128)} %get-tuple-element.94), channel_id=1, source_target_pairs={{0,4},{4,0},{8,12},{12,8},{16,20},{20,16},{24,28},{28,24},{1,5},{5... | collective-permute-start | bytes 1228808 | tf_op jit(solution)/shard_map/ppermute | solution.py:404
  56.1 1.6 collective-permute-done.3.got_ref
  58.5 2.6 %cut_sums.2 = (f32[200,128]{1,0:T(8,128)}, f32[200,128]{1,0:T(8,128)}, f32[200,128]{1,0:T(8,128)}, f32[200,128]{1,0:T(8,128)}) custom-call(s32[5]{0:T(128)} %copy-done.11, f32[800,128]{1,0:T(8,128)} %get-tuple-element.93.mine_ref, f32[800,128]{1,0:T(8,128)} %copy-done.21), custom_call_target="tpu_custom_call" | custom-call | flops 102400 | bytes 1228800 | tf_op jit(solution)/shard_map/cut_sums/pallas_call | solution.py:410
  61.1 1.3 collective-permute-start.4
  62.4 2.3 %collective-permute-start.5 = (f32[200,128]{1,0:T(8,128)}, f32[200,128]{1,0:T(8,128)S(1)}, u32[]{:S(2)}, u32[]{:S(2)}) collective-permute-start(f32[200,128]{1,0:T(8,128)} %get-tuple-element.97), channel_id=1, source_target_pairs={{0,16},{4,20},{8,24},{12,28},{16,0},{20,4},{24,8},{28,12},{1,17},{... | collective-permute-start | bytes 307208 | tf_op jit(solution)/shard_map/ppermute | solution.py:404
  65.4 1.2 collective-permute-start.9
  67.0 4.9 %collective-permute-done.6 = f32[200,128]{1,0:T(8,128)S(1)} collective-permute-done((f32[200,128]{1,0:T(8,128)}, f32[200,128]{1,0:T(8,128)S(1)}, u32[]{:S(2)}, u32[]{:S(2)}) %collective-permute-start.6) | collective-permute-done | bytes 102432 | tf_op jit(solution)/shard_map/ppermute | solution.py:404
  72.8 2.6 %collective-permute-start.10 = (f32[200,128]{1,0:T(8,128)S(1)}, f32[200,128]{1,0:T(8,128)S(1)}, u32[]{:S(2)}, u32[]{:S(2)}) collective-permute-start(f32[200,128]{1,0:T(8,128)S(1)} %add_add_fusion.1), channel_id=1, source_target_pairs={{0,8},{4,12},{8,0},{12,4},{16,24},{20,28},{24,16},{28,20},{1,9},{5... | collective-permute-start | bytes 307208 | tf_op jit(solution)/shard_map/ppermute | solution.py:404
  75.5 1.0 collective-permute-start.11
  76.5 1.2 collective-permute-start.12
  77.9 3.6 %collective-permute-done.11 = f32[200,128]{1,0:T(8,128)S(1)} collective-permute-done((f32[200,128]{1,0:T(8,128)S(1)}, f32[200,128]{1,0:T(8,128)S(1)}, u32[]{:S(2)}, u32[]{:S(2)}) %collective-permute-start.11) | collective-permute-done | bytes 102432 | tf_op jit(solution)/shard_map/ppermute | solution.py:404
  81.6 1.6 collective-permute-done.12
  83.2 4.0 %collective-permute-start.13 = (f32[800,128]{1,0:T(8,128)S(1)}, f32[800,128]{1,0:T(8,128)}, u32[]{:S(2)}, u32[]{:S(2)}) collective-permute-start(f32[800,128]{1,0:T(8,128)S(1)} %constant_dynamic-update-slice_fusion.refs_12_), channel_id=1, source_target_pairs={{0,4},{4,0},{8,12},{12,8},{16,20},{20,16},{24,28},{28,24},{1,5},{5... | collective-permute-start | bytes 1228808 | tf_op jit(solution)/shard_map/ppermute | solution.py:404
  88.8 11.6 %query_low_rank.1 = (f32[768,512]{1,0:T(8,128)}, f32[768,512]{1,0:T(8,128)}, f32[800,128]{1,0:T(8,128)}, f32[800,128]{1,0:T(8,128)}) custom-call(s32[5]{0:T(128)} %copy-done.11, f32[128,3072]{1,0:T(8,128)} %refs_0_.7, f32[1544,128]{1,0:T(8,128)} %copy-done.15, f32[1544,128]{1,0:T(8,128)} %copy-done.16, ...), custom_call_target="tpu_custom_call" | custom-call | flops 2818572288 | bytes 7929856 | tf_op jit(solution)/shard_map/query_low_rank/pallas_call | solution.py:383
  100.8 3.3 %collective-permute-start.18 = (f32[768,128]{1,0:T(8,128)}, f32[768,128]{1,0:T(8,128)S(1)}, u32[]{:S(2)}, u32[]{:S(2)}) collective-permute-start(f32[768,128]{1,0:T(8,128)} %get-tuple-element.121), channel_id=1, source_target_pairs={{0,4},{4,8},{8,12},{12,16},{16,20},{20,24},{24,28},{1,5},{5,9},{9,... | collective-permute-start | bytes 1179656 | tf_op jit(solution)/shard_map/ppermute | solution.py:445
  104.1 2.1 collective-permute-start.19
  107.0 2.6 %cut_sums.3 = (f32[200,128]{1,0:T(8,128)}, f32[200,128]{1,0:T(8,128)}, f32[200,128]{1,0:T(8,128)}, f32[200,128]{1,0:T(8,128)}) custom-call(s32[5]{0:T(128)} %copy-done.11, f32[800,128]{1,0:T(8,128)} %get-tuple-element.107.mine_ref, f32[800,128]{1,0:T(8,128)} %copy-done.20), custom_call_target="tpu_custom_call" | custom-call | flops 102400 | bytes 1228800 | tf_op jit(solution)/shard_map/cut_sums/pallas_call | solution.py:410
  109.6 1.0 collective-permute-start.15
  110.8 2.3 %collective-permute-start.17 = (f32[200,128]{1,0:T(8,128)}, f32[200,128]{1,0:T(8,128)S(1)}, u32[]{:S(2)}, u32[]{:S(2)}) collective-permute-start(f32[200,128]{1,0:T(8,128)} %get-tuple-element.118), channel_id=1, source_target_pairs={{0,24},{4,28},{8,16},{12,20},{16,8},{20,12},{24,0},{28,4},{1,25},{... | collective-permute-start | bytes 307208 | tf_op jit(solution)/shard_map/ppermute | solution.py:404
  114.9 12.7 %sparse.2 = (f32[776,128]{1,0:T(8,128)}, f32[776,128]{1,0:T(8,128)}, f32[776,128]{1,0:T(8,128)}, f32[776,128]{1,0:T(8,128)}, f32[1536,128]{1,0:T(8,128)}, /*inde...) custom-call(s32[5]{0:T(128)} %copy-done.11, f32[128,3072]{1,0:T(8,128)} %refs_0_.7, f32[1544,128]{1,0:T(8,128)} %copy-done.15, ...), custom_call_target="tpu_custom_call" | custom-call | flops 5284823040 | bytes 7110656 | tf_op jit(solution)/shard_map/sparse/pallas_call | solution.py:383
  128.2 3.1 %collective-permute-start.25 = (f32[200,128]{1,0:T(8,128)S(1)}, f32[200,128]{1,0:T(8,128)S(1)}, u32[]{:S(2)}, u32[]{:S(2)}) collective-permute-start(f32[200,128]{1,0:T(8,128)S(1)} %add_add_fusion), channel_id=1, source_target_pairs={{0,24},{4,28},{8,16},{12,20},{16,8},{20,12},{24,0},{28,4},{1,25},{... | collective-permute-start | bytes 307208 | tf_op jit(solution)/shard_map/ppermute | solution.py:404
  131.4 1.2 collective-permute-start.20
  132.8 12.6 %sparse.3 = (f32[776,128]{1,0:T(8,128)}, f32[776,128]{1,0:T(8,128)}, f32[776,128]{1,0:T(8,128)}, f32[776,128]{1,0:T(8,128)}, f32[1536,128]{1,0:T(8,128)}, /*inde...) custom-call(s32[5]{0:T(128)} %copy-done.11, f32[128,3072]{1,0:T(8,128)} %refs_0_.7, f32[1544,128]{1,0:T(8,128)} %copy-done.15, ...), custom_call_target="tpu_custom_call" | custom-call | flops 5284823040 | bytes 7110656 | tf_op jit(solution)/shard_map/sparse/pallas_call | solution.py:383
  145.4 1.3 collective-permute-start.22
  146.7 3.5 %collective-permute-start.35 = (f32[384,128]{1,0:T(8,128)}, f32[384,128]{1,0:T(8,128)S(1)}, u32[]{:S(2)}, u32[]{:S(2)}) collective-permute-start(f32[384,128]{1,0:T(8,128)} %get-tuple-element.155), channel_id=1, source_target_pairs={{0,4},{4,8},{8,12},{12,16},{16,20},{20,24},{24,28},{1,5},{5,9},{9,... | collective-permute-start | bytes 589832 | tf_op jit(solution)/shard_map/ppermute | solution.py:445
  150.3 1.9 collective-permute-start.36
  153.0 1.3 collective-permute-start.26
  154.3 3.9 %collective-permute-start.30 = (f32[384,128]{1,0:T(8,128)S(1)}, f32[384,128]{1,0:T(8,128)S(1)}, u32[]{:S(2)}, u32[]{:S(2)}) collective-permute-start(f32[384,128]{1,0:T(8,128)S(1)} %copy-done.33), channel_id=1, source_target_pairs={{0,4},{4,8},{8,12},{12,16},{16,20},{20,24},{24,28},{1,5},{5,9},{9,... | collective-permute-start | bytes 589832 | tf_op jit(solution)/shard_map/ppermute | solution.py:445
  158.7 1.5 collective-permute-start.28
  160.2 6.8 %key_low_rank.3 = (f32[768,128]{1,0:T(8,128)}, f32[768,128]{1,0:T(8,128)}, f32[768,128]{1,0:T(8,128)}, f32[768,128]{1,0:T(8,128)}) custom-call(s32[5]{0:T(128)} %copy-done.11, f32[3072,128]{1,0:T(8,128)} %get-tuple-element.119.refs_12_.refs_0_, f32[3072,128]{1,0:T(8,128)} %get-tuple-element.120.refs_13_.refs_1_, f32[800,128]{1,0:T(8,128)} %copy-done.17, ...), custom_call_target="tpu_custom_call" | custom-call | flops 1308622848 | bytes 3145728 | tf_op jit(solution)/shard_map/key_low_rank/pallas_call | solution.py:383
  167.9 2.3 %collective-permute-start.31 = (f32[384,128]{1,0:T(8,128)S(1)}, f32[384,128]{1,0:T(8,128)S(1)}, u32[]{:S(2)}, u32[]{:S(2)}) collective-permute-start(f32[384,128]{1,0:T(8,128)S(1)} %copy-done.32), channel_id=1, source_target_pairs={{4,0},{8,4},{12,8},{16,12},{20,16},{24,20},{28,24},{5,1},{9,5},{13... | collective-permute-start | bytes 589832 | tf_op jit(solution)/shard_map/ppermute | solution.py:450
  170.3 4.9 %collective-permute-done.31.refs_7_ = f32[384,128]{1,0:T(8,128)S(1)} collective-permute-done((f32[384,128]{1,0:T(8,128)S(1)}, f32[384,128]{1,0:T(8,128)S(1)}, u32[]{:S(2)}, u32[]{:S(2)}) %collective-permute-start.31) | collective-permute-done | bytes 196640 | tf_op jit(solution)/shard_map/ppermute | solution.py:450
  176.1 6.9 %key_low_rank.2 = (f32[768,128]{1,0:T(8,128)}, f32[768,128]{1,0:T(8,128)}, f32[768,128]{1,0:T(8,128)}, f32[768,128]{1,0:T(8,128)}) custom-call(s32[5]{0:T(128)} %copy-done.11, f32[3072,128]{1,0:T(8,128)} %get-tuple-element.119.refs_12_.refs_0_, f32[3072,128]{1,0:T(8,128)} %get-tuple-element.120.refs_13_.refs_1_, f32[800,128]{1,0:T(8,128)} %copy-done.17, ...), custom_call_target="tpu_custom_call" | custom-call | flops 1308622848 | bytes 3145728 | tf_op jit(solution)/shard_map/key_low_rank/pallas_call | solution.py:383
  187.1 3.1 %unpack_od.1 = (f32[128,3072]{1,0:T(8,128)}, f32[128,3072]{1,0:T(8,128)}) custom-call(s32[5]{0:T(128)S(1)} %copy-done.12, f32[776,128]{1,0:T(8,128)S(1)} %copy-done.4, f32[776,128]{1,0:T(8,128)S(1)} %collective-permute-done.20.refs_2_, f32[776,128]{1,0:T(8,128)S(1)} %collective-permute-done.21.refs_3_, f32[776,128]{1,0:T(8,128)S(1)} %collective-permute-done.22.refs_4_, ...), custom_call_target="tpu_custom_call" | custom-call | bytes 6291456 | tf_op jit(solution)/shard_map/unpack_od/pallas_call | solution.py:140
  190.2 5.0 %collective-permute-done.38.refs_7_ = f32[768,128]{1,0:T(8,128)} collective-permute-done((f32[768,128]{1,0:T(8,128)}, f32[768,128]{1,0:T(8,128)}, u32[]{:S(2)}, u32[]{:S(2)}) %collective-permute-start.38) | collective-permute-done | bytes 393248 | tf_op jit(solution)/shard_map/ppermute | solution.py:404
  195.2 3.3 %collective-permute-done.32.refs_2_ = f32[768,128]{1,0:T(8,128)} collective-permute-done((f32[768,128]{1,0:T(8,128)}, f32[768,128]{1,0:T(8,128)}, u32[]{:S(2)}, u32[]{:S(2)}) %collective-permute-start.32) | collective-permute-done | bytes 393248 | tf_op jit(solution)/shard_map/ppermute | solution.py:404
  198.5 12.2 %collective-permute-done.33.refs_3_ = f32[768,128]{1,0:T(8,128)} collective-permute-done((f32[768,128]{1,0:T(8,128)}, f32[768,128]{1,0:T(8,128)}, u32[]{:S(2)}, u32[]{:S(2)}) %collective-permute-start.33) | collective-permute-done | bytes 393248 | tf_op jit(solution)/shard_map/ppermute | solution.py:404
  210.7 4.2 %unpack_kv.1 = (f32[128,3072]{1,0:T(8,128)}, f32[128,3072]{1,0:T(8,128)}) custom-call(s32[5]{0:T(128)S(1)} %copy-done.12, f32[768,128]{1,0:T(8,128)S(1)} %copy-done.9, f32[768,128]{1,0:T(8,128)} %collective-permute-done.32.refs_2_, f32[768,128]{1,0:T(8,128)} %collective-permute-done.33.refs_3_, f32[768,128]{1,0:T(8,128)} %collective-permute-done.34.refs_4_, ...), custom_call_target="tpu_custom_call" | custom-call | bytes 6291456 | tf_op jit(solution)/shard_map/unpack_kv/pallas_call | solution.py:140
  (148 shorter events, 19.7 us)
Async XLA Ops:
  6.3 19.7 %collective-permute-start = (f32[1536,128]{1,0:T(8,128)}, f32[1536,128]{1,0:T(8,128)}, u32[]{:S(2)}, u32[]{:S(2)}) collective-permute-start(f32[1536,128]{1,0:T(8,128)} %get-tuple-element.84), channel_id=1, source_target_pairs={{0,1},{1,0},{2,3},{3,2},{4,5},{5,4},{6,7},{7,6},{8,9},{9,8},{10,11... | collective-permute-start | bytes 2359304 | tf_op jit(solution)/shard_map/ppermute | solution.py:404
  8.4 18.4 %collective-permute-start.1 = (f32[1536,128]{1,0:T(8,128)}, f32[1536,128]{1,0:T(8,128)}, u32[]{:S(2)}, u32[]{:S(2)}) collective-permute-start(f32[1536,128]{1,0:T(8,128)} %get-tuple-element.85), channel_id=1, source_target_pairs={{0,2},{1,3},{2,0},{3,1},{4,6},{5,7},{6,4},{7,5},{8,10},{9,11},{10,... | collective-permute-start | bytes 2359304 | tf_op jit(solution)/shard_map/ppermute | solution.py:404
  9.6 34.1 %collective-permute-start.2 = (f32[1536,128]{1,0:T(8,128)}, f32[1536,128]{1,0:T(8,128)}, u32[]{:S(2)}, u32[]{:S(2)}) collective-permute-start(f32[1536,128]{1,0:T(8,128)} %get-tuple-element.86), channel_id=1, source_target_pairs={{0,3},{1,2},{2,1},{3,0},{4,7},{5,6},{6,5},{7,4},{8,11},{9,10},{10,... | collective-permute-start | bytes 2359304 | tf_op jit(solution)/shard_map/ppermute | solution.py:404
  43.8 21.6 %copy-start.14 = (f32[1544,128]{1,0:T(8,128)S(1)}, f32[1544,128]{1,0:T(8,128)}, u32[]{:S(2)}) copy-start(f32[1544,128]{1,0:T(8,128)} %copy-done.13) | copy-start | bytes 2371588
  43.8 29.0 %collective-permute-start.7 = (f32[1544,128]{1,0:T(8,128)}, f32[1544,128]{1,0:T(8,128)S(1)}, u32[]{:S(2)}, u32[]{:S(2)}) collective-permute-start(f32[1544,128]{1,0:T(8,128)} %get-tuple-element.99), channel_id=1, source_target_pairs={{0,1},{1,0},{2,3},{3,2},{4,5},{5,4},{6,7},{7,6},{8,9},{9,8},{10,11... | collective-permute-start | bytes 2371592 | tf_op jit(solution)/shard_map/ppermute | solution.py:404
  44.9 27.9 %collective-permute-start.8 = (f32[1544,128]{1,0:T(8,128)}, f32[1544,128]{1,0:T(8,128)S(1)}, u32[]{:S(2)}, u32[]{:S(2)}) collective-permute-start(f32[1544,128]{1,0:T(8,128)} %get-tuple-element.100), channel_id=1, source_target_pairs={{0,2},{1,3},{2,0},{3,1},{4,6},{5,7},{6,4},{7,5},{8,10},{9,11},{10,... | collective-permute-start | bytes 2371592 | tf_op jit(solution)/shard_map/ppermute | solution.py:404
  53.7 4.0 %collective-permute-start.3 = (f32[800,128]{1,0:T(8,128)}, f32[800,128]{1,0:T(8,128)S(1)}, u32[]{:S(2)}, u32[]{:S(2)}) collective-permute-start(f32[800,128]{1,0:T(8,128)} %get-tuple-element.94), channel_id=1, source_target_pairs={{0,4},{4,0},{8,12},{12,8},{16,20},{20,16},{24,28},{28,24},{1,5},{5... | collective-permute-start | bytes 1228808 | tf_op jit(solution)/shard_map/ppermute | solution.py:404
  61.1 4.3 %collective-permute-start.4 = (f32[200,128]{1,0:T(8,128)}, f32[200,128]{1,0:T(8,128)S(1)}, u32[]{:S(2)}, u32[]{:S(2)}) collective-permute-start(f32[200,128]{1,0:T(8,128)} %get-tuple-element.96), channel_id=1, source_target_pairs={{0,8},{4,12},{8,0},{12,4},{16,24},{20,28},{24,16},{28,20},{1,9},{5... | collective-permute-start | bytes 307208 | tf_op jit(solution)/shard_map/ppermute | solution.py:404
  62.4 4.6 %collective-permute-start.5 = (f32[200,128]{1,0:T(8,128)}, f32[200,128]{1,0:T(8,128)S(1)}, u32[]{:S(2)}, u32[]{:S(2)}) collective-permute-start(f32[200,128]{1,0:T(8,128)} %get-tuple-element.97), channel_id=1, source_target_pairs={{0,16},{4,20},{8,24},{12,28},{16,0},{20,4},{24,8},{28,12},{1,17},{... | collective-permute-start | bytes 307208 | tf_op jit(solution)/shard_map/ppermute | solution.py:404
  64.7 7.2 %collective-permute-start.6 = (f32[200,128]{1,0:T(8,128)}, f32[200,128]{1,0:T(8,128)S(1)}, u32[]{:S(2)}, u32[]{:S(2)}) collective-permute-start(f32[200,128]{1,0:T(8,128)} %get-tuple-element.98), channel_id=1, source_target_pairs={{0,24},{4,28},{8,16},{12,20},{16,8},{20,12},{24,0},{28,4},{1,25},{... | collective-permute-start | bytes 307208 | tf_op jit(solution)/shard_map/ppermute | solution.py:404
  65.4 22.6 %collective-permute-start.9 = (f32[1544,128]{1,0:T(8,128)S(1)}, f32[1544,128]{1,0:T(8,128)}, u32[]{:S(2)}, u32[]{:S(2)}) collective-permute-start(f32[1544,128]{1,0:T(8,128)S(1)} %copy-done.14), channel_id=1, source_target_pairs={{0,3},{1,2},{2,1},{3,0},{4,7},{5,6},{6,5},{7,4},{8,11},{9,10},{10,... | collective-permute-start | bytes 2371592 | tf_op jit(solution)/shard_map/ppermute | solution.py:404
  72.8 5.1 %collective-permute-start.10 = (f32[200,128]{1,0:T(8,128)S(1)}, f32[200,128]{1,0:T(8,128)S(1)}, u32[]{:S(2)}, u32[]{:S(2)}) collective-permute-start(f32[200,128]{1,0:T(8,128)S(1)} %add_add_fusion.1), channel_id=1, source_target_pairs={{0,8},{4,12},{8,0},{12,4},{16,24},{20,28},{24,16},{28,20},{1,9},{5... | collective-permute-start | bytes 307208 | tf_op jit(solution)/shard_map/ppermute | solution.py:404
  75.5 6.1 %collective-permute-start.11 = (f32[200,128]{1,0:T(8,128)S(1)}, f32[200,128]{1,0:T(8,128)S(1)}, u32[]{:S(2)}, u32[]{:S(2)}) collective-permute-start(f32[200,128]{1,0:T(8,128)S(1)} %add_add_fusion.1), channel_id=1, source_target_pairs={{0,16},{4,20},{8,24},{12,28},{16,0},{20,4},{24,8},{28,12},{1,17},{... | collective-permute-start | bytes 307208 | tf_op jit(solution)/shard_map/ppermute | solution.py:404
  76.5 6.7 %collective-permute-start.12 = (f32[200,128]{1,0:T(8,128)S(1)}, f32[200,128]{1,0:T(8,128)S(1)}, u32[]{:S(2)}, u32[]{:S(2)}) collective-permute-start(f32[200,128]{1,0:T(8,128)S(1)} %add_add_fusion.1), channel_id=1, source_target_pairs={{0,24},{4,28},{8,16},{12,20},{16,8},{20,12},{24,0},{28,4},{1,25},{... | collective-permute-start | bytes 307208 | tf_op jit(solution)/shard_map/ppermute | solution.py:404
  83.2 5.5 %collective-permute-start.13 = (f32[800,128]{1,0:T(8,128)S(1)}, f32[800,128]{1,0:T(8,128)}, u32[]{:S(2)}, u32[]{:S(2)}) collective-permute-start(f32[800,128]{1,0:T(8,128)S(1)} %constant_dynamic-update-slice_fusion.refs_12_), channel_id=1, source_target_pairs={{0,4},{4,0},{8,12},{12,8},{16,20},{20,16},{24,28},{28,24},{1,5},{5... | collective-permute-start | bytes 1228808 | tf_op jit(solution)/shard_map/ppermute | solution.py:404
  88.0 16.1 %copy-start.29 = (f32[768,128]{1,0:T(8,128)S(1)}, f32[768,128]{1,0:T(8,128)}, u32[]{:S(2)}) copy-start(f32[768,128]{1,0:T(8,128)} %get-tuple-element.122) | copy-start | bytes 1179652
  100.3 5.9 %collective-permute-start.14 = (f32[800,128]{1,0:T(8,128)}, f32[800,128]{1,0:T(8,128)S(1)}, u32[]{:S(2)}, u32[]{:S(2)}) collective-permute-start(f32[800,128]{1,0:T(8,128)} %get-tuple-element.108), channel_id=1, source_target_pairs={{0,4},{4,0},{8,12},{12,8},{16,20},{20,16},{24,28},{28,24},{1,5},{5... | collective-permute-start | bytes 1228808 | tf_op jit(solution)/shard_map/ppermute | solution.py:404
  100.8 12.4 %collective-permute-start.18 = (f32[768,128]{1,0:T(8,128)}, f32[768,128]{1,0:T(8,128)S(1)}, u32[]{:S(2)}, u32[]{:S(2)}) collective-permute-start(f32[768,128]{1,0:T(8,128)} %get-tuple-element.121), channel_id=1, source_target_pairs={{0,4},{4,8},{8,12},{12,16},{16,20},{20,24},{24,28},{1,5},{5,9},{9,... | collective-permute-start | bytes 1179656 | tf_op jit(solution)/shard_map/ppermute | solution.py:445
  104.1 10.0 %collective-permute-start.19 = (f32[768,128]{1,0:T(8,128)S(1)}, f32[768,128]{1,0:T(8,128)S(1)}, u32[]{:S(2)}, u32[]{:S(2)}) collective-permute-start(f32[768,128]{1,0:T(8,128)S(1)} %copy-done.29), channel_id=1, source_target_pairs={{4,0},{8,4},{12,8},{16,12},{20,16},{24,20},{28,24},{5,1},{9,5},{13... | collective-permute-start | bytes 1179656 | tf_op jit(solution)/shard_map/ppermute | solution.py:450
  109.6 18.0 %collective-permute-start.15 = (f32[200,128]{1,0:T(8,128)}, f32[200,128]{1,0:T(8,128)S(1)}, u32[]{:S(2)}, u32[]{:S(2)}) collective-permute-start(f32[200,128]{1,0:T(8,128)} %get-tuple-element.116), channel_id=1, source_target_pairs={{0,8},{4,12},{8,0},{12,4},{16,24},{20,28},{24,16},{28,20},{1,9},{5... | collective-permute-start | bytes 307208 | tf_op jit(solution)/shard_map/ppermute | solution.py:404
  110.6 17.0 %collective-permute-start.16 = (f32[200,128]{1,0:T(8,128)}, f32[200,128]{1,0:T(8,128)S(1)}, u32[]{:S(2)}, u32[]{:S(2)}) collective-permute-start(f32[200,128]{1,0:T(8,128)} %get-tuple-element.117), channel_id=1, source_target_pairs={{0,16},{4,20},{8,24},{12,28},{16,0},{20,4},{24,8},{28,12},{1,17},{... | collective-permute-start | bytes 307208 | tf_op jit(solution)/shard_map/ppermute | solution.py:404
  110.8 16.8 %collective-permute-start.17 = (f32[200,128]{1,0:T(8,128)}, f32[200,128]{1,0:T(8,128)S(1)}, u32[]{:S(2)}, u32[]{:S(2)}) collective-permute-start(f32[200,128]{1,0:T(8,128)} %get-tuple-element.118), channel_id=1, source_target_pairs={{0,24},{4,28},{8,16},{12,20},{16,8},{20,12},{24,0},{28,4},{1,25},{... | collective-permute-start | bytes 307208 | tf_op jit(solution)/shard_map/ppermute | solution.py:404
  127.7 17.7 %copy-start.4 = (f32[776,128]{1,0:T(8,128)S(1)}, f32[776,128]{1,0:T(8,128)}, u32[]{:S(2)}) copy-start(f32[776,128]{1,0:T(8,128)} %get-tuple-element.127.refs_1_) | copy-start | bytes 1191940
  127.7 17.7 %copy-start.28 = (f32[776,128]{1,0:T(8,128)S(1)}, f32[776,128]{1,0:T(8,128)}, u32[]{:S(2)}) copy-start(f32[776,128]{1,0:T(8,128)} %get-tuple-element.130) | copy-start | bytes 1191940
  127.7 26.5 %copy-start.33 = (f32[384,128]{1,0:T(8,128)S(1)}, f32[384,128]{1,0:T(8,128)}, u32[]{:S(2)}) copy-start(f32[384,128]{1,0:T(8,128)} %get-tuple-element.147) | copy-start | bytes 589828
  127.7 17.7 %collective-permute-start.23 = (f32[200,128]{1,0:T(8,128)S(1)}, f32[200,128]{1,0:T(8,128)S(1)}, u32[]{:S(2)}, u32[]{:S(2)}) collective-permute-start(f32[200,128]{1,0:T(8,128)S(1)} %add_add_fusion), channel_id=1, source_target_pairs={{0,8},{4,12},{8,0},{12,4},{16,24},{20,28},{24,16},{28,20},{1,9},{5... | collective-permute-start | bytes 307208 | tf_op jit(solution)/shard_map/ppermute | solution.py:404
  127.9 18.8 %collective-permute-start.24 = (f32[200,128]{1,0:T(8,128)S(1)}, f32[200,128]{1,0:T(8,128)S(1)}, u32[]{:S(2)}, u32[]{:S(2)}) collective-permute-start(f32[200,128]{1,0:T(8,128)S(1)} %add_add_fusion), channel_id=1, source_target_pairs={{0,16},{4,20},{8,24},{12,28},{16,0},{20,4},{24,8},{28,12},{1,17},{... | collective-permute-start | bytes 307208 | tf_op jit(solution)/shard_map/ppermute | solution.py:404
  128.2 22.1 %collective-permute-start.25 = (f32[200,128]{1,0:T(8,128)S(1)}, f32[200,128]{1,0:T(8,128)S(1)}, u32[]{:S(2)}, u32[]{:S(2)}) collective-permute-start(f32[200,128]{1,0:T(8,128)S(1)} %add_add_fusion), channel_id=1, source_target_pairs={{0,24},{4,28},{8,16},{12,20},{16,8},{20,12},{24,0},{28,4},{1,25},{... | collective-permute-start | bytes 307208 | tf_op jit(solution)/shard_map/ppermute | solution.py:404
  131.4 21.6 %collective-permute-start.20 = (f32[776,128]{1,0:T(8,128)}, f32[776,128]{1,0:T(8,128)S(1)}, u32[]{:S(2)}, u32[]{:S(2)}) collective-permute-start(f32[776,128]{1,0:T(8,128)} %get-tuple-element.128), channel_id=1, source_target_pairs={{0,1},{1,0},{2,3},{3,2},{4,5},{5,4},{6,7},{7,6},{8,9},{9,8},{10,11... | collective-permute-start | bytes 1191944 | tf_op jit(solution)/shard_map/ppermute | solution.py:404
  132.6 20.4 %collective-permute-start.21 = (f32[776,128]{1,0:T(8,128)}, f32[776,128]{1,0:T(8,128)S(1)}, u32[]{:S(2)}, u32[]{:S(2)}) collective-permute-start(f32[776,128]{1,0:T(8,128)} %get-tuple-element.129), channel_id=1, source_target_pairs={{0,2},{1,3},{2,0},{3,1},{4,6},{5,7},{6,4},{7,5},{8,10},{9,11},{10,... | collective-permute-start | bytes 1191944 | tf_op jit(solution)/shard_map/ppermute | solution.py:404
  145.4 21.6 %collective-permute-start.22 = (f32[776,128]{1,0:T(8,128)S(1)}, f32[776,128]{1,0:T(8,128)S(1)}, u32[]{:S(2)}, u32[]{:S(2)}) collective-permute-start(f32[776,128]{1,0:T(8,128)S(1)} %copy-done.28), channel_id=1, source_target_pairs={{0,3},{1,2},{2,1},{3,0},{4,7},{5,6},{6,5},{7,4},{8,11},{9,10},{10,... | collective-permute-start | bytes 1191944 | tf_op jit(solution)/shard_map/ppermute | solution.py:404
  146.7 7.5 %collective-permute-start.35 = (f32[384,128]{1,0:T(8,128)}, f32[384,128]{1,0:T(8,128)S(1)}, u32[]{:S(2)}, u32[]{:S(2)}) collective-permute-start(f32[384,128]{1,0:T(8,128)} %get-tuple-element.155), channel_id=1, source_target_pairs={{0,4},{4,8},{8,12},{12,16},{16,20},{20,24},{24,28},{1,5},{5,9},{9,... | collective-permute-start | bytes 589832 | tf_op jit(solution)/shard_map/ppermute | solution.py:445
  150.3 7.9 %collective-permute-start.36 = (f32[384,128]{1,0:T(8,128)}, f32[384,128]{1,0:T(8,128)S(1)}, u32[]{:S(2)}, u32[]{:S(2)}) collective-permute-start(f32[384,128]{1,0:T(8,128)} %get-tuple-element.156), channel_id=1, source_target_pairs={{4,0},{8,4},{12,8},{16,12},{20,16},{24,20},{28,24},{5,1},{9,5},{13... | collective-permute-start | bytes 589832 | tf_op jit(solution)/shard_map/ppermute | solution.py:450
  153.0 5.7 %collective-permute-start.29 = (f32[800,128]{1,0:T(8,128)S(1)}, f32[800,128]{1,0:T(8,128)S(1)}, u32[]{:S(2)}, u32[]{:S(2)}) collective-permute-start(f32[800,128]{1,0:T(8,128)S(1)} %pad_maximum_fusion.refs_2_), channel_id=1, source_target_pairs={{0,4},{4,0},{8,12},{12,8},{16,20},{20,16},{24,28},{28,24},{1,5},{5... | collective-permute-start | bytes 1228808 | tf_op jit(solution)/shard_map/ppermute | solution.py:404
  153.0 14.9 %collective-permute-start.26 = (f32[776,128]{1,0:T(8,128)}, f32[776,128]{1,0:T(8,128)S(1)}, u32[]{:S(2)}, u32[]{:S(2)}) collective-permute-start(f32[776,128]{1,0:T(8,128)} %get-tuple-element.139), channel_id=1, source_target_pairs={{0,1},{1,0},{2,3},{3,2},{4,5},{5,4},{6,7},{7,6},{8,9},{9,8},{10,11... | collective-permute-start | bytes 1191944 | tf_op jit(solution)/shard_map/ppermute | solution.py:404
  154.3 15.9 %collective-permute-start.30 = (f32[384,128]{1,0:T(8,128)S(1)}, f32[384,128]{1,0:T(8,128)S(1)}, u32[]{:S(2)}, u32[]{:S(2)}) collective-permute-start(f32[384,128]{1,0:T(8,128)S(1)} %copy-done.33), channel_id=1, source_target_pairs={{0,4},{4,8},{8,12},{12,16},{16,20},{20,24},{24,28},{1,5},{5,9},{9,... | collective-permute-start | bytes 589832 | tf_op jit(solution)/shard_map/ppermute | solution.py:445
  158.2 24.7 %collective-permute-start.27 = (f32[776,128]{1,0:T(8,128)}, f32[776,128]{1,0:T(8,128)S(1)}, u32[]{:S(2)}, u32[]{:S(2)}) collective-permute-start(f32[776,128]{1,0:T(8,128)} %get-tuple-element.140), channel_id=1, source_target_pairs={{0,2},{1,3},{2,0},{3,1},{4,6},{5,7},{6,4},{7,5},{8,10},{9,11},{10,... | collective-permute-start | bytes 1191944 | tf_op jit(solution)/shard_map/ppermute | solution.py:404
  158.7 25.1 %collective-permute-start.28 = (f32[776,128]{1,0:T(8,128)}, f32[776,128]{1,0:T(8,128)S(1)}, u32[]{:S(2)}, u32[]{:S(2)}) collective-permute-start(f32[776,128]{1,0:T(8,128)} %get-tuple-element.141), channel_id=1, source_target_pairs={{0,3},{1,2},{2,1},{3,0},{4,7},{5,6},{6,5},{7,4},{8,11},{9,10},{10,... | collective-permute-start | bytes 1191944 | tf_op jit(solution)/shard_map/ppermute | solution.py:404
  167.0 17.7 %collective-permute-start.37 = (f32[768,128]{1,0:T(8,128)}, f32[768,128]{1,0:T(8,128)S(1)}, u32[]{:S(2)}, u32[]{:S(2)}) collective-permute-start(f32[768,128]{1,0:T(8,128)} %get-tuple-element.158), channel_id=1, source_target_pairs={{0,1},{1,0},{2,3},{3,2},{4,5},{5,4},{6,7},{7,6},{8,9},{9,8},{10,11... | collective-permute-start | bytes 1179656 | tf_op jit(solution)/shard_map/ppermute | solution.py:404
  167.9 7.3 %collective-permute-start.31 = (f32[384,128]{1,0:T(8,128)S(1)}, f32[384,128]{1,0:T(8,128)S(1)}, u32[]{:S(2)}, u32[]{:S(2)}) collective-permute-start(f32[384,128]{1,0:T(8,128)S(1)} %copy-done.32), channel_id=1, source_target_pairs={{4,0},{8,4},{12,8},{16,12},{20,16},{24,20},{28,24},{5,1},{9,5},{13... | collective-permute-start | bytes 589832 | tf_op jit(solution)/shard_map/ppermute | solution.py:450
  170.2 25.0 %collective-permute-start.38 = (f32[768,128]{1,0:T(8,128)}, f32[768,128]{1,0:T(8,128)}, u32[]{:S(2)}, u32[]{:S(2)}) collective-permute-start(f32[768,128]{1,0:T(8,128)} %get-tuple-element.159), channel_id=1, source_target_pairs={{0,2},{1,3},{2,0},{3,1},{4,6},{5,7},{6,4},{7,5},{8,10},{9,11},{10,... | collective-permute-start | bytes 1179656 | tf_op jit(solution)/shard_map/ppermute | solution.py:404
  175.2 20.0 %collective-permute-start.39 = (f32[768,128]{1,0:T(8,128)}, f32[768,128]{1,0:T(8,128)}, u32[]{:S(2)}, u32[]{:S(2)}) collective-permute-start(f32[768,128]{1,0:T(8,128)} %get-tuple-element.160), channel_id=1, source_target_pairs={{0,3},{1,2},{2,1},{3,0},{4,7},{5,6},{6,5},{7,4},{8,11},{9,10},{10,... | collective-permute-start | bytes 1179656 | tf_op jit(solution)/shard_map/ppermute | solution.py:404
  182.9 15.6 %collective-permute-start.32 = (f32[768,128]{1,0:T(8,128)}, f32[768,128]{1,0:T(8,128)}, u32[]{:S(2)}, u32[]{:S(2)}) collective-permute-start(f32[768,128]{1,0:T(8,128)} %get-tuple-element.150), channel_id=1, source_target_pairs={{0,1},{1,0},{2,3},{3,2},{4,5},{5,4},{6,7},{7,6},{8,9},{9,8},{10,11... | collective-permute-start | bytes 1179656 | tf_op jit(solution)/shard_map/ppermute | solution.py:404
  183.8 26.9 %collective-permute-start.33 = (f32[768,128]{1,0:T(8,128)}, f32[768,128]{1,0:T(8,128)}, u32[]{:S(2)}, u32[]{:S(2)}) collective-permute-start(f32[768,128]{1,0:T(8,128)} %get-tuple-element.151), channel_id=1, source_target_pairs={{0,2},{1,3},{2,0},{3,1},{4,6},{5,7},{6,4},{7,5},{8,10},{9,11},{10,... | collective-permute-start | bytes 1179656 | tf_op jit(solution)/shard_map/ppermute | solution.py:404
  185.5 25.2 %collective-permute-start.34 = (f32[768,128]{1,0:T(8,128)}, f32[768,128]{1,0:T(8,128)}, u32[]{:S(2)}, u32[]{:S(2)}) collective-permute-start(f32[768,128]{1,0:T(8,128)} %get-tuple-element.152), channel_id=1, source_target_pairs={{0,3},{1,2},{2,1},{3,0},{4,7},{5,6},{6,5},{7,4},{8,11},{9,10},{10,... | collective-permute-start | bytes 1179656 | tf_op jit(solution)/shard_map/ppermute | solution.py:404
  187.0 23.7 %copy-start.6 = (f32[768,128]{1,0:T(8,128)S(1)}, f32[768,128]{1,0:T(8,128)}, u32[]{:S(2)}) copy-start(f32[768,128]{1,0:T(8,128)} %get-tuple-element.157.refs_5_) | copy-start | bytes 1179652
  187.0 23.7 %copy-start.8 = (f32[768,128]{1,0:T(8,128)S(1)}, f32[768,128]{1,0:T(8,128)}, u32[]{:S(2)}) copy-start(f32[768,128]{1,0:T(8,128)} %copy-done.7) | copy-start | bytes 1179652
  187.1 23.7 %copy-start.9 = (f32[768,128]{1,0:T(8,128)S(1)}, f32[768,128]{1,0:T(8,128)}, u32[]{:S(2)}) copy-start(f32[768,128]{1,0:T(8,128)} %get-tuple-element.149.refs_1_) | copy-start | bytes 1179652
  (27 other events, 155.0 us)

commit v4 on v3

--- a/solution.py
+++ b/solution.py
@@ -148,6 +148,46 @@
         ),
         out_shape=out_shapes,
         compiler_params=pltpu.CompilerParams(vmem_limit_bytes=32 * 1024 * 1024),
+        cost_estimate=pl.CostEstimate(flops=0, bytes_accessed=2 * size, transcendentals=0),
+        name=name,
+    )(index, *ins)
+
+
+def tile_kernel(moves_of, n_in, n_out, index, *refs):
+    ins, outs = refs[:n_in], refs[-3 - n_out : -3]
+    tiles, in_sems, out_sems = refs[-3:]
+    moves = moves_of(index, ins, outs)
+    loads, stores = [], []
+    for position, (source, target) in enumerate(moves):
+        tile = tiles.at[position, pl.ds(0, source.shape[0]), :]
+        loads.append(pltpu.make_async_copy(source, tile, in_sems.at[position]))
+        stores.append(pltpu.make_async_copy(tile, target, out_sems.at[position]))
+    for load in loads:
+        load.start()
+    for load, store in zip(loads, stores):
+        load.wait()
+        store.start()
+    for store in stores:
+        store.wait()
+
+
+def tile_copies(moves_of, n_moves, index, ins, out_shapes, name):
+    size = n_moves * 128 * 128 * 4
+    return pl.pallas_call(
+        functools.partial(tile_kernel, moves_of, len(ins), len(out_shapes)),
+        grid_spec=pltpu.PrefetchScalarGridSpec(
+            num_scalar_prefetch=1,
+            grid=(1,),
+            in_specs=[pl.BlockSpec(memory_space=pl.ANY)] * len(ins),
+            out_specs=[pl.BlockSpec(memory_space=pl.ANY)] * len(out_shapes),
+            scratch_shapes=[
+                pltpu.VMEM((n_moves, 128, 128), F32),
+                pltpu.SemaphoreType.DMA((n_moves,)),
+                pltpu.SemaphoreType.DMA((n_moves,)),
+            ],
+        ),
+        out_shape=out_shapes,
+        compiler_params=pltpu.CompilerParams(vmem_limit_bytes=56 * 1024 * 1024),
         cost_estimate=pl.CostEstimate(flops=0, bytes_accessed=2 * size, transcendentals=0),
         name=name,
     )(index, *ins)
@@ -531,7 +571,7 @@
                         )
         return moves
 
-    kv_sent = local_copies(
+    kv_sent = tile_copies(
         functools.partial(packing, extra=False),
         2 * heads * (members - 1),
         index,

time: 216 us -> 215 us (level)
  local copies, waits for them, and re-layouts: 10.1 us -> 6.99 us
  waiting for transfers between devices: 68.3 us -> 70.5 us
    pallas_call x0 -> x1, Pallas kernels: none -> 3.88 us  [tile_copies(): pl.pallas_call(functools.partial(tile_kernel, moves_of, len(ins), len(out...]
    unnamed x74 -> x72, local copies, waits for them, and re-layouts: 7.84 us -> 4.14 us
    pallas_call x4 -> x3, Pallas kernels: 12.5 us -> 9.82 us  [local_copies(): pl.pallas_call(functools.partial(copy_kernel, moves_of, len(ins)), grid_s...]
where the time goes in v4:
time: 215 us; the launch traced here: 214 us
  Pallas kernels  78 us (36%)
  waiting for transfers between devices  70.5 us (33%)
  starting transfers between devices  55 us (26%)
  local copies, waits for them, and re-layouts  6.99 us (3%)
    ppermute x34, waiting for transfers between devices, swap(): lax.ppermute(block, axis, [(i, i ^ distance) for i in range(lax.axis_size...  63.6 us
    pallas_call x6, Pallas kernels, per_head_call(): pl.pallas_call(functools.partial(kernel, dims), grid_spec=pltpu.PrefetchS...  59.1 us
    ppermute x34, starting transfers between devices, swap(): lax.ppermute(block, axis, [(i, i ^ distance) for i in range(lax.axis_size...  39.2 us
    pallas_call x3, Pallas kernels, local_copies(): pl.pallas_call(functools.partial(copy_kernel, moves_of, len(ins)), grid_s...  9.82 us
    ppermute x3, starting transfers between devices, to_next(): return lax.ppermute(block, 'seq', [(i, i + 1) for i in range(count - 1)])  9.18 us
    ppermute x3, waiting for transfers between devices, to_previous(): return lax.ppermute(block, 'seq', [(i + 1, i) for i in range(count - 1)])  6.92 us
    ppermute x3, starting transfers between devices, to_previous(): return lax.ppermute(block, 'seq', [(i + 1, i) for i in range(count - 1)])  6.59 us
    pallas_call x2, Pallas kernels, cut_sums(): pl.pallas_call(cut_kernel, grid_spec=pltpu.PrefetchScalarGridSpec(num_sca...  5.21 us
  transfers between devices with their start and end apart: 40, of which 16 were waited for; matrix products, arithmetic and copies ran while one was open for 2% of the time, Pallas kernels for 27%

profile of v4, /device:TPU:1, one launch (start us, length us, event | category | flops | bytes accessed | tf_op | source)
XLA Modules:
  0.0 214.3 jit_solution(8222962163540834555)
XLA Ops:
  1.3 3.9 %pack_kv.1 = (f32[1536,128]{1,0:T(8,128)}, f32[1536,128]{1,0:T(8,128)}, f32[1536,128]{1,0:T(8,128)}) custom-call(s32[5]{0:T(128)} %stack.31.index.refs_0_, f32[128,3072]{1,0:T(8,128)} %refs_0_.6, f32[128,3072]{1,0:T(8,128)} %refs_4_.4), custom_call_target="tpu_custom_call" | custom-call | bytes 4718592 | tf_op jit(solution)/shard_map/pack_kv/pallas_call | solution.py:176
  5.2 2.1 collective-permute-start
  7.3 1.2 collective-permute-start.1
  9.7 2.5 %pack_qd.1 = (f32[1544,128]{1,0:T(8,128)}, f32[1544,128]{1,0:T(8,128)}, f32[1544,128]{1,0:T(8,128)S(1)}) custom-call(s32[5]{0:T(128)S(1)} %copy-done.9, f32[128,3072]{1,0:T(8,128)S(1)} %copy-done, f32[128,3072]{1,0:T(8,128)S(1)} %copy-done.1, f32[32,128]{1,0:T(8,128)S(1)} %maximum_bitcast_fusion.refs_3_.refs_8_), custom_call_target="tpu_custom_call" | custom-call | bytes 4743168 | tf_op jit(solution)/shard_map/pack_qd/pallas_call | solution.py:140
  13.7 11.2 %collective-permute-done.refs_1_.refs_5_ = f32[1536,128]{1,0:T(8,128)} collective-permute-done((f32[1536,128]{1,0:T(8,128)}, f32[1536,128]{1,0:T(8,128)}, u32[]{:S(2)}, u32[]{:S(2)}) %collective-permute-start) | collective-permute-done | bytes 786464 | tf_op jit(solution)/shard_map/ppermute | solution.py:444
  25.7 17.0 %collective-permute-done.2.refs_3_.refs_7_ = f32[1536,128]{1,0:T(8,128)} collective-permute-done((f32[1536,128]{1,0:T(8,128)}, f32[1536,128]{1,0:T(8,128)}, u32[]{:S(2)}, u32[]{:S(2)}) %collective-permute-start.2) | collective-permute-done | bytes 786464 | tf_op jit(solution)/shard_map/ppermute | solution.py:444
  42.7 1.2 collective-permute-start.7
  44.1 8.5 %key_sums.1 = (f32[3072,128]{1,0:T(8,128)}, f32[3072,128]{1,0:T(8,128)}, f32[800,128]{1,0:T(8,128)}, f32[800,128]{1,0:T(8,128)}, f32[768,128]{1,0:T(8,128)}, /*index=5*/f32[768,128]{1,0:T(8,128)}) custom-call(s32[5]{0:T(128)} %stack.31.index.refs_0_, f32[128,3072]{1,0:T(8,128)} %refs_0_.6, f32[1536,128]{1,0:T(8,128)} %collective-permute-done.refs_1_.refs_5_, ...), custom_call_target="tpu_custom_call" | custom-call | flops 1207959552 | bytes 9502720 | tf_op jit(solution)/shard_map/key_sums/pallas_call | solution.py:423
  52.6 2.4 %collective-permute-start.3 = (f32[800,128]{1,0:T(8,128)}, f32[800,128]{1,0:T(8,128)S(1)}, u32[]{:S(2)}, u32[]{:S(2)}) collective-permute-start(f32[800,128]{1,0:T(8,128)} %get-tuple-element.94), channel_id=1, source_target_pairs={{0,4},{4,0},{8,12},{12,8},{16,20},{20,16},{24,28},{28,24},{1,5},{5... | collective-permute-start | bytes 1228808 | tf_op jit(solution)/shard_map/ppermute | solution.py:444
  55.1 1.6 collective-permute-done.3.got_ref
  57.4 2.6 %cut_sums.2 = (f32[200,128]{1,0:T(8,128)}, f32[200,128]{1,0:T(8,128)}, f32[200,128]{1,0:T(8,128)}, f32[200,128]{1,0:T(8,128)}) custom-call(s32[5]{0:T(128)} %stack.31.index.refs_0_, f32[800,128]{1,0:T(8,128)} %get-tuple-element.93.mine_ref, f32[800,128]{1,0:T(8,128)} %copy-done.19), custom_call_target="tpu_custom_call" | custom-call | flops 102400 | bytes 1228800 | tf_op jit(solution)/shard_map/cut_sums/pallas_call | solution.py:450
  60.0 1.3 collective-permute-start.4
  61.3 2.3 %collective-permute-start.5 = (f32[200,128]{1,0:T(8,128)}, f32[200,128]{1,0:T(8,128)S(1)}, u32[]{:S(2)}, u32[]{:S(2)}) collective-permute-start(f32[200,128]{1,0:T(8,128)} %get-tuple-element.97), channel_id=1, source_target_pairs={{0,16},{4,20},{8,24},{12,28},{16,0},{20,4},{24,8},{28,12},{1,17},{... | collective-permute-start | bytes 307208 | tf_op jit(solution)/shard_map/ppermute | solution.py:444
  64.3 1.1 collective-permute-start.9
  65.9 4.8 %collective-permute-done.6 = f32[200,128]{1,0:T(8,128)S(1)} collective-permute-done((f32[200,128]{1,0:T(8,128)}, f32[200,128]{1,0:T(8,128)S(1)}, u32[]{:S(2)}, u32[]{:S(2)}) %collective-permute-start.6) | collective-permute-done | bytes 102432 | tf_op jit(solution)/shard_map/ppermute | solution.py:444
  71.7 2.6 %collective-permute-start.10 = (f32[200,128]{1,0:T(8,128)S(1)}, f32[200,128]{1,0:T(8,128)S(1)}, u32[]{:S(2)}, u32[]{:S(2)}) collective-permute-start(f32[200,128]{1,0:T(8,128)S(1)} %add_add_fusion.1), channel_id=1, source_target_pairs={{0,8},{4,12},{8,0},{12,4},{16,24},{20,28},{24,16},{28,20},{1,9},{5... | collective-permute-start | bytes 307208 | tf_op jit(solution)/shard_map/ppermute | solution.py:444
  75.4 1.2 collective-permute-start.12
  76.8 3.6 %collective-permute-done.11 = f32[200,128]{1,0:T(8,128)S(1)} collective-permute-done((f32[200,128]{1,0:T(8,128)S(1)}, f32[200,128]{1,0:T(8,128)S(1)}, u32[]{:S(2)}, u32[]{:S(2)}) %collective-permute-start.11) | collective-permute-done | bytes 102432 | tf_op jit(solution)/shard_map/ppermute | solution.py:444
  80.5 1.6 collective-permute-done.12
  82.2 4.0 %collective-permute-start.13 = (f32[800,128]{1,0:T(8,128)S(1)}, f32[800,128]{1,0:T(8,128)}, u32[]{:S(2)}, u32[]{:S(2)}) collective-permute-start(f32[800,128]{1,0:T(8,128)S(1)} %constant_dynamic-update-slice_fusion.refs_12_), channel_id=1, source_target_pairs={{0,4},{4,0},{8,12},{12,8},{16,20},{20,16},{24,28},{28,24},{1,5},{5... | collective-permute-start | bytes 1228808 | tf_op jit(solution)/shard_map/ppermute | solution.py:444
  87.7 11.6 %query_low_rank.1 = (f32[768,512]{1,0:T(8,128)}, f32[768,512]{1,0:T(8,128)}, f32[800,128]{1,0:T(8,128)}, f32[800,128]{1,0:T(8,128)}) custom-call(s32[5]{0:T(128)} %stack.31.index.refs_0_, f32[128,3072]{1,0:T(8,128)} %refs_0_.9, f32[1544,128]{1,0:T(8,128)} %copy-done.13, f32[1544,128]{1,0:T(8,128)} %copy-done.14, ...), custom_call_target="tpu_custom_call" | custom-call | flops 2818572288 | bytes 7929856 | tf_op jit(solution)/shard_map/query_low_rank/pallas_call | solution.py:423
  99.7 3.3 %collective-permute-start.18 = (f32[768,128]{1,0:T(8,128)}, f32[768,128]{1,0:T(8,128)S(1)}, u32[]{:S(2)}, u32[]{:S(2)}) collective-permute-start(f32[768,128]{1,0:T(8,128)} %get-tuple-element.121), channel_id=1, source_target_pairs={{0,4},{4,8},{8,12},{12,16},{16,20},{20,24},{24,28},{1,5},{5,9},{9,... | collective-permute-start | bytes 1179656 | tf_op jit(solution)/shard_map/ppermute | solution.py:485
  103.1 1.9 collective-permute-start.19
  105.8 2.6 %cut_sums.3 = (f32[200,128]{1,0:T(8,128)}, f32[200,128]{1,0:T(8,128)}, f32[200,128]{1,0:T(8,128)}, f32[200,128]{1,0:T(8,128)}) custom-call(s32[5]{0:T(128)} %stack.31.index.refs_0_, f32[800,128]{1,0:T(8,128)} %get-tuple-element.107.mine_ref, f32[800,128]{1,0:T(8,128)} %copy-done.18), custom_call_target="tpu_custom_call" | custom-call | flops 102400 | bytes 1228800 | tf_op jit(solution)/shard_map/cut_sums/pallas_call | solution.py:450
  108.4 1.0 collective-permute-start.15
  109.6 2.3 %collective-permute-start.17 = (f32[200,128]{1,0:T(8,128)}, f32[200,128]{1,0:T(8,128)S(1)}, u32[]{:S(2)}, u32[]{:S(2)}) collective-permute-start(f32[200,128]{1,0:T(8,128)} %get-tuple-element.118), channel_id=1, source_target_pairs={{0,24},{4,28},{8,16},{12,20},{16,8},{20,12},{24,0},{28,4},{1,25},{... | collective-permute-start | bytes 307208 | tf_op jit(solution)/shard_map/ppermute | solution.py:444
  111.9 2.3 %collective-permute-done.19.refs_15_ = f32[768,128]{1,0:T(8,128)S(1)} collective-permute-done((f32[768,128]{1,0:T(8,128)S(1)}, f32[768,128]{1,0:T(8,128)S(1)}, u32[]{:S(2)}, u32[]{:S(2)}) %collective-permute-start.19) | collective-permute-done | bytes 393248 | tf_op jit(solution)/shard_map/ppermute | solution.py:490
  115.0 12.7 %sparse.2 = (f32[776,128]{1,0:T(8,128)}, f32[776,128]{1,0:T(8,128)}, f32[776,128]{1,0:T(8,128)}, f32[776,128]{1,0:T(8,128)}, f32[1536,128]{1,0:T(8,128)}, /*inde...) custom-call(s32[5]{0:T(128)} %stack.31.index.refs_0_, f32[128,3072]{1,0:T(8,128)} %refs_0_.9, ...), custom_call_target="tpu_custom_call" | custom-call | flops 5284823040 | bytes 7110656 | tf_op jit(solution)/shard_map/sparse/pallas_call | solution.py:423
  128.0 3.5 %collective-permute-start.25 = (f32[200,128]{1,0:T(8,128)S(1)}, f32[200,128]{1,0:T(8,128)S(1)}, u32[]{:S(2)}, u32[]{:S(2)}) collective-permute-start(f32[200,128]{1,0:T(8,128)S(1)} %add_add_fusion), channel_id=1, source_target_pairs={{0,24},{4,28},{8,16},{12,20},{16,8},{20,12},{24,0},{28,4},{1,25},{... | collective-permute-start | bytes 307208 | tf_op jit(solution)/shard_map/ppermute | solution.py:444
  131.5 1.2 collective-permute-start.20
  132.9 12.6 %sparse.3 = (f32[776,128]{1,0:T(8,128)}, f32[776,128]{1,0:T(8,128)}, f32[776,128]{1,0:T(8,128)}, f32[776,128]{1,0:T(8,128)}, f32[1536,128]{1,0:T(8,128)}, /*inde...) custom-call(s32[5]{0:T(128)} %stack.31.index.refs_0_, f32[128,3072]{1,0:T(8,128)} %refs_0_.9, ...), custom_call_target="tpu_custom_call" | custom-call | flops 5284823040 | bytes 7110656 | tf_op jit(solution)/shard_map/sparse/pallas_call | solution.py:423
  145.6 1.3 collective-permute-start.22
  146.9 2.2 %collective-permute-start.35 = (f32[384,128]{1,0:T(8,128)}, f32[384,128]{1,0:T(8,128)S(1)}, u32[]{:S(2)}, u32[]{:S(2)}) collective-permute-start(f32[384,128]{1,0:T(8,128)} %get-tuple-element.155), channel_id=1, source_target_pairs={{0,4},{4,8},{8,12},{12,16},{16,20},{20,24},{24,28},{1,5},{5,9},{9,... | collective-permute-start | bytes 589832 | tf_op jit(solution)/shard_map/ppermute | solution.py:485
  149.1 2.3 %collective-permute-start.36 = (f32[384,128]{1,0:T(8,128)}, f32[384,128]{1,0:T(8,128)S(1)}, u32[]{:S(2)}, u32[]{:S(2)}) collective-permute-start(f32[384,128]{1,0:T(8,128)} %get-tuple-element.156), channel_id=1, source_target_pairs={{4,0},{8,4},{12,8},{16,12},{20,16},{24,20},{28,24},{5,1},{9,5},{13... | collective-permute-start | bytes 589832 | tf_op jit(solution)/shard_map/ppermute | solution.py:490
  152.2 1.3 collective-permute-start.26
  153.5 3.7 %collective-permute-start.30 = (f32[384,128]{1,0:T(8,128)S(1)}, f32[384,128]{1,0:T(8,128)S(1)}, u32[]{:S(2)}, u32[]{:S(2)}) collective-permute-start(f32[384,128]{1,0:T(8,128)S(1)} %copy-done.32), channel_id=1, source_target_pairs={{0,4},{4,8},{8,12},{12,16},{16,20},{20,24},{24,28},{1,5},{5,9},{9,... | collective-permute-start | bytes 589832 | tf_op jit(solution)/shard_map/ppermute | solution.py:485
  157.5 1.5 collective-permute-start.28
  159.0 6.8 %key_low_rank.3 = (f32[768,128]{1,0:T(8,128)}, f32[768,128]{1,0:T(8,128)}, f32[768,128]{1,0:T(8,128)}, f32[768,128]{1,0:T(8,128)}) custom-call(s32[5]{0:T(128)} %stack.31.index.refs_0_, f32[3072,128]{1,0:T(8,128)} %get-tuple-element.119.refs_12_.refs_0_, f32[3072,128]{1,0:T(8,128)} %get-tuple-element.120.refs_13_.refs_1_, f32[800,128]{1,0:T(8,128)} %copy-done.15, ...), custom_call_target="tpu_custom_call" | custom-call | flops 1308622848 | bytes 3145728 | tf_op jit(solution)/shard_map/key_low_rank/pallas_call | solution.py:423
  165.8 1.0 collective-permute-start.37
  166.9 2.4 %collective-permute-start.31 = (f32[384,128]{1,0:T(8,128)S(1)}, f32[384,128]{1,0:T(8,128)S(1)}, u32[]{:S(2)}, u32[]{:S(2)}) collective-permute-start(f32[384,128]{1,0:T(8,128)S(1)} %copy-done.31), channel_id=1, source_target_pairs={{4,0},{8,4},{12,8},{16,12},{20,16},{24,20},{28,24},{5,1},{9,5},{13... | collective-permute-start | bytes 589832 | tf_op jit(solution)/shard_map/ppermute | solution.py:490
  169.5 4.6 %collective-permute-done.31.refs_7_ = f32[384,128]{1,0:T(8,128)S(1)} collective-permute-done((f32[384,128]{1,0:T(8,128)S(1)}, f32[384,128]{1,0:T(8,128)S(1)}, u32[]{:S(2)}, u32[]{:S(2)}) %collective-permute-start.31) | collective-permute-done | bytes 196640 | tf_op jit(solution)/shard_map/ppermute | solution.py:490
  175.1 6.9 %key_low_rank.2 = (f32[768,128]{1,0:T(8,128)}, f32[768,128]{1,0:T(8,128)}, f32[768,128]{1,0:T(8,128)}, f32[768,128]{1,0:T(8,128)}) custom-call(s32[5]{0:T(128)} %stack.31.index.refs_0_, f32[3072,128]{1,0:T(8,128)} %get-tuple-element.119.refs_12_.refs_0_, f32[3072,128]{1,0:T(8,128)} %get-tuple-element.120.refs_13_.refs_1_, f32[800,128]{1,0:T(8,128)} %copy-done.15, ...), custom_call_target="tpu_custom_call" | custom-call | flops 1308622848 | bytes 3145728 | tf_op jit(solution)/shard_map/key_low_rank/pallas_call | solution.py:423
  182.5 1.2 collective-permute-start.33
  186.1 3.1 %unpack_od.1 = (f32[128,3072]{1,0:T(8,128)}, f32[128,3072]{1,0:T(8,128)}) custom-call(s32[5]{0:T(128)S(1)} %copy-done.10, f32[776,128]{1,0:T(8,128)S(1)} %copy-done.2, f32[776,128]{1,0:T(8,128)S(1)} %collective-permute-done.20.refs_2_, f32[776,128]{1,0:T(8,128)S(1)} %collective-permute-done.21.refs_3_, f32[776,128]{1,0:T(8,128)S(1)} %collective-permute-done.22.refs_4_, ...), custom_call_target="tpu_custom_call" | custom-call | bytes 6291456 | tf_op jit(solution)/shard_map/unpack_od/pallas_call | solution.py:140
  189.2 5.0 %collective-permute-done.38.refs_7_ = f32[768,128]{1,0:T(8,128)} collective-permute-done((f32[768,128]{1,0:T(8,128)}, f32[768,128]{1,0:T(8,128)}, u32[]{:S(2)}, u32[]{:S(2)}) %collective-permute-start.38) | collective-permute-done | bytes 393248 | tf_op jit(solution)/shard_map/ppermute | solution.py:444
  194.2 5.6 %collective-permute-done.32.refs_2_ = f32[768,128]{1,0:T(8,128)} collective-permute-done((f32[768,128]{1,0:T(8,128)}, f32[768,128]{1,0:T(8,128)}, u32[]{:S(2)}, u32[]{:S(2)}) %collective-permute-start.32) | collective-permute-done | bytes 393248 | tf_op jit(solution)/shard_map/ppermute | solution.py:444
  199.8 10.2 %collective-permute-done.33.refs_3_ = f32[768,128]{1,0:T(8,128)} collective-permute-done((f32[768,128]{1,0:T(8,128)}, f32[768,128]{1,0:T(8,128)}, u32[]{:S(2)}, u32[]{:S(2)}) %collective-permute-start.33) | collective-permute-done | bytes 393248 | tf_op jit(solution)/shard_map/ppermute | solution.py:444
  210.0 4.2 %unpack_kv.1 = (f32[128,3072]{1,0:T(8,128)}, f32[128,3072]{1,0:T(8,128)}) custom-call(s32[5]{0:T(128)S(1)} %copy-done.10, f32[768,128]{1,0:T(8,128)S(1)} %copy-done.7, f32[768,128]{1,0:T(8,128)} %collective-permute-done.32.refs_2_, f32[768,128]{1,0:T(8,128)} %collective-permute-done.33.refs_3_, f32[768,128]{1,0:T(8,128)} %collective-permute-done.34.refs_4_, ...), custom_call_target="tpu_custom_call" | custom-call | bytes 6291456 | tf_op jit(solution)/shard_map/unpack_kv/pallas_call | solution.py:140
  (146 shorter events, 17.1 us)
Async XLA Ops:
  5.2 19.7 %collective-permute-start = (f32[1536,128]{1,0:T(8,128)}, f32[1536,128]{1,0:T(8,128)}, u32[]{:S(2)}, u32[]{:S(2)}) collective-permute-start(f32[1536,128]{1,0:T(8,128)} %get-tuple-element.84), channel_id=1, source_target_pairs={{0,1},{1,0},{2,3},{3,2},{4,5},{5,4},{6,7},{7,6},{8,9},{9,8},{10,11... | collective-permute-start | bytes 2359304 | tf_op jit(solution)/shard_map/ppermute | solution.py:444
  7.3 18.4 %collective-permute-start.1 = (f32[1536,128]{1,0:T(8,128)}, f32[1536,128]{1,0:T(8,128)}, u32[]{:S(2)}, u32[]{:S(2)}) collective-permute-start(f32[1536,128]{1,0:T(8,128)} %get-tuple-element.85), channel_id=1, source_target_pairs={{0,2},{1,3},{2,0},{3,1},{4,6},{5,7},{6,4},{7,5},{8,10},{9,11},{10,... | collective-permute-start | bytes 2359304 | tf_op jit(solution)/shard_map/ppermute | solution.py:444
  8.6 34.1 %collective-permute-start.2 = (f32[1536,128]{1,0:T(8,128)}, f32[1536,128]{1,0:T(8,128)}, u32[]{:S(2)}, u32[]{:S(2)}) collective-permute-start(f32[1536,128]{1,0:T(8,128)} %get-tuple-element.86), channel_id=1, source_target_pairs={{0,3},{1,2},{2,1},{3,0},{4,7},{5,6},{6,5},{7,4},{8,11},{9,10},{10,... | collective-permute-start | bytes 2359304 | tf_op jit(solution)/shard_map/ppermute | solution.py:444
  42.7 21.6 %copy-start.12 = (f32[1544,128]{1,0:T(8,128)S(1)}, f32[1544,128]{1,0:T(8,128)}, u32[]{:S(2)}) copy-start(f32[1544,128]{1,0:T(8,128)} %copy-done.11) | copy-start | bytes 2371588
  42.7 29.0 %collective-permute-start.7 = (f32[1544,128]{1,0:T(8,128)}, f32[1544,128]{1,0:T(8,128)S(1)}, u32[]{:S(2)}, u32[]{:S(2)}) collective-permute-start(f32[1544,128]{1,0:T(8,128)} %get-tuple-element.99), channel_id=1, source_target_pairs={{0,1},{1,0},{2,3},{3,2},{4,5},{5,4},{6,7},{7,6},{8,9},{9,8},{10,11... | collective-permute-start | bytes 2371592 | tf_op jit(solution)/shard_map/ppermute | solution.py:444
  43.9 27.9 %collective-permute-start.8 = (f32[1544,128]{1,0:T(8,128)}, f32[1544,128]{1,0:T(8,128)S(1)}, u32[]{:S(2)}, u32[]{:S(2)}) collective-permute-start(f32[1544,128]{1,0:T(8,128)} %get-tuple-element.100), channel_id=1, source_target_pairs={{0,2},{1,3},{2,0},{3,1},{4,6},{5,7},{6,4},{7,5},{8,10},{9,11},{10,... | collective-permute-start | bytes 2371592 | tf_op jit(solution)/shard_map/ppermute | solution.py:444
  52.6 4.0 %collective-permute-start.3 = (f32[800,128]{1,0:T(8,128)}, f32[800,128]{1,0:T(8,128)S(1)}, u32[]{:S(2)}, u32[]{:S(2)}) collective-permute-start(f32[800,128]{1,0:T(8,128)} %get-tuple-element.94), channel_id=1, source_target_pairs={{0,4},{4,0},{8,12},{12,8},{16,20},{20,16},{24,28},{28,24},{1,5},{5... | collective-permute-start | bytes 1228808 | tf_op jit(solution)/shard_map/ppermute | solution.py:444
  60.0 4.3 %collective-permute-start.4 = (f32[200,128]{1,0:T(8,128)}, f32[200,128]{1,0:T(8,128)S(1)}, u32[]{:S(2)}, u32[]{:S(2)}) collective-permute-start(f32[200,128]{1,0:T(8,128)} %get-tuple-element.96), channel_id=1, source_target_pairs={{0,8},{4,12},{8,0},{12,4},{16,24},{20,28},{24,16},{28,20},{1,9},{5... | collective-permute-start | bytes 307208 | tf_op jit(solution)/shard_map/ppermute | solution.py:444
  61.3 4.6 %collective-permute-start.5 = (f32[200,128]{1,0:T(8,128)}, f32[200,128]{1,0:T(8,128)S(1)}, u32[]{:S(2)}, u32[]{:S(2)}) collective-permute-start(f32[200,128]{1,0:T(8,128)} %get-tuple-element.97), channel_id=1, source_target_pairs={{0,16},{4,20},{8,24},{12,28},{16,0},{20,4},{24,8},{28,12},{1,17},{... | collective-permute-start | bytes 307208 | tf_op jit(solution)/shard_map/ppermute | solution.py:444
  63.6 7.2 %collective-permute-start.6 = (f32[200,128]{1,0:T(8,128)}, f32[200,128]{1,0:T(8,128)S(1)}, u32[]{:S(2)}, u32[]{:S(2)}) collective-permute-start(f32[200,128]{1,0:T(8,128)} %get-tuple-element.98), channel_id=1, source_target_pairs={{0,24},{4,28},{8,16},{12,20},{16,8},{20,12},{24,0},{28,4},{1,25},{... | collective-permute-start | bytes 307208 | tf_op jit(solution)/shard_map/ppermute | solution.py:444
  64.3 22.6 %collective-permute-start.9 = (f32[1544,128]{1,0:T(8,128)S(1)}, f32[1544,128]{1,0:T(8,128)}, u32[]{:S(2)}, u32[]{:S(2)}) collective-permute-start(f32[1544,128]{1,0:T(8,128)S(1)} %copy-done.12), channel_id=1, source_target_pairs={{0,3},{1,2},{2,1},{3,0},{4,7},{5,6},{6,5},{7,4},{8,11},{9,10},{10,... | collective-permute-start | bytes 2371592 | tf_op jit(solution)/shard_map/ppermute | solution.py:444
  71.7 5.1 %collective-permute-start.10 = (f32[200,128]{1,0:T(8,128)S(1)}, f32[200,128]{1,0:T(8,128)S(1)}, u32[]{:S(2)}, u32[]{:S(2)}) collective-permute-start(f32[200,128]{1,0:T(8,128)S(1)} %add_add_fusion.1), channel_id=1, source_target_pairs={{0,8},{4,12},{8,0},{12,4},{16,24},{20,28},{24,16},{28,20},{1,9},{5... | collective-permute-start | bytes 307208 | tf_op jit(solution)/shard_map/ppermute | solution.py:444
  74.4 6.1 %collective-permute-start.11 = (f32[200,128]{1,0:T(8,128)S(1)}, f32[200,128]{1,0:T(8,128)S(1)}, u32[]{:S(2)}, u32[]{:S(2)}) collective-permute-start(f32[200,128]{1,0:T(8,128)S(1)} %add_add_fusion.1), channel_id=1, source_target_pairs={{0,16},{4,20},{8,24},{12,28},{16,0},{20,4},{24,8},{28,12},{1,17},{... | collective-permute-start | bytes 307208 | tf_op jit(solution)/shard_map/ppermute | solution.py:444
  75.4 6.7 %collective-permute-start.12 = (f32[200,128]{1,0:T(8,128)S(1)}, f32[200,128]{1,0:T(8,128)S(1)}, u32[]{:S(2)}, u32[]{:S(2)}) collective-permute-start(f32[200,128]{1,0:T(8,128)S(1)} %add_add_fusion.1), channel_id=1, source_target_pairs={{0,24},{4,28},{8,16},{12,20},{16,8},{20,12},{24,0},{28,4},{1,25},{... | collective-permute-start | bytes 307208 | tf_op jit(solution)/shard_map/ppermute | solution.py:444
  82.2 5.6 %collective-permute-start.13 = (f32[800,128]{1,0:T(8,128)S(1)}, f32[800,128]{1,0:T(8,128)}, u32[]{:S(2)}, u32[]{:S(2)}) collective-permute-start(f32[800,128]{1,0:T(8,128)S(1)} %constant_dynamic-update-slice_fusion.refs_12_), channel_id=1, source_target_pairs={{0,4},{4,0},{8,12},{12,8},{16,20},{20,16},{24,28},{28,24},{1,5},{5... | collective-permute-start | bytes 1228808 | tf_op jit(solution)/shard_map/ppermute | solution.py:444
  87.0 16.1 %copy-start.28 = (f32[768,128]{1,0:T(8,128)S(1)}, f32[768,128]{1,0:T(8,128)}, u32[]{:S(2)}) copy-start(f32[768,128]{1,0:T(8,128)} %get-tuple-element.122) | copy-start | bytes 1179652
  99.3 5.7 %collective-permute-start.14 = (f32[800,128]{1,0:T(8,128)}, f32[800,128]{1,0:T(8,128)S(1)}, u32[]{:S(2)}, u32[]{:S(2)}) collective-permute-start(f32[800,128]{1,0:T(8,128)} %get-tuple-element.108), channel_id=1, source_target_pairs={{0,4},{4,0},{8,12},{12,8},{16,20},{20,16},{24,28},{28,24},{1,5},{5... | collective-permute-start | bytes 1228808 | tf_op jit(solution)/shard_map/ppermute | solution.py:444
  99.7 12.2 %collective-permute-start.18 = (f32[768,128]{1,0:T(8,128)}, f32[768,128]{1,0:T(8,128)S(1)}, u32[]{:S(2)}, u32[]{:S(2)}) collective-permute-start(f32[768,128]{1,0:T(8,128)} %get-tuple-element.121), channel_id=1, source_target_pairs={{0,4},{4,8},{8,12},{12,16},{16,20},{20,24},{24,28},{1,5},{5,9},{9,... | collective-permute-start | bytes 1179656 | tf_op jit(solution)/shard_map/ppermute | solution.py:485
  103.1 11.2 %collective-permute-start.19 = (f32[768,128]{1,0:T(8,128)S(1)}, f32[768,128]{1,0:T(8,128)S(1)}, u32[]{:S(2)}, u32[]{:S(2)}) collective-permute-start(f32[768,128]{1,0:T(8,128)S(1)} %copy-done.28), channel_id=1, source_target_pairs={{4,0},{8,4},{12,8},{16,12},{20,16},{24,20},{28,24},{5,1},{9,5},{13... | collective-permute-start | bytes 1179656 | tf_op jit(solution)/shard_map/ppermute | solution.py:490
  108.4 19.4 %collective-permute-start.15 = (f32[200,128]{1,0:T(8,128)}, f32[200,128]{1,0:T(8,128)S(1)}, u32[]{:S(2)}, u32[]{:S(2)}) collective-permute-start(f32[200,128]{1,0:T(8,128)} %get-tuple-element.116), channel_id=1, source_target_pairs={{0,8},{4,12},{8,0},{12,4},{16,24},{20,28},{24,16},{28,20},{1,9},{5... | collective-permute-start | bytes 307208 | tf_op jit(solution)/shard_map/ppermute | solution.py:444
  109.4 18.4 %collective-permute-start.16 = (f32[200,128]{1,0:T(8,128)}, f32[200,128]{1,0:T(8,128)S(1)}, u32[]{:S(2)}, u32[]{:S(2)}) collective-permute-start(f32[200,128]{1,0:T(8,128)} %get-tuple-element.117), channel_id=1, source_target_pairs={{0,16},{4,20},{8,24},{12,28},{16,0},{20,4},{24,8},{28,12},{1,17},{... | collective-permute-start | bytes 307208 | tf_op jit(solution)/shard_map/ppermute | solution.py:444
  109.6 18.2 %collective-permute-start.17 = (f32[200,128]{1,0:T(8,128)}, f32[200,128]{1,0:T(8,128)S(1)}, u32[]{:S(2)}, u32[]{:S(2)}) collective-permute-start(f32[200,128]{1,0:T(8,128)} %get-tuple-element.118), channel_id=1, source_target_pairs={{0,24},{4,28},{8,16},{12,20},{16,8},{20,12},{24,0},{28,4},{1,25},{... | collective-permute-start | bytes 307208 | tf_op jit(solution)/shard_map/ppermute | solution.py:444
  127.8 17.7 %copy-start.2 = (f32[776,128]{1,0:T(8,128)S(1)}, f32[776,128]{1,0:T(8,128)}, u32[]{:S(2)}) copy-start(f32[776,128]{1,0:T(8,128)} %get-tuple-element.127.refs_1_) | copy-start | bytes 1191940
  127.8 17.7 %copy-start.27 = (f32[776,128]{1,0:T(8,128)S(1)}, f32[776,128]{1,0:T(8,128)}, u32[]{:S(2)}) copy-start(f32[776,128]{1,0:T(8,128)} %get-tuple-element.130) | copy-start | bytes 1191940
  127.8 25.6 %copy-start.32 = (f32[384,128]{1,0:T(8,128)S(1)}, f32[384,128]{1,0:T(8,128)}, u32[]{:S(2)}) copy-start(f32[384,128]{1,0:T(8,128)} %get-tuple-element.147) | copy-start | bytes 589828
  127.9 17.7 %collective-permute-start.23 = (f32[200,128]{1,0:T(8,128)S(1)}, f32[200,128]{1,0:T(8,128)S(1)}, u32[]{:S(2)}, u32[]{:S(2)}) collective-permute-start(f32[200,128]{1,0:T(8,128)S(1)} %add_add_fusion), channel_id=1, source_target_pairs={{0,8},{4,12},{8,0},{12,4},{16,24},{20,28},{24,16},{28,20},{1,9},{5... | collective-permute-start | bytes 307208 | tf_op jit(solution)/shard_map/ppermute | solution.py:444
  127.9 18.9 %collective-permute-start.24 = (f32[200,128]{1,0:T(8,128)S(1)}, f32[200,128]{1,0:T(8,128)S(1)}, u32[]{:S(2)}, u32[]{:S(2)}) collective-permute-start(f32[200,128]{1,0:T(8,128)S(1)} %add_add_fusion), channel_id=1, source_target_pairs={{0,16},{4,20},{8,24},{12,28},{16,0},{20,4},{24,8},{28,12},{1,17},{... | collective-permute-start | bytes 307208 | tf_op jit(solution)/shard_map/ppermute | solution.py:444
  128.0 21.0 %collective-permute-start.25 = (f32[200,128]{1,0:T(8,128)S(1)}, f32[200,128]{1,0:T(8,128)S(1)}, u32[]{:S(2)}, u32[]{:S(2)}) collective-permute-start(f32[200,128]{1,0:T(8,128)S(1)} %add_add_fusion), channel_id=1, source_target_pairs={{0,24},{4,28},{8,16},{12,20},{16,8},{20,12},{24,0},{28,4},{1,25},{... | collective-permute-start | bytes 307208 | tf_op jit(solution)/shard_map/ppermute | solution.py:444
  131.5 20.7 %collective-permute-start.20 = (f32[776,128]{1,0:T(8,128)}, f32[776,128]{1,0:T(8,128)S(1)}, u32[]{:S(2)}, u32[]{:S(2)}) collective-permute-start(f32[776,128]{1,0:T(8,128)} %get-tuple-element.128), channel_id=1, source_target_pairs={{0,1},{1,0},{2,3},{3,2},{4,5},{5,4},{6,7},{7,6},{8,9},{9,8},{10,11... | collective-permute-start | bytes 1191944 | tf_op jit(solution)/shard_map/ppermute | solution.py:444
  132.7 19.5 %collective-permute-start.21 = (f32[776,128]{1,0:T(8,128)}, f32[776,128]{1,0:T(8,128)S(1)}, u32[]{:S(2)}, u32[]{:S(2)}) collective-permute-start(f32[776,128]{1,0:T(8,128)} %get-tuple-element.129), channel_id=1, source_target_pairs={{0,2},{1,3},{2,0},{3,1},{4,6},{5,7},{6,4},{7,5},{8,10},{9,11},{10,... | collective-permute-start | bytes 1191944 | tf_op jit(solution)/shard_map/ppermute | solution.py:444
  145.6 20.3 %collective-permute-start.22 = (f32[776,128]{1,0:T(8,128)S(1)}, f32[776,128]{1,0:T(8,128)S(1)}, u32[]{:S(2)}, u32[]{:S(2)}) collective-permute-start(f32[776,128]{1,0:T(8,128)S(1)} %copy-done.27), channel_id=1, source_target_pairs={{0,3},{1,2},{2,1},{3,0},{4,7},{5,6},{6,5},{7,4},{8,11},{9,10},{10,... | collective-permute-start | bytes 1191944 | tf_op jit(solution)/shard_map/ppermute | solution.py:444
  146.9 6.6 %collective-permute-start.35 = (f32[384,128]{1,0:T(8,128)}, f32[384,128]{1,0:T(8,128)S(1)}, u32[]{:S(2)}, u32[]{:S(2)}) collective-permute-start(f32[384,128]{1,0:T(8,128)} %get-tuple-element.155), channel_id=1, source_target_pairs={{0,4},{4,8},{8,12},{12,16},{16,20},{20,24},{24,28},{1,5},{5,9},{9,... | collective-permute-start | bytes 589832 | tf_op jit(solution)/shard_map/ppermute | solution.py:485
  149.1 8.1 %collective-permute-start.36 = (f32[384,128]{1,0:T(8,128)}, f32[384,128]{1,0:T(8,128)S(1)}, u32[]{:S(2)}, u32[]{:S(2)}) collective-permute-start(f32[384,128]{1,0:T(8,128)} %get-tuple-element.156), channel_id=1, source_target_pairs={{4,0},{8,4},{12,8},{16,12},{20,16},{24,20},{28,24},{5,1},{9,5},{13... | collective-permute-start | bytes 589832 | tf_op jit(solution)/shard_map/ppermute | solution.py:490
  152.2 5.4 %collective-permute-start.29 = (f32[800,128]{1,0:T(8,128)S(1)}, f32[800,128]{1,0:T(8,128)S(1)}, u32[]{:S(2)}, u32[]{:S(2)}) collective-permute-start(f32[800,128]{1,0:T(8,128)S(1)} %pad_maximum_fusion.refs_2_), channel_id=1, source_target_pairs={{0,4},{4,0},{8,12},{12,8},{16,20},{20,16},{24,28},{28,24},{1,5},{5... | collective-permute-start | bytes 1228808 | tf_op jit(solution)/shard_map/ppermute | solution.py:444
  152.2 14.7 %collective-permute-start.26 = (f32[776,128]{1,0:T(8,128)}, f32[776,128]{1,0:T(8,128)S(1)}, u32[]{:S(2)}, u32[]{:S(2)}) collective-permute-start(f32[776,128]{1,0:T(8,128)} %get-tuple-element.139), channel_id=1, source_target_pairs={{0,1},{1,0},{2,3},{3,2},{4,5},{5,4},{6,7},{7,6},{8,9},{9,8},{10,11... | collective-permute-start | bytes 1191944 | tf_op jit(solution)/shard_map/ppermute | solution.py:444
  153.5 15.8 %collective-permute-start.30 = (f32[384,128]{1,0:T(8,128)S(1)}, f32[384,128]{1,0:T(8,128)S(1)}, u32[]{:S(2)}, u32[]{:S(2)}) collective-permute-start(f32[384,128]{1,0:T(8,128)S(1)} %copy-done.32), channel_id=1, source_target_pairs={{0,4},{4,8},{8,12},{12,16},{16,20},{20,24},{24,28},{1,5},{5,9},{9,... | collective-permute-start | bytes 589832 | tf_op jit(solution)/shard_map/ppermute | solution.py:485
  157.2 24.7 %collective-permute-start.27 = (f32[776,128]{1,0:T(8,128)}, f32[776,128]{1,0:T(8,128)S(1)}, u32[]{:S(2)}, u32[]{:S(2)}) collective-permute-start(f32[776,128]{1,0:T(8,128)} %get-tuple-element.140), channel_id=1, source_target_pairs={{0,2},{1,3},{2,0},{3,1},{4,6},{5,7},{6,4},{7,5},{8,10},{9,11},{10,... | collective-permute-start | bytes 1191944 | tf_op jit(solution)/shard_map/ppermute | solution.py:444
  157.5 25.0 %collective-permute-start.28 = (f32[776,128]{1,0:T(8,128)}, f32[776,128]{1,0:T(8,128)S(1)}, u32[]{:S(2)}, u32[]{:S(2)}) collective-permute-start(f32[776,128]{1,0:T(8,128)} %get-tuple-element.141), channel_id=1, source_target_pairs={{0,3},{1,2},{2,1},{3,0},{4,7},{5,6},{6,5},{7,4},{8,11},{9,10},{10,... | collective-permute-start | bytes 1191944 | tf_op jit(solution)/shard_map/ppermute | solution.py:444
  165.8 17.9 %collective-permute-start.37 = (f32[768,128]{1,0:T(8,128)}, f32[768,128]{1,0:T(8,128)S(1)}, u32[]{:S(2)}, u32[]{:S(2)}) collective-permute-start(f32[768,128]{1,0:T(8,128)} %get-tuple-element.158), channel_id=1, source_target_pairs={{0,1},{1,0},{2,3},{3,2},{4,5},{5,4},{6,7},{7,6},{8,9},{9,8},{10,11... | collective-permute-start | bytes 1179656 | tf_op jit(solution)/shard_map/ppermute | solution.py:444
  166.9 7.3 %collective-permute-start.31 = (f32[384,128]{1,0:T(8,128)S(1)}, f32[384,128]{1,0:T(8,128)S(1)}, u32[]{:S(2)}, u32[]{:S(2)}) collective-permute-start(f32[384,128]{1,0:T(8,128)S(1)} %copy-done.31), channel_id=1, source_target_pairs={{4,0},{8,4},{12,8},{16,12},{20,16},{24,20},{28,24},{5,1},{9,5},{13... | collective-permute-start | bytes 589832 | tf_op jit(solution)/shard_map/ppermute | solution.py:490
  169.3 24.9 %collective-permute-start.38 = (f32[768,128]{1,0:T(8,128)}, f32[768,128]{1,0:T(8,128)}, u32[]{:S(2)}, u32[]{:S(2)}) collective-permute-start(f32[768,128]{1,0:T(8,128)} %get-tuple-element.159), channel_id=1, source_target_pairs={{0,2},{1,3},{2,0},{3,1},{4,6},{5,7},{6,4},{7,5},{8,10},{9,11},{10,... | collective-permute-start | bytes 1179656 | tf_op jit(solution)/shard_map/ppermute | solution.py:444
  174.2 20.0 %collective-permute-start.39 = (f32[768,128]{1,0:T(8,128)}, f32[768,128]{1,0:T(8,128)}, u32[]{:S(2)}, u32[]{:S(2)}) collective-permute-start(f32[768,128]{1,0:T(8,128)} %get-tuple-element.160), channel_id=1, source_target_pairs={{0,3},{1,2},{2,1},{3,0},{4,7},{5,6},{6,5},{7,4},{8,11},{9,10},{10,... | collective-permute-start | bytes 1179656 | tf_op jit(solution)/shard_map/ppermute | solution.py:444
  182.0 17.8 %collective-permute-start.32 = (f32[768,128]{1,0:T(8,128)}, f32[768,128]{1,0:T(8,128)}, u32[]{:S(2)}, u32[]{:S(2)}) collective-permute-start(f32[768,128]{1,0:T(8,128)} %get-tuple-element.150), channel_id=1, source_target_pairs={{0,1},{1,0},{2,3},{3,2},{4,5},{5,4},{6,7},{7,6},{8,9},{9,8},{10,11... | collective-permute-start | bytes 1179656 | tf_op jit(solution)/shard_map/ppermute | solution.py:444
  182.5 27.4 %collective-permute-start.33 = (f32[768,128]{1,0:T(8,128)}, f32[768,128]{1,0:T(8,128)}, u32[]{:S(2)}, u32[]{:S(2)}) collective-permute-start(f32[768,128]{1,0:T(8,128)} %get-tuple-element.151), channel_id=1, source_target_pairs={{0,2},{1,3},{2,0},{3,1},{4,6},{5,7},{6,4},{7,5},{8,10},{9,11},{10,... | collective-permute-start | bytes 1179656 | tf_op jit(solution)/shard_map/ppermute | solution.py:444
  184.5 25.4 %collective-permute-start.34 = (f32[768,128]{1,0:T(8,128)}, f32[768,128]{1,0:T(8,128)}, u32[]{:S(2)}, u32[]{:S(2)}) collective-permute-start(f32[768,128]{1,0:T(8,128)} %get-tuple-element.152), channel_id=1, source_target_pairs={{0,3},{1,2},{2,1},{3,0},{4,7},{5,6},{6,5},{7,4},{8,11},{9,10},{10,... | collective-permute-start | bytes 1179656 | tf_op jit(solution)/shard_map/ppermute | solution.py:444
  186.1 23.9 %copy-start.4 = (f32[768,128]{1,0:T(8,128)S(1)}, f32[768,128]{1,0:T(8,128)}, u32[]{:S(2)}) copy-start(f32[768,128]{1,0:T(8,128)} %get-tuple-element.157.refs_5_) | copy-start | bytes 1179652
  186.1 23.9 %copy-start.6 = (f32[768,128]{1,0:T(8,128)S(1)}, f32[768,128]{1,0:T(8,128)}, u32[]{:S(2)}) copy-start(f32[768,128]{1,0:T(8,128)} %copy-done.5) | copy-start | bytes 1179652
  186.1 23.9 %copy-start.7 = (f32[768,128]{1,0:T(8,128)S(1)}, f32[768,128]{1,0:T(8,128)}, u32[]{:S(2)}) copy-start(f32[768,128]{1,0:T(8,128)} %get-tuple-element.149.refs_1_) | copy-start | bytes 1179652
  (26 other events, 163.0 us)
